TPU v7x, 512 devices: a whole 4x4x16 slice. The times are simulated.
512 devices in a mesh: fsdp: 32 (over z, y_hi), grp: 2 (over core), slab: 8 (over x, y_lo).
Axes of the slice: x: 4, y: 4 (y_hi: 2, y_lo: 2; y = y_hi * 2 + y_lo), z: 16, core: 2. Of those that a mesh axis runs over, the one named last changes fastest.
Arguments:
- hidden: bfloat16 [64, 64, 64, 3072], P(('fsdp', 'grp'), 'slab'), may hold values from -6 to 6
- modulation: bfloat16 [64, 2, 3072], P(('fsdp', 'grp')), may hold values from -3 to 3
- noisy: bfloat16 [64, 64, 64, 64], P(('fsdp', 'grp'), 'slab'), may hold values from -6 to 6
- step_index: int32 [64], P(('fsdp', 'grp')), may hold values from 0 to 27
- proj_weight: bfloat16 [3072, 64], P('fsdp'), may hold values from -0.109375 to 0.109375
- proj_bias: float32 [64], replicated, may hold values from -3 to 3
- conv_weight: bfloat16 [3, 3, 16, 512], P(None, None, None, 'fsdp'), may hold values from -0.5 to 0.5
- conv_bias: float32 [512], replicated, may hold values from -3 to 3
- norm_gain: float32 [512], replicated, may hold values from 0.25 to 1.75
- norm_shift: float32 [512], replicated, may hold values from -3 to 3
- head_weight: bfloat16 [512, 192], P('fsdp'), may hold values from -1 to 1
- head_bias: float32 [192], replicated, may hold values from -2 to 2
- patch_weight: bfloat16 [588, 1280], P(None, 'fsdp'), may hold values from -0.25 to 0.25
- position: bfloat16 [256, 1280], P('slab'), may hold values from -3 to 3
- class_token: float32 [1280], replicated, may hold values from -6 to 6
- vit_gain: float32 [4, 1280], replicated, may hold values from 0.25 to 1.75
- vit_shift: float32 [4, 1280], replicated, may hold values from -2 to 2
- attn_in: bfloat16 [1280, 3840], P('fsdp', 'slab'), may hold values from -0.15625 to 0.15625
- attn_out: bfloat16 [1280, 1280], P('slab', 'fsdp'), may hold values from -0.625 to 0.625
- attn_out_bias: float32 [1280], replicated, may hold values from -3 to 3
- mlp_in: bfloat16 [1280, 5120], P(None, ('fsdp', 'slab')), may hold values from -0.15625 to 0.15625
- mlp_in_bias: bfloat16 [5120], P(('fsdp', 'slab')), may hold values from -3 to 3
- mlp_out: bfloat16 [5120, 1280], P(('fsdp', 'slab')), may hold values from -0.078125 to 0.078125
- mlp_out_bias: float32 [1280], replicated, may hold values from -3 to 3
- vit_proj: bfloat16 [1280, 1024], P('fsdp'), may hold values from -0.15625 to 0.15625
- text_embed: float32 [64, 1024], P(('fsdp', 'grp')), may hold values from -6 to 6
Outputs:
- proj_grad: float32 [3072, 64], P('fsdp')
- scores: float32 [64], P(('fsdp', 'grp'))
All inputs are finite; a program needn't handle non-finite values.
Results may differ from a plain program's by a relative error of at most 0.023.
Values may be sent and summed in bfloat16 or wider, within the bound.
A program may use at most 128 MiB of HBM per device.

v0:
```python
import jax
import jax.numpy as jnp
from jax import lax
from jax.sharding import PartitionSpec as P

GROUPS = 32
HEAD_DIM = 80
STEPS = 28
PROWS = 2
HALO = 2


LAT_SCALE = 0.3611
LAT_SHIFT = 0.1159
PIX_MEAN = (0.48145466, 0.4578275, 0.40821073)
PIX_STD = (0.26862954, 0.26130258, 0.27577711)
HIGH = lax.Precision.HIGHEST


def with_halo(block, sides, width):
    for axis, dim in sides:
        count = lax.axis_size(axis)
        forward = [(i, i + 1) for i in range(count - 1)]
        backward = [(target, source) for source, target in forward]
        low = lax.ppermute(
            lax.slice_in_dim(block, block.shape[dim] - width, None, axis=dim), axis, forward
        )
        high = lax.ppermute(lax.slice_in_dim(block, 0, width, axis=dim), axis, backward)
        block = jnp.concatenate([low, block, high], axis=dim)
    return block


def norm_rows(values, epsilon):
    average = jnp.mean(values, axis=-1, keepdims=True)
    centered = values - average
    return centered / jnp.sqrt(jnp.mean(centered * centered, axis=-1, keepdims=True) + epsilon)


def affine_norm(values, gain, shift):
    return norm_rows(values, 1e-05) * gain + shift


def exact_gelu(values):
    return jax.nn.gelu(values, approximate=False)


def flow_sigma(step_index):
    remain = 1.0 - step_index.astype(jnp.float32) / STEPS
    return 3.0 * remain / (1.0 + 2.0 * remain)


def channel_consts():
    return (
        jnp.array(PIX_MEAN, jnp.float32).reshape(1, 3, 1, 1),
        jnp.array(PIX_STD, jnp.float32).reshape(1, 3, 1, 1),
    )


def resize_table(out_count, in_count):
    stretch = in_count / out_count
    centers = (jnp.arange(out_count, dtype=jnp.float32) + 0.5) * stretch
    places = jnp.arange(in_count, dtype=jnp.float32) + 0.5
    weights = jnp.maximum(0.0, 1.0 - jnp.abs(places[None, :] - centers[:, None]) / stretch)
    return weights / jnp.sum(weights, axis=1, keepdims=True)


def tokens_to_latent(tokens):
    count, rows, cols, chans = tokens.shape
    view = tokens.reshape(count, rows, cols, chans // 4, 2, 2).transpose(0, 1, 4, 2, 5, 3)
    return view.reshape(count, rows * 2, cols * 2, chans // 4)


def latent_to_tokens(latent):
    count, rows, cols, chans = latent.shape
    view = latent.reshape(count, rows // 2, 2, cols // 2, 2, chans).transpose(0, 1, 3, 5, 2, 4)
    return view.reshape(count, rows // 2, cols // 2, chans * 4)


def cells_to_pixels(cells):
    count, rows, cols, chans = cells.shape
    view = cells.reshape(count, rows, cols, 3, 8, 8).transpose(0, 3, 1, 4, 2, 5)
    return view.reshape(count, 3, rows * 8, cols * 8)


def pixels_to_cells(pixels):
    count, chans, rows, cols = pixels.shape
    view = pixels.reshape(count, 3, rows // 8, 8, cols // 8, 8).transpose(0, 2, 4, 1, 3, 5)
    return view.reshape(count, rows // 8, cols // 8, 192)


def image_to_patches(image):
    count, chans, rows, cols = image.shape
    view = image.reshape(count, 3, rows // 14, 14, cols // 14, 14).transpose(0, 2, 4, 1, 3, 5)
    return view.reshape(count, rows // 14 * (cols // 14), 588)


def patches_to_image(patches, rows, cols):
    count = patches.shape[0]
    view = patches.reshape(count, rows // 14, cols // 14, 3, 14, 14).transpose(0, 3, 1, 4, 2, 5)
    return view.reshape(count, 3, rows, cols)


def conv_columns(padded, rows, cols):
    return jnp.concatenate(
        [padded[:, tap // 3 : tap // 3 + rows, tap % 3 : tap % 3 + cols] for tap in range(9)],
        axis=-1,
    )


def columns_back(d_columns, rows, cols):
    chans = d_columns.shape[-1] // 9
    total = jnp.zeros(d_columns.shape[:1] + (rows + 2, cols + 2, chans), jnp.float32)
    for tap in range(9):
        shift_row = tap // 3
        shift_col = tap % 3
        piece = d_columns[..., tap * chans : (tap + 1) * chans]
        total = total + jnp.pad(
            piece, ((0, 0), (shift_row, 2 - shift_row), (shift_col, 2 - shift_col), (0, 0))
        )
    return total


def group_view(values):
    count, rows, cols, chans = values.shape
    return values.reshape(count, rows * cols, GROUPS, chans // GROUPS)


def group_sums(conv_out):
    view = group_view(conv_out)
    return (jnp.sum(view, axis=(1, 3)), jnp.sum(view * view, axis=(1, 3)))


def group_apply(conv_out, totals, cells):
    average = totals[0] / cells
    inverse = 1.0 / jnp.sqrt(totals[1] / cells - average * average + 1e-06)
    normed = (group_view(conv_out) - average[:, None, :, None]) * inverse[:, None, :, None]
    return (normed.reshape(conv_out.shape), inverse)


def group_pair(d_normed, normed):
    return (
        jnp.sum(group_view(d_normed), axis=(1, 3)),
        jnp.sum(group_view(d_normed * normed), axis=(1, 3)),
    )


def group_back(d_normed, normed, inverse, totals, cells):
    grads = group_view(d_normed) - totals[0][:, None, :, None] / cells
    grads = grads - group_view(normed) * (totals[1][:, None, :, None] / cells)
    return (grads * inverse[:, None, :, None]).reshape(d_normed.shape)


def match_score(embed, text):
    dots = jnp.sum(embed * text, axis=-1)
    sizes = jnp.sqrt(jnp.sum(embed * embed, axis=-1) + 1e-06) * jnp.sqrt(
        jnp.sum(text * text, axis=-1) + 1e-06
    )
    return 100.0 * dots / sizes


def local(
    hidden,
    modulation,
    noisy,
    step_index,
    proj_weight,
    proj_bias,
    conv_weight,
    conv_bias,
    norm_gain,
    norm_shift,
    head_weight,
    head_bias,
    patch_weight,
    position,
    class_token,
    vit_gain,
    vit_shift,
    attn_in,
    attn_out,
    attn_out_bias,
    mlp_in,
    mlp_in_bias,
    mlp_out,
    mlp_out_bias,
    vit_proj,
    text_embed,
):
    slabs = lax.axis_size("slab")
    place = lax.axis_index("slab")
    images, tok_rows, tok_cols, width = hidden.shape
    lat_rows = 2 * tok_rows
    lat_cols = 2 * tok_cols
    pix_rows = 8 * lat_rows
    pix_side = 8 * lat_cols
    grid_side = PROWS * slabs
    vit_side = 14 * grid_side
    res_rows = 14 * PROWS
    tokens = grid_side * grid_side
    total_images = images * lax.axis_size("fsdp") * lax.axis_size("grp")
    root = HEAD_DIM**0.5
    pix_mean, pix_std = channel_consts()
    proj_full, conv_full, head_full, patch_full, attn_full, attn_rows = (
        lax.all_gather(proj_weight, "fsdp", axis=0, tiled=True),
        lax.all_gather(conv_weight, "fsdp", axis=3, tiled=True),
        lax.all_gather(head_weight, "fsdp", axis=0, tiled=True),
        lax.all_gather(patch_weight, "fsdp", axis=1, tiled=True),
        lax.all_gather(attn_in, "fsdp", axis=0, tiled=True),
        lax.all_gather(attn_out, "fsdp", axis=1, tiled=True),
    )
    width_vd = patch_full.shape[1]
    own_heads = attn_full.shape[1] // (3 * HEAD_DIM)
    attn_view = attn_full.reshape(width_vd, own_heads, 3, HEAD_DIM)
    query_w = attn_view[:, :, 0]
    key_w = attn_view[:, :, 1]
    value_w = attn_view[:, :, 2]
    pair_w = attn_view[:, :, 1:].reshape(width_vd, own_heads * 2 * HEAD_DIM)
    conv_mat = conv_full.reshape(-1, conv_full.shape[-1])
    cells = lat_rows * slabs * lat_cols * (conv_full.shape[-1] // GROUPS)
    table = resize_table(vit_side, pix_side)
    padded_table = jnp.pad(table, ((0, 0), (HALO, HALO)))
    local_rows = lax.dynamic_slice(
        padded_table, (place * res_rows, place * pix_rows), (res_rows, pix_rows + 2 * HALO)
    )
    sigma = flow_sigma(step_index)
    modulated = (
        norm_rows(hidden.astype(jnp.float32), 1e-06)
        * (1.0 + modulation[:, 1].astype(jnp.float32)[:, None, None, :])
        + modulation[:, 0].astype(jnp.float32)[:, None, None, :]
    ).astype(jnp.bfloat16)
    velocity = (
        jnp.einsum("nijd,dk->nijk", modulated, proj_full, preferred_element_type=jnp.float32)
        + proj_bias
    )
    clean = noisy.astype(jnp.float32) - sigma[:, None, None, None] * velocity
    latent = (tokens_to_latent(clean) / LAT_SCALE + LAT_SHIFT).astype(jnp.bfloat16)
    latent_ext = with_halo(latent, (("slab", 1),), 1)
    latent_ext = jnp.pad(latent_ext, ((0, 0), (0, 0), (1, 1), (0, 0)))
    conv_out = (
        jnp.einsum(
            "nrck,ko->nrco",
            conv_columns(latent_ext, lat_rows, lat_cols),
            conv_mat,
            preferred_element_type=jnp.float32,
        )
        + conv_bias
    )
    totals = lax.psum(group_sums(conv_out), "slab")
    normed, inverse = group_apply(conv_out, totals, cells)
    gained = normed * norm_gain + norm_shift
    active_vae, silu_back = jax.vjp(jax.nn.silu, gained)
    cell_vals = (
        jnp.einsum(
            "nrco,ok->nrck",
            active_vae.astype(jnp.bfloat16),
            head_full,
            preferred_element_type=jnp.float32,
        )
        + head_bias
    )
    pixels = cells_to_pixels(cell_vals).astype(jnp.bfloat16)
    pixel_ext = with_halo(pixels, (("slab", 2),), HALO)
    shrunk = jnp.einsum("ik,nckp->ncip", local_rows, pixel_ext.astype(jnp.float32), precision=HIGH)
    shrunk = jnp.einsum("ncip,jp->ncij", shrunk, table, precision=HIGH)
    image = ((shrunk + 1.0) * 0.5 - pix_mean) / pix_std
    patches = image_to_patches(image).astype(jnp.bfloat16)
    embedded = (
        jnp.einsum("ntk,kd->ntd", patches, patch_full, preferred_element_type=jnp.float32)
        + position.astype(jnp.float32)[None]
    )
    pre_x, pre_back = jax.vjp(
        lambda values: affine_norm(values, vit_gain[0], vit_shift[0]), embedded
    )
    unit, unit_back = jax.vjp(lambda values: affine_norm(values, vit_gain[1], vit_shift[1]), pre_x)
    unit_b = unit.astype(jnp.bfloat16)
    class_pre = affine_norm(class_token[None], vit_gain[0], vit_shift[0])
    class_unit = affine_norm(class_pre, vit_gain[1], vit_shift[1]).astype(jnp.bfloat16)
    query = jnp.einsum(
        "nd,dhe->nhe", class_unit, query_w, preferred_element_type=jnp.float32
    ).astype(jnp.bfloat16)
    class_key = jnp.einsum(
        "nd,dhe->nhe", class_unit, key_w, preferred_element_type=jnp.float32
    ).astype(jnp.bfloat16)
    class_val = jnp.einsum(
        "nd,dhe->nhe", class_unit, value_w, preferred_element_type=jnp.float32
    ).astype(jnp.bfloat16)
    pairs = (
        jnp.einsum(
            "ntd,dk->ntk",
            lax.all_gather(unit_b, "slab", axis=1, tiled=True),
            pair_w,
            preferred_element_type=jnp.float32,
        )
        .astype(jnp.bfloat16)
        .reshape(images, tokens, own_heads, 2, HEAD_DIM)
    )
    keys = pairs[:, :, :, 0]
    vals = pairs[:, :, :, 1]
    class_logit = (
        jnp.einsum("nhe,nhe->nh", query, class_key, preferred_element_type=jnp.float32) / root
    )
    token_logits = (
        jnp.einsum("nhe,nthe->nht", query, keys, preferred_element_type=jnp.float32) / root
    )
    class_exp = jnp.exp(class_logit)
    token_exp = jnp.exp(token_logits)
    denominator = class_exp + jnp.sum(token_exp, axis=-1)
    class_weight = class_exp / denominator
    token_weight = token_exp / denominator[..., None]
    class_rounded = class_weight.astype(jnp.bfloat16)
    token_rounded = token_weight.astype(jnp.bfloat16)
    heads = class_rounded.astype(jnp.float32)[..., None] * class_val.astype(
        jnp.float32
    ) + jnp.einsum("nht,nthe->nhe", token_rounded, vals, preferred_element_type=jnp.float32)
    heads_b = heads.astype(jnp.bfloat16).reshape(images, own_heads * HEAD_DIM)
    attn_part = jnp.dot(heads_b, attn_rows, preferred_element_type=jnp.float32)
    block_mid = class_pre + lax.psum(attn_part, "slab") + attn_out_bias
    mlp_input, mid_back = jax.vjp(
        lambda values: affine_norm(values, vit_gain[2], vit_shift[2]), block_mid
    )
    mlp_input_b = mlp_input.astype(jnp.bfloat16)
    in_share, bias_share, out_share = (
        lax.all_gather(mlp_in, "fsdp", axis=1, tiled=True),
        lax.all_gather(mlp_in_bias, "fsdp", axis=0, tiled=True),
        lax.all_gather(mlp_out, "fsdp", axis=0, tiled=True),
    )
    preact = jnp.dot(mlp_input_b, in_share, preferred_element_type=jnp.float32) + bias_share.astype(
        jnp.float32
    )
    active, gelu_back = jax.vjp(exact_gelu, preact)
    mlp_part = jnp.dot(active.astype(jnp.bfloat16), out_share, preferred_element_type=jnp.float32)
    mlp_result = lax.psum(mlp_part, "slab")
    block_out = block_mid + mlp_result + mlp_out_bias
    post, post_back = jax.vjp(
        lambda values: affine_norm(values, vit_gain[3], vit_shift[3]), block_out
    )
    post_b = post.astype(jnp.bfloat16)
    proj_rows_full = lax.all_gather(vit_proj, "fsdp", axis=0, tiled=True)
    embed = jnp.dot(post_b, proj_rows_full, preferred_element_type=jnp.float32)
    score, score_back = jax.vjp(lambda values: match_score(values, text_embed), embed)
    d_embed = score_back(jnp.full_like(score, -1.0 / total_images))[0].astype(jnp.bfloat16)
    d_post = jnp.dot(d_embed, proj_rows_full.T, preferred_element_type=jnp.float32)
    d_second = post_back(d_post)[0]
    d_second_b = d_second.astype(jnp.bfloat16)
    d_active = jnp.dot(d_second_b, out_share.T, preferred_element_type=jnp.float32)
    d_pre = gelu_back(d_active)[0].astype(jnp.bfloat16)
    input_part = jnp.dot(d_pre, in_share.T, preferred_element_type=jnp.float32)
    d_input = lax.psum(input_part, "slab")
    d_first = d_second + mid_back(d_input)[0]
    d_heads = jnp.dot(d_first.astype(jnp.bfloat16), attn_rows.T, preferred_element_type=jnp.float32)
    d_heads = d_heads.astype(jnp.bfloat16).reshape(images, own_heads, HEAD_DIM)
    class_dots = jnp.einsum("nhe,nhe->nh", d_heads, class_val, preferred_element_type=jnp.float32)
    token_dots = jnp.einsum("nhe,nthe->nht", d_heads, vals, preferred_element_type=jnp.float32)
    expected = class_weight * class_dots + jnp.sum(token_weight * token_dots, axis=-1)
    logit_grads = token_weight * (token_dots - expected[..., None])
    key_dir = jnp.einsum("nhe,dhe->nhd", query, key_w, preferred_element_type=jnp.float32)
    value_dir = jnp.einsum("nhe,dhe->nhd", d_heads, value_w, preferred_element_type=jnp.float32)
    scaled = logit_grads / root
    weights_t = token_rounded.astype(jnp.float32)
    spread = jnp.einsum("nht,nhd->ntd", scaled, key_dir, precision=HIGH) + jnp.einsum(
        "nht,nhd->ntd", weights_t, value_dir, precision=HIGH
    )
    d_unit = lax.psum_scatter(
        spread.astype(jnp.bfloat16), "slab", scatter_dimension=1, tiled=True
    ).astype(jnp.float32)
    d_pre_x = unit_back(d_unit)[0]
    d_embedded = pre_back(d_pre_x)[0].astype(jnp.bfloat16)
    d_patches = jnp.einsum(
        "ntd,kd->ntk", d_embedded, patch_full, preferred_element_type=jnp.float32
    )
    d_image = patches_to_image(d_patches, res_rows, vit_side) / (2.0 * pix_std)
    folded = jnp.einsum("ncij,jp->ncip", d_image, table, precision=HIGH)
    d_ext = jnp.einsum("ik,ncip->nckp", local_rows, folded, precision=HIGH)
    rims = jnp.concatenate([d_ext[:, :, :HALO], d_ext[:, :, -HALO:]], axis=2)
    arrived = with_halo(rims.astype(jnp.bfloat16), (("slab", 2),), HALO).astype(rims.dtype)
    d_pixels = d_ext[:, :, HALO : HALO + pix_rows]
    d_pixels = d_pixels.at[:, :, :HALO].add(arrived[:, :, :HALO])
    d_pixels = d_pixels.at[:, :, pix_rows - HALO :].add(arrived[:, :, 3 * HALO :])
    d_cells = pixels_to_cells(d_pixels).astype(jnp.bfloat16)
    d_act = jnp.einsum("nrck,ok->nrco", d_cells, head_full, preferred_element_type=jnp.float32)
    d_normed = silu_back(d_act)[0] * norm_gain
    grad_totals = lax.psum(group_pair(d_normed, normed), "slab")
    d_conv = group_back(d_normed, normed, inverse, grad_totals, cells).astype(jnp.bfloat16)
    d_columns = jnp.einsum("nrco,ko->nrck", d_conv, conv_mat, preferred_element_type=jnp.float32)
    d_lat_ext = columns_back(d_columns, lat_rows, lat_cols)[:, :, 1:-1]
    lat_rims = jnp.concatenate([d_lat_ext[:, :1], d_lat_ext[:, -1:]], axis=1)
    lat_arrived = with_halo(lat_rims, (("slab", 1),), 1)
    d_latent = d_lat_ext[:, 1 : 1 + lat_rows]
    d_latent = d_latent.at[:, 0].add(lat_arrived[:, 0])
    d_latent = d_latent.at[:, lat_rows - 1].add(lat_arrived[:, 3])
    d_clean = latent_to_tokens(d_latent) / LAT_SCALE
    d_velocity = (-sigma[:, None, None, None] * d_clean).astype(jnp.bfloat16)
    grad_local = jnp.einsum(
        "nijd,nijk->dk", modulated, d_velocity, preferred_element_type=jnp.float32
    )
    row_share = lax.psum_scatter(
        grad_local.astype(jnp.bfloat16), "fsdp", scatter_dimension=0, tiled=True
    ).astype(jnp.float32)
    proj_grad = lax.psum(row_share, ("grp", "slab"))
    return (proj_grad, score)


def solution(mesh):
    placed = (
        P(("fsdp", "grp"), "slab", None, None),
        P(("fsdp", "grp"), None, None),
        P(("fsdp", "grp"), "slab", None, None),
        P(("fsdp", "grp")),
        P("fsdp", None),
        P(),
        P(None, None, None, "fsdp"),
        P(),
        P(),
        P(),
        P("fsdp", None),
        P(),
        P(None, "fsdp"),
        P("slab", None),
        P(),
        P(),
        P(),
        P("fsdp", "slab"),
        P("slab", "fsdp"),
        P(),
        P(None, ("fsdp", "slab")),
        P(("fsdp", "slab")),
        P(("fsdp", "slab"), None),
        P(),
        P("fsdp", None),
        P(("fsdp", "grp"), None),
    )
    return jax.shard_map(
        local,
        mesh=mesh,
        in_specs=placed,
        out_specs=(P("fsdp", None), P(("fsdp", "grp"))),
        check_vma=False,
    )
```

profile of v0, /device:TPU:1, one launch (start us, length us, event | category | flops | bytes accessed | tf_op | source)
XLA Modules:
  0.0 1648.1 jit_solution(16606948638825848335)
XLA Ops:
  14.6 72.7 %all-gather.1 = bf16[32,96,64]{1,2,0:T(8,128)(2,1)S(1)} all-gather(bf16[1,96,64]{1,2,0:T(8,128)(2,1)S(1)} %bitcast.284), channel_id=1, replica_groups=mesh['fsdp'=32,'grp'=2,'slab'=8] {'fsdp'}, dimensions={0}, use_global_device_ids=true | all-gather | bytes 405504 | tf_op jit(solution)/shard_map/all_gather | solution.py:204
  100.2 64.0 %all_gather.36 = bf16[512,192]{1,0:T(8,128)(2,1)} all-gather(bf16[16,192]{1,0:T(8,128)(2,1)S(1)} %copy-done.35), channel_id=1, replica_groups=mesh['fsdp'=32,'grp'=2,'slab'=8] {'fsdp'}, dimensions={0}, use_global_device_ids=true | all-gather | bytes 202752 | tf_op jit(solution)/shard_map/all_gather | solution.py:206
  167.4 63.4 %all_gather.39 = bf16[160,1280]{0,1:T(8,128)(2,1)S(1)} all-gather(bf16[160,40]{0,1:T(8,128)(2,1)S(1)} %copy-done.22), channel_id=1, replica_groups=mesh['fsdp'=32,'grp'=2,'slab'=8] {'fsdp'}, dimensions={1}, use_global_device_ids=true | all-gather | bytes 422400 | tf_op jit(solution)/shard_map/all_gather | solution.py:209
  231.5 70.3 %all_gather.35 = bf16[3,3,16,512]{2,1,0,3:T(4,128)(2,1)S(1)} all-gather(bf16[3,3,16,16]{2,1,0,3:T(4,128)(2,1)S(1)} %copy.99), channel_id=1, replica_groups=mesh['fsdp'=32,'grp'=2,'slab'=8] {'fsdp'}, dimensions={3}, use_global_device_ids=true | all-gather | bytes 152064 | tf_op jit(solution)/shard_map/all_gather | solution.py:205
  307.5 19.0 %all-reduce.13 = (f32[1,32]{1,0:T(1,128)S(1)}, f32[1,32]{1,0:T(1,128)S(1)}) all-reduce(f32[1,32]{1,0:T(1,128)S(1)} %bitcast.294, f32[1,32]{1,0:T(1,128)S(1)} %bitcast.292), channel_id=1, replica_groups=mesh['fsdp'=32,'grp'=2,'slab'=8] {'slab'}, use_global_device_ids=true, to_apply=%region_11.12 | all-reduce | flops 64 | bytes 512 | tf_op jit(solution)/shard_map/psum | solution.py:248
  326.8 4.0 add_convert_fusion
  330.9 8.5 copy.101
  339.3 18.7 %convert_element_type.289 = bf16[1,3,128,1024]{3,2,1,0:T(8,128)(2,1)S(1)} reshape(bf16[1,3,16,8,128,8]{5,4,3,2,1,0:T(8,128)(2,1)} %bitcast.253) | data formatting | bytes 1572864 | tf_op jit(solution)/shard_map/convert_element_type | solution.py:261
  364.6 59.4 %all-reduce.11 = bf16[640]{0:T(1024)(128)(2,1)S(1)} all-reduce(bf16[640]{0:T(1024)(128)(2,1)S(1)} %dynamic-update-slice.12), channel_id=1, replica_groups=mesh['fsdp'=32,'grp'=2,'slab'=8] {'fsdp'}, use_global_device_ids=true, to_apply=%add.11 | all-reduce | flops 640 | bytes 2560
  433.8 24.4 %all-gather = bf16[256,1280]{1,0:T(8,128)(2,1)S(1)} all-gather(bf16[32,1280]{1,0:T(8,128)(2,1)S(1)} %add_convert_fusion.2), channel_id=2, replica_groups=mesh['fsdp'=32,'grp'=2,'slab'=8] {'slab'}, dimensions={0}, use_global_device_ids=true | all-gather | bytes 737280 | tf_op jit(solution)/shard_map/all_gather | solution.py:290
  460.0 13.5 psum.58
  479.9 115.6 %all-gather.18.cloned.1.call-done = bf16[32,20,1280]{2,1,0:T(8,128)(2,1)} async-done(((bf16[1,20,1280]{2,1,0:T(8,128)(2,1)}), bf16[32,20,1280]{2,1,0:T(8,128)(2,1)}) %all-gather.18.cloned.1.call-update) | async-done | bytes 1638416 | tf_op jit(solution)/shard_map/all_gather | solution.py:325
  598.2 15.0 psum.59
  616.7 129.5 %all-gather.14.cloned.1.call-done = bf16[1280,1024]{1,0:T(8,128)(2,1)} async-done(((bf16[40,1024]{1,0:T(8,128)(2,1)}), bf16[1280,1024]{1,0:T(8,128)(2,1)}) %all-gather.14.cloned.1.call-update) | async-done | bytes 2621456 | tf_op jit(solution)/shard_map/all_gather | solution.py:338
  751.9 3.2 multiply_reduce_fusion.6
  757.9 15.5 psum.60
  785.2 45.0 %reduce-scatter.5.cloned.1.call-done = bf16[1,32,1280]{2,1,0:T(8,128)(2,1)} async-done(((bf16[1,256,1280]{2,1,0:T(8,128)(2,1)}), bf16[1,32,1280]{2,1,0:T(8,128)(2,1)}) %reduce-scatter.5.cloned.1.call-update) | async-done | bytes 81936 | tf_op jit(solution)/shard_map/reduce_scatter | solution.py:363
  844.7 15.7 convert_element_type.320
  860.4 10.0 copy.105
  870.6 6.0 fusion.159
  876.9 14.3 all-reduce.12
  891.5 4.8 fusion.22
  910.0 661.2 %reduce-scatter.7.cloned.1.call-done = bf16[96,64]{1,0:T(8,128)(2,1)} async-done(((bf16[3072,64]{1,0:T(8,128)(2,1)}), bf16[96,64]{1,0:T(8,128)(2,1)}) %reduce-scatter.7.cloned.1.call-update) | async-done | bytes 12304
  1572.0 68.1 %psum.63 = f32[96,64]{0,1:T(8,128)} all-reduce(bf16[96,64]{0,1:T(8,128)(2,1)S(1)} %copy.130), channel_id=1, replica_groups=mesh['fsdp'=32,'grp'=2,'slab'=8] {'grp','slab'}, use_global_device_ids=true, to_apply=%region_45.46 | all-reduce | flops 6144 | bytes 36864 | tf_op jit(solution)/shard_map/psum | solution.py:399
  (314 shorter events, 97.6 us)
Async XLA Ops:
  7.2 419.6 %all-gather.10.cloned.1.call-start = ((), (), s32[]{:S(2)}) async-start(), calls=%async_computation.2 | async-start | bytes 1351680 | tf_op jit(solution)/shard_map/all_gather | solution.py:208
  7.9 421.8 %all-gather.12.cloned.1.call-start = ((), (), s32[]{:S(2)}) async-start(), calls=%async_computation.3 | async-start | bytes 1689600 | tf_op jit(solution)/shard_map/all_gather | solution.py:207
  8.7 467.5 %all-gather.16.cloned.1.call-start = ((), (), s32[]{:S(2)}) async-start(), calls=%async_computation.6 | async-start | bytes 2027520 | tf_op jit(solution)/shard_map/all_gather | solution.py:323
  9.4 586.1 %all-gather.18.cloned.1.call-start = ((), (), s32[]{:S(2)}) async-start(), calls=%async_computation.7 | async-start | bytes 2027520 | tf_op jit(solution)/shard_map/all_gather | solution.py:325
  10.0 736.3 %all-gather.14.cloned.1.call-start = ((), (), s32[]{:S(2)}) async-start(), calls=%async_computation.4 | async-start | bytes 2703360 | tf_op jit(solution)/shard_map/all_gather | solution.py:338
  94.5 136.3 %copy-start.12 = (f32[4,1280]{1,0:T(4,128)S(1)}, f32[4,1280]{1,0:T(4,128)}, u32[]{:S(2)}) copy-start(f32[4,1280]{1,0:T(4,128)} %param.51) | copy-start | bytes 61444
  94.5 136.3 %copy-start.16 = (f32[4,1280]{1,0:T(4,128)S(1)}, f32[4,1280]{1,0:T(4,128)}, u32[]{:S(2)}) copy-start(f32[4,1280]{1,0:T(4,128)} %param.52) | copy-start | bytes 61444
  96.3 207.3 %collective-permute-start = (bf16[1,1,128,16]{2,3,1,0:T(8,128)(2,1)S(1)}, bf16[1,1,128,16]{2,3,1,0:T(8,128)(2,1)S(1)}, u32[]{:S(2)}, u32[]{:S(2)}) collective-permute-start(bf16[1,1,128,16]{2,3,1,0:T(8,128)(2,1)S(1)} %get-tuple-element.101), channel_id=1, source_target_pairs={{0,1},{1,2},{2,3},{3,4},{4,5},{5,6},{6,7},{8,9},{9,10},{10,11},{11... | collective-permute-start | bytes 12296 | tf_op jit(solution)/shard_map/ppermute | solution.py:25
  98.6 205.1 %collective-permute-start.1 = (bf16[1,1,128,16]{2,3,1,0:T(8,128)(2,1)S(1)}, bf16[1,1,128,16]{2,3,1,0:T(8,128)(2,1)S(1)}, u32[]{:S(2)}, u32[]{:S(2)}) collective-permute-start(bf16[1,1,128,16]{2,3,1,0:T(8,128)(2,1)S(1)} %get-tuple-element.102), channel_id=1, source_target_pairs={{1,0},{2,1},{3,2},{4,3},{5,4},{6,5},{7,6},{9,8},{10,9},{11,10},{12... | collective-permute-start | bytes 12296 | tf_op jit(solution)/shard_map/ppermute | solution.py:28
  99.9 730.3 %reduce-scatter.5.cloned.1.call-start = ((), (), s32[]{:S(2)}) async-start(), calls=%async_computation.5 | async-start | bytes 737280 | tf_op jit(solution)/shard_map/reduce_scatter | solution.py:363
  100.0 324.6 %copy-start.37 = (f32[224]{0:T(256)}, f32[224]{0:T(256)S(1)}, u32[]{:S(2)}) copy-start(f32[224]{0:T(256)S(1)} %add_multiply_fusion.2) | copy-start | bytes 2692
  164.5 260.2 %copy-start.39 = (f32[224]{0:T(256)}, f32[224]{0:T(256)S(1)}, u32[]{:S(2)}) copy-start(f32[224]{0:T(256)S(1)} %fusion.40) | copy-start | bytes 2692
  164.5 139.8 %copy-start.25 = (f32[512]{0:T(512)S(1)}, f32[512]{0:T(512)}, u32[]{:S(2)}) copy-start(f32[512]{0:T(512)} %param.43) | copy-start | bytes 6148
  164.8 259.3 %copy-start.3 = (f32[224,1024]{1,0:T(8,128)}, f32[224,1024]{1,0:T(8,128)S(1)}, u32[]{:S(2)}) copy-start(f32[224,1024]{1,0:T(8,128)S(1)} %fusion.39) | copy-start | bytes 2752516
  230.8 228.9 %copy-start.7 = (bf16[160,1280]{0,1:T(8,128)(2,1)}, bf16[160,1280]{0,1:T(8,128)(2,1)S(1)}, u32[]{:S(2)}) copy-start(bf16[160,1280]{0,1:T(8,128)(2,1)S(1)} %all_gather.39) | copy-start | bytes 1228804
  339.3 85.3 %copy-start.63 = (f32[3]{0:T(128)S(1)}, f32[3]{0:T(128)}, u32[]{:S(2)}) copy-start(f32[3]{0:T(128)} %constant.346) | copy-start | bytes 40
  358.1 66.0 %collective-permute-start.2 = (bf16[1,3,2,1024]{3,2,1,0:T(2,128)(2,1)S(1)}, bf16[1,3,2,1024]{3,2,1,0:T(2,128)(2,1)S(1)}, u32[]{:S(2)}, u32[]{:S(2)}) collective-permute-start(bf16[1,3,2,1024]{3,2,1,0:T(2,128)(2,1)S(1)} %get-tuple-element.97), channel_id=1, source_target_pairs={{0,1},{1,2},{2,3},{3,4},{4,5},{5,6},{6,7},{8,9},{9,10},{10,11},{11... | collective-permute-start | bytes 36872 | tf_op jit(solution)/shard_map/ppermute | solution.py:25
  359.8 64.2 %collective-permute-start.3 = (bf16[1,3,2,1024]{3,2,1,0:T(2,128)(2,1)S(1)}, bf16[1,3,2,1024]{3,2,1,0:T(2,128)(2,1)S(1)}, u32[]{:S(2)}, u32[]{:S(2)}) collective-permute-start(bf16[1,3,2,1024]{3,2,1,0:T(2,128)(2,1)S(1)} %get-tuple-element.98), channel_id=1, source_target_pairs={{1,0},{2,1},{3,2},{4,3},{5,4},{6,5},{7,6},{9,8},{10,9},{11,10},{12... | collective-permute-start | bytes 36872 | tf_op jit(solution)/shard_map/ppermute | solution.py:28
  616.7 140.8 %copy-start.24 = (f32[640]{0:T(1024)S(1)}, f32[640]{0:T(1024)}, u32[]{:S(2)}) copy-start(f32[640]{0:T(1024)} %get-tuple-element.75) | copy-start | bytes 7684
  783.4 787.8 %reduce-scatter.7.cloned.1.call-start = ((), (), s32[]{:S(2)}) async-start(), calls=%async_computation.8 | async-start | bytes 811008
  838.7 2.9 collective-permute-start.4
  840.0 4.4 collective-permute-start.5
  897.0 3.4 collective-permute-start.6
  899.1 4.4 collective-permute-start.7
  (55 other events, 1341.4 us)
Sparse Core Ops, SparseCore 0:
  11.1 142.9 all-gather.9
  157.2 144.4 all-gather.11
  304.8 144.1 all-gather.15
  451.9 143.5 all-gather.17
  598.4 147.8 all-gather.13
  783.4 46.7 reduce-scatter.4
  909.5 661.6 reduce-scatter.6
where the time goes:
time: 1650 us
  waiting for transfers between devices  960 us (58%)
  blocking collectives  499 us (30%)
  local copies, waits for them, and re-layouts  78.1 us (5%)
  matrix products  45 us (3%)
  between operations  28.8 us (2%)
  other arithmetic  24.1 us (1%)
    unnamed x8, waiting for transfers between devices  664 us
    all_gather x1, waiting for transfers between devices, local(): proj_rows_full = lax.all_gather(vit_proj, 'fsdp', axis=0, tiled=True)  130 us
    all_gather x1, waiting for transfers between devices, local(): lax.all_gather(mlp_out, 'fsdp', axis=0, tiled=True)  116 us
    all_gather x1, blocking collectives, local(): lax.all_gather(proj_weight, 'fsdp', axis=0, tiled=True)  72.7 us
    all_gather x1, blocking collectives, local(): lax.all_gather(conv_weight, 'fsdp', axis=3, tiled=True)  70.3 us
    psum x1, blocking collectives, local(): proj_grad = lax.psum(row_share, ('grp', 'slab'))  68.1 us
    all_gather x1, blocking collectives, local(): lax.all_gather(head_weight, 'fsdp', axis=0, tiled=True)  64 us
    all_gather x1, blocking collectives, local(): lax.all_gather(attn_out, 'fsdp', axis=1, tiled=True)  63.4 us
  transfers between devices with their start and end apart: 15, of which 6 were waited for; matrix products, arithmetic and copies ran while one was open for 5% of the time, Pallas kernels for 0%

commit v1 on v0

v1 whole, which is shorter than its diff:
```python
import functools

import jax
import jax.numpy as jnp
import numpy as np
from jax import lax
from jax.experimental import pallas as pl
from jax.experimental.pallas import tpu as pltpu
from jax.sharding import PartitionSpec as P

HEAD_DIM = 80
STEPS = 28
LAT_SCALE = 0.3611
LAT_SHIFT = 0.1159
PIX_MEAN = (0.48145466, 0.4578275, 0.40821073)
PIX_STD = (0.26862954, 0.26130258, 0.27577711)
HIGH = lax.Precision.HIGHEST
MESH = pl.DeviceIdType.MESH
F32 = jnp.float32
BF16 = jnp.bfloat16
ANY = pl.BlockSpec(memory_space=pl.ANY)
VMEM = pl.BlockSpec(memory_space=pltpu.VMEM)
SMEM = pl.BlockSpec(memory_space=pltpu.SMEM)
ROOT = HEAD_DIM**0.5
WIDTH = 1280
WIDE = 1536
CELLS = 128 * 128 * 16
NF, NS, NZ = 32, 8, 16
LANES = 2048


def nn(a, b, precision=None):
    return lax.dot_general(
        a, b, (((1,), (0,)), ((), ())), precision=precision, preferred_element_type=F32
    )


def nt(a, b, precision=None):
    return lax.dot_general(
        a, b, (((1,), (1,)), ((), ())), precision=precision, preferred_element_type=F32
    )


def halves(values):
    high = values.astype(BF16)
    return high, (values - high.astype(F32)).astype(BF16)


def three(product, a, b):
    return product(a[0], b[0]) + (product(a[1], b[0]) + product(a[0], b[1]))


def remote(source, dest, send, recv, target):
    return pltpu.make_async_remote_copy(
        src_ref=source, dst_ref=dest, send_sem=send, recv_sem=recv,
        device_id=target, device_id_type=MESH,
    )


def iota(shape, dim):
    return lax.broadcasted_iota(jnp.int32, shape, dim)


def norm_stats(values, mask, epsilon):
    average = jnp.sum(values, axis=-1, keepdims=True) * (1.0 / WIDTH)
    centered = (values - average) * mask
    square = jnp.sum(centered * centered, axis=-1, keepdims=True) * (1.0 / WIDTH)
    inverse = 1.0 / jnp.sqrt(square + epsilon)
    return centered * inverse, inverse


def norm_back(grads, scaled, inverse, gain):
    grads = grads * gain
    first = jnp.sum(grads, axis=-1, keepdims=True) * (1.0 / WIDTH)
    second = jnp.sum(grads * scaled, axis=-1, keepdims=True) * (1.0 / WIDTH)
    return (grads - first - scaled * second) * inverse


class Weights:
    def __init__(self, s_in, r_in, s_buf, r_buf, sems):
        self.s_in, self.r_in, self.s_buf, self.r_buf = s_in, r_in, s_buf, r_buf
        (self.z_send, self.z_recv, self.sh_send, self.sh_recv, self.fw_send, self.fw_recv,
         self.loc, self.pair_sem, self.ring_send, self.ring_recv, self.core_sem) = sems
        self.f = lax.axis_index("fsdp")
        self.g = lax.axis_index("grp")
        self.s = lax.axis_index("slab")
        self.w = self.g * NS + self.s
        self.z, self.half = self.f // 2, lax.rem(self.f, 2)
        self.core = {"grp": 1 - self.g}
        self.sent = []

    def r_start(self, slot):
        source = self.r_in.at[slot, self.w]
        mine = pltpu.make_async_copy(
            source, self.r_buf.at[slot, self.w, self.f], self.loc.at[slot]
        )
        mine.start()

        def send(d, carry):
            target = {"fsdp": lax.rem(self.f + d, NF)}
            remote(
                source, self.r_buf.at[slot, self.w, self.f],
                self.z_send.at[slot], self.z_recv.at[slot], target,
            ).start()
            return carry

        lax.fori_loop(1, NF, send, 0)

    def r_share(self, slot):
        block = self.r_buf.at[slot, self.w]
        many = self.r_buf.at[slot, self.w, pl.ds(0, NF - 1)]
        remote(many, many, self.z_send.at[slot], self.z_recv.at[slot], self.core).wait_recv()
        pltpu.make_async_copy(
            self.r_in.at[slot, self.w], self.r_buf.at[slot, self.w, self.f], self.loc.at[slot]
        ).wait()
        for d in range(1, NS):
            remote(
                block, block, self.sh_send.at[slot, d - 1], self.sh_recv.at[slot, d - 1],
                {"slab": lax.rem(self.s + d, NS)},
            ).start()

    def r_core(self, slot):
        for d in range(1, NS):
            block = self.r_buf.at[slot, self.g * NS + lax.rem(self.s + NS - d, NS)]
            remote(
                block, block, self.sh_send.at[slot, d - 1], self.sh_recv.at[slot, d - 1], self.core
            ).wait_recv()
        many = self.r_buf.at[slot, pl.ds(self.g * NS, NS)]
        remote(many, many, self.fw_send.at[slot], self.fw_recv.at[slot], self.core).start()

    def r_done(self, slot):
        many = self.r_buf.at[slot, pl.ds((1 - self.g) * NS, NS)]
        remote(many, many, self.fw_send.at[slot], self.fw_recv.at[slot], self.core).wait_recv()

    def s_pair(self):
        dest = self.s_buf.at[self.g, self.z, self.half]
        return remote(
            self.s_in.at[self.g], dest, self.pair_sem.at[0], self.pair_sem.at[1],
            {"fsdp": self.z * 2 + 1 - self.half},
        ), pltpu.make_async_copy(self.s_in.at[self.g], dest, self.loc.at[3])

    def s_start(self):
        for copy in self.s_pair():
            copy.start()

    def s_step(self, step, way):
        sign = NZ - 1 if way == 0 else 1
        block = self.s_buf.at[self.g, lax.rem(self.z + sign * step, NZ)]
        hop = 1 if way == 0 else NZ - 1
        target = {"fsdp": lax.rem(self.z + hop, NZ) * 2 + self.half}
        slot = way * 8 + step
        return remote(block, block, self.ring_send.at[slot], self.ring_recv.at[slot], target)

    def s_share(self, block):
        block = self.s_buf.at[self.g, lax.rem(block, NZ)]
        remote(block, block, self.core_sem.at[0], self.core_sem.at[1], self.core).start()

    def s_pump(self, step):
        steps = (NZ // 2, NZ // 2 - 1)
        if step == 0:
            pair, own = self.s_pair()
            own.wait()
            pair.wait_recv()
            self.s_share(self.z)
        for way in (0, 1):
            if 0 < step <= steps[way]:
                self.s_step(step - 1, way).wait_recv()
            if step < steps[way]:
                self.s_step(step, way).start()
            if 0 < step <= steps[way]:
                self.s_share(self.z + (NZ - step if way == 0 else step))

    def s_done(self):
        theirs, mine = self.s_buf.at[1 - self.g], self.s_buf.at[self.g]
        remote(theirs, theirs, self.core_sem.at[0], self.core_sem.at[1], self.core).wait_recv()
        remote(mine, mine, self.core_sem.at[0], self.core_sem.at[1], self.core).wait_send()
        self.s_pair()[0].wait_send()
        for way, steps in ((0, NZ // 2), (1, NZ // 2 - 1)):
            for step in range(steps):
                self.s_step(step, way).wait_send()

    def r_finish(self, slot):
        many = self.r_buf.at[slot, self.w, pl.ds(0, NF - 1)]
        remote(many, many, self.z_send.at[slot], self.z_recv.at[slot], self.core).wait_send()
        block = self.r_buf.at[slot, self.w]
        for d in range(1, NS):
            remote(
                block, block, self.sh_send.at[slot, d - 1], self.sh_recv.at[slot, d - 1], self.core
            ).wait_send()
        many = self.r_buf.at[slot, pl.ds(self.g * NS, NS)]
        remote(many, many, self.fw_send.at[slot], self.fw_recv.at[slot], self.core).wait_send()


def greet(targets):
    barrier = pltpu.get_barrier_semaphore()
    for target in targets:
        pl.semaphore_signal(barrier, inc=1, device_id=target, device_id_type=MESH)
    pl.semaphore_wait(barrier, len(targets))


def block_targets(g, s):
    found = []
    for d in range(1, 2 * NS):
        other_g = lax.rem(g + d // NS, 2)
        other_s = lax.rem(s + d % NS, NS)
        found.append((other_g * NS + other_s, {"grp": other_g, "slab": other_s}))
    return found


def greet_all():
    f, g, s = lax.axis_index("fsdp"), lax.axis_index("grp"), lax.axis_index("slab")
    greet(
        [target for _, target in block_targets(g, s)]
        + [{"fsdp": lax.rem(f + d, NF)} for d in range(1, NF)]
    )


def reduce_gradient(mine, landed, terms, arrived, collected, sems):
    a_send, a_recv, b_send, b_recv, c_send, c_recv = sems
    f, g, s = lax.axis_index("fsdp"), lax.axis_index("grp"), lax.axis_index("slab")
    w = g * NS + s
    block = block_targets(g, s)
    copies = []
    for d, (index, target) in enumerate(block):
        copy = remote(mine.at[index], landed.at[w], a_send.at[d], a_recv.at[d], target)
        copy.start()
        copies.append(copy)
    landed[w] = mine[w]
    for copy in copies:
        copy.wait()
    total = landed[0].astype(F32)
    for index in range(1, 2 * NS):
        total = total + landed[index].astype(F32)
    for index in range(NF):
        rows, lanes = 4 * (index // 8), 96 * (index % 8)
        terms[index, :, 0:96] = total[rows : rows + 4, lanes : lanes + 96]
        terms[index, :, 96:128] = jnp.zeros((4, 32), F32)
    copies = []
    for d in range(1, NF):
        p = lax.rem(f + d, NF)
        copy = remote(terms.at[p], arrived.at[f], b_send.at[d - 1], b_recv.at[d - 1], {"fsdp": p})
        copy.start()
        copies.append(copy)
    arrived[f] = terms[f]
    for copy in copies:
        copy.wait()
    collected[w] = jnp.sum(arrived[...], axis=0)
    copies = []
    for d, (index, target) in enumerate(block):
        copy = remote(collected.at[w], collected.at[w], c_send.at[d], c_recv.at[d], target)
        copy.start()
        copies.append(copy)
    for copy in copies:
        copy.wait()


def step_kernel(
    fetch, hidden, s_in, r_in, mods, noisy, sigma_ref, proj_bias, vecs, text, chan, head_bias,
    perm, perm_t, inter, tth, ttl, rmh, rml, ph0, ph1, lane_rows,
    grad_out, score_out,
    hid, mod, s_buf, r_buf, proj_full, ext, halo_out, halo_in, nrm, dnrm, acc, stat_out, stat_in,
    cols_buf, pix, head_t, head_p, edge_out, edge_in, kd_out, kd_in, dirs, u_out, u_in,
    row_out, row_in, vd_out, vd_in, rim_out, rim_in, gsplit, mine, landed, terms, arrived, collected,
    x_send, x_recv, hid_sem, *sems,
):
    s = lax.axis_index("slab")
    low, high = s > 0, s < NS - 1
    low_f, high_f = jnp.where(low, 1.0, 0.0), jnp.where(high, 1.0, 0.0)
    before, after = {"slab": lax.rem(s + NS - 1, NS)}, {"slab": lax.rem(s + 1, NS)}
    hid_copy = pltpu.make_async_copy(hidden, hid, hid_sem.at[0])
    hid_copy.start()
    sigma = sigma_ref[0, 0]
    live = []

    def to_all(kind, source, dest, swap=False):
        copies = []
        for d in range(1, NS):
            p = lax.rem(s + d, NS)
            copies.append(
                remote(
                    source.at[p] if swap else source, dest.at[s],
                    x_send.at[kind, d - 1], x_recv.at[kind, d - 1], {"slab": p},
                )
            )
        for copy in copies:
            copy.start()
        live.extend(copies)
        return copies

    def to_sides(kind, source, dest):
        copies = [
            remote(source.at[0], dest.at[0], x_send.at[kind, 0], x_recv.at[kind, 0], after),
            remote(source.at[1], dest.at[1], x_send.at[kind, 1], x_recv.at[kind, 1], before),
        ]
        for copy in copies:
            copy.start()
        live.extend(copies)
        return copies

    def landed_all(copies):
        for copy in copies:
            copy.wait_recv()

    if fetch:
        greet_all()
        weights = Weights(s_in, r_in, s_buf, r_buf, sems[:11])
        weights.r_start(0)
        weights.s_start()
        weights.r_start(1)
        weights.r_start(2)
    else:
        greet([{"slab": lax.rem(s + d, NS)} for d in range(1, NS)])
        s_buf[...] = s_in[...]
        r_buf[...] = r_in[...]
        weights = None

    def pump(step):
        if weights is not None:
            weights.s_pump(step)

    hid_copy.wait()
    scale = 1.0 + mods[1:2].astype(F32)
    shift = mods[0:1].astype(F32)

    def modulate(lo, hi):
        def body(i, carry):
            rows = pl.ds(pl.multiple_of(i * 16, 16), 16)
            values = hid[rows, :].astype(F32)
            average = jnp.mean(values, axis=-1, keepdims=True)
            centered = values - average
            square = jnp.mean(centered * centered, axis=-1, keepdims=True)
            scaled = centered * (1.0 / jnp.sqrt(square + 1e-06))
            mod[rows, :] = (scaled * scale + shift).astype(BF16)
            return carry

        lax.fori_loop(lo, hi, body, 0)

    modulate(0, 16)
    pump(0)
    modulate(16, 32)
    if weights is not None:
        weights.r_share(0)
        weights.s_pump(1)
        weights.r_core(0)
        weights.r_done(0)

    def blocks(first, count):
        parts = [r_buf[n // 16, n % 16] for n in range(first, first + count)]
        return jnp.concatenate(parts, axis=1).reshape(NF * 16 * count, 128)

    def s_unit(index):
        return s_buf[index // 9, :, :, index % 9].reshape(WIDE, 128)

    for f in range(NF):
        for n in range(6):
            proj_full[96 * f + 16 * n : 96 * f + 16 * n + 16, :] = r_buf[0, n, f]
    velocity = nn(mod[...], proj_full[...])[:, :64] + proj_bias[...]
    clean = noisy[...].astype(F32) - sigma * velocity
    lat_tok = (clean / LAT_SCALE + LAT_SHIFT).astype(BF16)
    tok_t = nt(perm_t[...], lat_tok)
    stacked = jnp.concatenate(
        [
            jnp.concatenate(
                [tok_t[0:32, 128 * k : 128 * k + 128], tok_t[32:64, 128 * k : 128 * k + 128]], axis=1
            )
            for k in range(4)
        ],
        axis=0,
    ).astype(BF16)
    latent = nn(stacked, inter[...]).astype(BF16)
    for k in range(4):
        for i2 in range(2):
            for p in range(2):
                r = 4 * k + 2 * i2 + p + 1
                for b in range(3):
                    at = (i2 * 3 + b) * 128
                    ext[16 * b : 16 * b + 16, 128 * r : 128 * r + 128] = latent[
                        32 * k + 16 * p : 32 * k + 16 * p + 16, at : at + 128
                    ]
    halo_out[0] = ext[:, 2048:2176]
    halo_out[1] = ext[:, 128:256]
    copies = to_sides(0, halo_out, halo_in)
    identity = (iota((512, 512), 0) == iota((512, 512), 1)).astype(F32)
    same = (iota((512, 512), 0) // 16 == iota((512, 512), 1) // 16).astype(F32)
    chan_cols = nt(identity, chan[...], HIGH)
    conv_bias, gain, gshift = chan_cols[:, 0:1], chan_cols[:, 1:2], chan_cols[:, 2:3]
    eye = (iota((128, 128), 0) == iota((128, 128), 1)).astype(BF16)
    conv0 = r_buf[0, 6].reshape(512, 128)
    head0 = r_buf[0, 7].reshape(512, 128)
    tail = r_buf[0, 8].reshape(512, 128)
    head_p[...] = (nn(head0, ph0[...]) + nn(tail, ph1[...])).astype(BF16)
    head_t[...] = (
        lax.dot_general(ph0[...], head0, (((0,), (1,)), ((), ())), preferred_element_type=F32)
        + lax.dot_general(ph1[...], tail, (((0,), (1,)), ((), ())), preferred_element_type=F32)
    ).astype(BF16)
    bias_cols = nt(
        lax.dot_general(
            ph0[...].astype(F32), eye.astype(F32), (((0,), (0,)), ((), ())),
            preferred_element_type=F32,
        ),
        head_bias[:, 0:128], HIGH,
    ) + nt(
        lax.dot_general(
            ph1[...].astype(F32), eye.astype(F32), (((0,), (0,)), ((), ())),
            preferred_element_type=F32,
        ),
        head_bias[:, 128:256], HIGH,
    )
    head_col = bias_cols[:, 0:1]
    pump(2)
    landed_all(copies)
    ext[:, 0:128] = (halo_in[0].astype(F32) * low_f).astype(BF16)
    ext[:, 2176:2304] = (halo_in[1].astype(F32) * high_f).astype(BF16)
    acc[...] = jnp.zeros_like(acc)

    def conv_chunk(i, carry):
        at = pl.multiple_of(i * 256, 256)
        parts = [ext[:, pl.ds(pl.multiple_of(at + 128 * a, 128), 256)] for a in range(3)]
        columns = jnp.concatenate(parts + [jnp.zeros((112, 256), BF16)], axis=0)
        out = nn(conv0, columns[0:128]) + nn(tail, columns[128:256]) + conv_bias
        nrm[:, pl.ds(at, 256)] = out
        acc[0] += out[:, 0:128] + out[:, 128:256]
        square = out * out
        acc[1] += square[:, 0:128] + square[:, 128:256]
        return carry

    lax.fori_loop(0, 8, conv_chunk, 0)

    def group_totals(kind, step=None):
        ones = jnp.ones((8, 128), F32)
        first, second = nt(ones, acc[0], HIGH), nt(ones, acc[1], HIGH)
        k = kind - 1
        stat_out[k] = jnp.where(iota((8, 512), 0) == 0, first, second)
        copies = to_all(kind, stat_out.at[k], stat_in.at[k])
        stat_in[k, s] = stat_out[k]
        if step is not None:
            pump(step)
        landed_all(copies)
        total = stat_in[k, 0]
        for index in range(1, NS):
            total = total + stat_in[k, index]
        columns = nt(same, total, HIGH)
        return columns[:, 0:1] * (1.0 / CELLS), columns[:, 1:2] * (1.0 / CELLS)

    average, square = group_totals(1, 3)
    inverse = 1.0 / jnp.sqrt(square - average * average + 1e-06)
    if weights is not None:
        weights.r_share(1)
        weights.r_share(2)

    def head_chunk(i, carry):
        at = pl.multiple_of(i * 256, 256)
        normed = (nrm[:, pl.ds(at, 256)] - average) * inverse
        nrm[:, pl.ds(at, 256)] = normed
        gained = normed * gain + gshift
        active = (gained * (1.0 / (1.0 + jnp.exp(-gained)))).astype(BF16)
        cells = (nn(head_t[...], active) + head_col).astype(BF16)
        for rr in range(2):
            rows = pl.ds(pl.multiple_of(i * 64 + 32 * rr, 32), 32)
            for x in range(8):
                pix[rows, 128 * x : 128 * x + 128] = cells[
                    32 * x : 32 * x + 32, 128 * rr : 128 * rr + 128
                ]
        return carry

    lax.fori_loop(0, 8, head_chunk, 0)
    pump(4)
    narrow = halves(nt(tth[...], pix[...]) + nt(ttl[...], pix[...]))
    raw = jnp.zeros((80, 512), F32)
    for m in range(3):
        part = [half[80 * m : 80 * m + 80] for half in narrow]
        table = [rmh[512 * m : 512 * m + 512, :], rml[512 * m : 512 * m + 512, :]]
        raw = raw + three(nn, part, table)
    edge_out[0, 0] = raw[:, 256:384]
    edge_out[0, 1] = raw[:, 384:512]
    copies = to_sides(2 + 1, edge_out.at[0], edge_in.at[0])
    pump(5)
    if weights is not None:
        weights.r_core(1)
        weights.s_pump(6)
    corr0 = jnp.where(low, 1.0, lane_rows[0:1, :])
    corr1 = jnp.where(high, 1.0, lane_rows[1:2, :])
    img_scale, img_shift = lane_rows[2:3, :], lane_rows[3:4, :]
    if weights is not None:
        weights.r_done(1)
    landed_all(copies)
    top = (raw[:, 0:128] * corr0 + edge_in[0, 0] * low_f) * img_scale + img_shift
    bottom = (raw[:, 128:256] * corr1 + edge_in[0, 1] * high_f) * img_scale + img_shift
    patches = jnp.concatenate(
        [
            jnp.concatenate([part[16 * u : 16 * u + 16] for u in range(5)], axis=1)
            for part in (top, bottom)
        ],
        axis=0,
    ).astype(BF16)
    embedded = vecs[16:48, :]
    for u in range(5):
        embedded = embedded + nt(patches[:, 128 * u : 128 * u + 128], blocks(9 + 3 * u, 3))
    lane = iota((1, WIDE), 1)
    inner = lax.rem(lane, 48)
    mask = (inner < 40).astype(F32)
    gains = [vecs[1 + i : 2 + i, :] for i in range(4)]
    shifts = [vecs[5 + i : 6 + i, :] for i in range(4)]
    hat0, inv0 = norm_stats(embedded, mask, 1e-05)
    hat1, inv1 = norm_stats(hat0 * gains[0] + shifts[0], mask, 1e-05)
    unit = hat1 * gains[1] + shifts[1]
    unit_b = unit.astype(BF16)
    unit = unit_b.astype(F32)
    if weights is not None:
        weights.s_pump(7)
        weights.r_core(2)
        weights.s_pump(8)
        weights.s_done()

    class_hat, _ = norm_stats(vecs[0:1, :], mask, 1e-05)
    class_pre = class_hat * gains[0] + shifts[0]
    class_hat, _ = norm_stats(class_pre, mask, 1e-05)
    class_unit = jnp.broadcast_to(class_hat * gains[1] + shifts[1], (8, WIDE)).astype(BF16)
    attn = [s_unit(i) for i in range(4)]
    class_qkv = jnp.concatenate([nn(class_unit, attn[i]) for i in range(4)], axis=1)
    class_qkv = class_qkv.astype(BF16).astype(F32)
    place512 = iota((8, 512), 1)
    row512 = iota((8, 512), 0)
    start = jnp.where(row512 == 0, 0, 240)
    in_head = row512 < 2
    key_at = in_head & (place512 >= start + 80) & (place512 < start + 160)
    val_at = in_head & (place512 >= start + 160) & (place512 < start + 240)
    query = jnp.where(key_at, pltpu.roll(class_qkv, 80, 1), 0.0)
    class_exp = jnp.exp(jnp.sum(query * class_qkv, axis=-1, keepdims=True) / ROOT)
    query_b = query.astype(BF16)
    key_dir = nt(query_b[:, 0:128], attn[0])
    for i in range(1, 4):
        key_dir = key_dir + nt(query_b[:, 128 * i : 128 * i + 128], attn[i])
    kd_out[...] = key_dir[0:2]
    copies = to_all(4, kd_out, kd_in)
    kd_in[s] = key_dir[0:2]
    landed_all(copies)
    for index in range(NS):
        dirs[2 * index : 2 * index + 2, :] = kd_in[index]
    token_exp = jnp.exp(nt(dirs[0:16, :], unit, HIGH) / ROOT)
    gathered = nn(token_exp, unit, HIGH)
    sums = jnp.broadcast_to(jnp.sum(token_exp, axis=1, keepdims=True), (16, WIDE))
    for index in range(NS):
        u_out[index, 0:2] = gathered[2 * index : 2 * index + 2]
        u_out[index, 2:4] = sums[2 * index : 2 * index + 2]
    copies = to_all(5, u_out, u_in, swap=True)
    u_in[s] = u_out[s]
    landed_all(copies)
    total = u_in[0]
    for index in range(1, NS):
        total = total + u_in[index]
    denominator = class_exp[0:2] + total[2:4, 0:1]
    mixed = halves(jnp.concatenate([total[0:2], jnp.zeros((6, WIDE), F32)], axis=0))
    first = nn(mixed[0], attn[1]) + nn(mixed[1], attn[1])
    second = nn(mixed[0], attn[3]) + nn(mixed[1], attn[3])
    heads1 = jnp.where(val_at[0:1, 128:256], first[0:1] + class_exp[0:1] * class_qkv[0:1, 128:256], 0.0)
    heads3 = jnp.where(val_at[1:2, 384:512], second[1:2] + class_exp[1:2] * class_qkv[0:1, 384:512], 0.0)
    heads1 = heads1 / denominator[0:1]
    heads3 = heads3 / denominator[1:2]
    rows1 = s_unit(4)
    rows3 = s_unit(5)

    def wide8(row):
        return jnp.broadcast_to(row, (8, row.shape[1])).astype(BF16)

    attn_part = nt(wide8(heads1), rows1) + nt(wide8(heads3), rows3)

    def slab_sum(kind, k, row):
        row_out[k] = row[0:1]
        copies = to_all(kind, row_out.at[k], row_in.at[k])
        row_in[k, s] = row[0:1]
        landed_all(copies)
        total = row_in[k, 0]
        for index in range(1, NS):
            total = total + row_in[k, index]
        return total

    block_mid = class_pre + slab_sum(6, 0, attn_part) + vecs[9:10, :]
    hat2, inv2 = norm_stats(block_mid, mask, 1e-05)
    mlp_input = hat2 * gains[2] + shifts[2]
    mlp_input = wide8(jnp.where(lane == 40, 1.0, mlp_input))
    hidden_units = [s_unit(6 + i) for i in range(12)]
    preact = nt(mlp_input[:, 0:128], hidden_units[0])
    for i in range(1, 12):
        preact = preact + nt(mlp_input[:, 128 * i : 128 * i + 128], hidden_units[i])
    preact = jnp.where(inner < 20, preact, 0.0)
    cdf = 0.5 * (1.0 + lax.erf(preact * 0.7071067811865476))
    active = preact * cdf
    active = pltpu.roll(active, 20, 1).astype(BF16)
    mlp_part = jnp.concatenate([nn(active, hidden_units[i]) for i in range(12)], axis=1)
    block_out = block_mid + slab_sum(7, 1, mlp_part) + vecs[10:11, :]
    hat3, inv3 = norm_stats(block_out, mask, 1e-05)
    post = wide8(hat3 * gains[3] + shifts[3])
    if weights is not None:
        weights.r_done(2)
    vit = [blocks(24 + 3 * u, 3) for u in range(8)]
    embed = jnp.concatenate([nn(post, vit[u]) for u in range(8)], axis=1)[0:1]
    words = text[...]
    dots = jnp.sum(embed * words, axis=-1, keepdims=True)
    size_e = jnp.sum(embed * embed, axis=-1, keepdims=True) + 1e-06
    size_t = jnp.sum(words * words, axis=-1, keepdims=True) + 1e-06
    sizes = jnp.sqrt(size_e) * jnp.sqrt(size_t)
    score = 100.0 * dots / sizes
    score_out[...] = jnp.broadcast_to(score, (8, 128))
    d_embed = wide8((-1.0 / 64.0) * (100.0 * words / sizes - score * embed / size_e))
    d_post = nt(d_embed[:, 0:128], vit[0])
    for u in range(1, 8):
        d_post = d_post + nt(d_embed[:, 128 * u : 128 * u + 128], vit[u])
    d_second = norm_back(d_post[0:1], hat3, inv3, gains[3])
    d_second_b = wide8(d_second)
    d_active = nt(d_second_b[:, 0:128], hidden_units[0])
    for i in range(1, 12):
        d_active = d_active + nt(d_second_b[:, 128 * i : 128 * i + 128], hidden_units[i])
    d_active = pltpu.roll(d_active, WIDE - 20, 1)
    slope = cdf + preact * jnp.exp(-0.5 * preact * preact) * 0.3989422804014327
    d_pre = jnp.where(inner < 20, d_active * slope, 0.0).astype(BF16)
    input_part = jnp.concatenate([nn(d_pre, hidden_units[i]) for i in range(12)], axis=1)
    d_input = slab_sum(8, 2, input_part)
    d_first = wide8(d_second + norm_back(d_input, hat2, inv2, gains[2]))
    d_heads1 = nn(d_first, rows1).astype(BF16)
    d_heads3 = nn(d_first, rows3).astype(BF16)
    value0 = nt(jnp.where(val_at[0:1, 128:256], d_heads1.astype(F32), 0.0).astype(BF16), attn[1])
    value1 = nt(jnp.where(val_at[1:2, 384:512], d_heads3.astype(F32), 0.0).astype(BF16), attn[3])
    expect0 = jnp.sum(d_heads1[0:1].astype(F32) * heads1, axis=-1, keepdims=True)
    expect1 = jnp.sum(d_heads3[0:1].astype(F32) * heads3, axis=-1, keepdims=True)
    vd_out[0:1, :] = value0[0:1]
    vd_out[1:2, :] = value1[0:1]
    vd_out[2:3, :] = jnp.where(lane < 128, denominator[0:1], denominator[1:2])
    vd_out[3:4, :] = jnp.where(lane < 128, expect0, expect1)
    copies = to_all(9, vd_out, vd_in)
    vd_in[s] = vd_out[...]
    token_logits = nt(unit, dirs[0:16, :], HIGH) / ROOT
    landed_all(copies)
    head_at = iota((1, 16), 1)
    denominators = jnp.zeros((1, 16), F32)
    expects = jnp.zeros((1, 16), F32)
    for index in range(NS):
        dirs[16 + 2 * index : 18 + 2 * index, :] = vd_in[index, 0:2]
        for h in range(2):
            here = head_at == 2 * index + h
            denominators = jnp.where(here, vd_in[index, 2:3, 128 * h : 128 * h + 1], denominators)
            expects = jnp.where(here, vd_in[index, 3:4, 128 * h : 128 * h + 1], expects)
    token_weight = jnp.exp(token_logits) / denominators
    token_dots = nt(unit, dirs[16:32, :], HIGH)
    logit_grads = token_weight * (token_dots - expects)
    d_unit = nn(logit_grads / ROOT, dirs[0:16, :], HIGH) + nn(
        token_weight.astype(BF16).astype(F32), dirs[16:32, :], HIGH
    )
    d_pre_x = norm_back(d_unit, hat1, inv1, gains[1])
    d_embedded = norm_back(d_pre_x, hat0, inv0, gains[0]).astype(BF16)
    d_parts = [nn(d_embedded, blocks(9 + 3 * u, 3)) for u in range(5)]
    d_top = jnp.concatenate([part[0:16] for part in d_parts], axis=0) * img_scale
    d_bottom = jnp.concatenate([part[16:32] for part in d_parts], axis=0) * img_scale
    edge_out[1, 0] = d_bottom
    edge_out[1, 1] = d_top
    copies = to_sides(10, edge_out.at[1], edge_in.at[1])
    landed_all(copies)
    d_raw = halves(
        jnp.concatenate(
            [d_top * corr0, d_bottom * corr1, edge_in[1, 1] * high_f, edge_in[1, 0] * low_f], axis=1
        )
    )
    d_narrow = []
    for m in range(3):
        table = [rmh[512 * m : 512 * m + 512, :], rml[512 * m : 512 * m + 512, :]]
        d_narrow.append(halves(three(nt, table, d_raw)))
    for x in range(8):
        d_pix = jnp.zeros((512, 128), F32)
        for m in range(3):
            table = [
                t[80 * m : 80 * m + 80, 128 * x : 128 * x + 128] for t in (tth, ttl)
            ]
            d_pix = d_pix + three(nn, d_narrow[m], table)
        d_pix = d_pix.astype(BF16)
        for r in range(16):
            cols_buf[32 * x : 32 * x + 32, 128 * r : 128 * r + 128] = d_pix[32 * r : 32 * r + 32]
    acc[...] = jnp.zeros_like(acc)

    def head_back(i, carry):
        at = pl.multiple_of(i * 256, 256)
        grads = nn(head_p[...], cols_buf[:, pl.ds(at, 256)])
        normed = nrm[:, pl.ds(at, 256)]
        gained = normed * gain + gshift
        gate = 1.0 / (1.0 + jnp.exp(-gained))
        grads = grads * (gate * (1.0 + gained * (1.0 - gate))) * gain
        dnrm[:, pl.ds(at, 256)] = grads
        acc[0] += grads[:, 0:128] + grads[:, 128:256]
        both = grads * normed
        acc[1] += both[:, 0:128] + both[:, 128:256]
        return carry

    lax.fori_loop(0, 8, head_back, 0)
    conv0_t = nt(eye, conv0).astype(BF16)
    tail_t = nt(eye[0:16], tail).astype(BF16)
    mean0, mean1 = group_totals(2)

    def conv_back(i, carry):
        at = pl.multiple_of(i * 256, 256)
        grads = (dnrm[:, pl.ds(at, 256)] - mean0 - nrm[:, pl.ds(at, 256)] * mean1) * inverse
        grads = grads.astype(BF16)
        dnrm[0:128, pl.ds(at, 256)] = nn(conv0_t, grads)
        dnrm[128:144, pl.ds(at, 256)] = nn(tail_t, grads)
        return carry

    lax.fori_loop(0, 8, conv_back, 0)
    total = jnp.zeros((16, 2304), F32)
    column = lax.rem(iota((16, 2304), 1), 128)
    for b in range(3):
        part = jnp.zeros((16, 2304), F32)
        for a in range(3):
            t = 3 * a + b
            pieces = [dnrm[16 * t : 16 * t + 16, :]]
            if a:
                pieces = [jnp.zeros((16, 128 * a), F32)] + pieces
            if a < 2:
                pieces = pieces + [jnp.zeros((16, 256 - 128 * a), F32)]
            part = part + jnp.concatenate(pieces, axis=1)
        if b == 0:
            part = jnp.where(column < 127, pltpu.roll(part, 2303, 1), 0.0)
        if b == 2:
            part = jnp.where(column > 0, pltpu.roll(part, 1, 1), 0.0)
        total = total + part
    rim_out[0] = total[:, 2176:2304]
    rim_out[1] = total[:, 0:128]
    copies = to_sides(11, rim_out, rim_in)
    landed_all(copies)
    rows = [total[:, 128 * r + 128 : 128 * r + 256] for r in range(16)]
    rows[0] = rows[0] + rim_in[0] * low_f
    rows[15] = rows[15] + rim_in[1] * high_f
    rows = [-sigma * (row / LAT_SCALE) for row in rows]
    stacked = jnp.concatenate(
        [
            jnp.concatenate([rows[4 * k + p], rows[4 * k + 2 + p]], axis=1)
            for k in range(4)
            for p in range(2)
        ],
        axis=0,
    ).astype(BF16)
    centre = jnp.concatenate([inter[:, 128:256], inter[:, 512:640]], axis=1)
    tok = nt(stacked, centre)
    tok_t = jnp.concatenate(
        [
            jnp.concatenate(
                [tok[32 * k : 32 * k + 32, 128 * q : 128 * q + 128] for k in range(4)], axis=1
            )
            for q in range(2)
        ],
        axis=0,
    ).astype(BF16)
    d_vel = nn(perm[...], tok_t).astype(BF16)
    for quarter in range(4):
        part = nn(d_vel, mod[:, 768 * quarter : 768 * quarter + 768])
        for w in range(2 * NS):
            gsplit[w, 4 * quarter : 4 * quarter + 4] = part[4 * w : 4 * w + 4]
    for copy in live:
        copy.wait_send()
    if weights is not None:
        for slot in range(3):
            weights.r_finish(slot)
        mine[...] = gsplit[...].astype(BF16)
        reduce_gradient(mine, landed, terms, arrived, collected, sems[11:])
        whole = jnp.concatenate([collected[w] for w in range(2 * NS)], axis=0)
        grad_out[...] = jnp.transpose(whole)[0:96, :]
    else:
        grad_out[...] = gsplit[...]


def resize_table(out_count, in_count):
    stretch = in_count / out_count
    centers = (np.arange(out_count) + 0.5) * stretch
    places = np.arange(in_count) + 0.5
    weights = np.maximum(0.0, 1.0 - np.abs(places[None, :] - centers[:, None]) / stretch)
    return weights / weights.sum(axis=1, keepdims=True)


def split_const(values):
    high = values.astype(np.float32).astype(jnp.bfloat16)
    rest = (values - high.astype(np.float64)).astype(jnp.bfloat16)
    return jnp.asarray(high), jnp.asarray(rest)


def constants():
    perm = np.zeros((64, 64))
    for c in range(16):
        for p in range(2):
            for q in range(2):
                perm[4 * c + 2 * p + q, q * 32 + p * 16 + c] = 1
    inter = np.zeros((2, 2, 64, 2, 3, 128))
    for q in range(2):
        for i2 in range(2):
            for j in range(64):
                for b in range(3):
                    at = 2 * j + q - b + 1
                    if 0 <= at < 128:
                        inter[q, i2, j, i2, b, at] = 1
    table = resize_table(224, 1024)
    columns = np.zeros((3, 5, 16, 8, 128))
    for m in range(3):
        for u in range(5):
            if 3 * u + m < 14:
                for pc in range(16):
                    columns[m, u, pc] = table[14 * pc + 3 * u + m].reshape(128, 8).T
    rows = np.zeros((3, 16, 4, 8, 4, 128))
    local = table[28 * 3 : 28 * 3 + 28, 128 * 3 : 128 * 3 + 128].reshape(28, 16, 8)
    to_next = table[28 * 4, 128 * 3 : 128 * 3 + 128].reshape(16, 8)
    to_prev = table[28 * 3 - 1, 128 * 3 : 128 * 3 + 128].reshape(16, 8)
    for m in range(3):
        for c in range(3):
            for a in range(14):
                at = 42 * m + 14 * c + a
                rows[m, :, c, :, 0, at] = local[a]
                rows[m, :, c, :, 1, at] = local[14 + a]
            rows[m, :, c, :, 2, 42 * m + 14 * c] = to_next
            rows[m, :, c, :, 3, 42 * m + 14 * c + 13] = to_prev
    lanes = np.zeros((8, 128))
    lanes[0:2] = 1
    for m in range(3):
        for c in range(3):
            for a in range(14):
                at = 42 * m + 14 * c + a
                lanes[2, at] = 0.5 / PIX_STD[c]
                lanes[3, at] = (0.5 - PIX_MEAN[c]) / PIX_STD[c]
            lanes[0, 42 * m + 14 * c] = table[0, 0] / table[28, 128]
            lanes[1, 42 * m + 14 * c + 13] = table[223, 1023] / table[27, 127]
    ph = np.zeros((2, 128, 8, 32))
    for c in range(3):
        for y in range(8):
            for x in range(8):
                k = 64 * c + 8 * y + x
                if k < 128:
                    ph[0, k, x, 8 * c + y] = 1
                else:
                    ph[1, 16 + k - 128, x, 8 * c + y] = 1
    tth, ttl = split_const(columns.reshape(240, 1024))
    rmh, rml = split_const(rows.reshape(1536, 512))
    one = lambda v: jnp.asarray(v.astype(jnp.bfloat16))
    ph = ph.reshape(2, 128, 256)
    return (
        one(perm), one(perm.T), one(inter.reshape(256, 768)), tth, ttl, rmh, rml,
        one(ph[0]), one(ph[1]), jnp.asarray(lanes.astype(np.float32)),
    )


def widen(values):
    shape = values.shape[:-1]
    view = values.reshape(shape + (32, 40))
    return jnp.pad(view, [(0, 0)] * len(shape) + [(0, 0), (0, 8)]).reshape(shape + (WIDE,))


def pack_weights(proj, conv, head, patch, attn_in, attn_out, mlp_in, mlp_bias, mlp_out, vit):
    attn = jnp.pad(attn_in, ((0, 8), (0, 32))).reshape(48, 4, 128).transpose(1, 0, 2)
    back = attn_out.T
    out0 = jnp.pad(back[:, :80], ((0, 8), (32, 16)))
    out1 = jnp.pad(back[:, 80:], ((0, 8), (16, 32)))
    mlp = widen(jnp.concatenate([mlp_in.T, mlp_out]))
    bias = jnp.pad(mlp_bias[:, None], ((0, 20), (40, WIDE - 41)))
    mlp = jnp.pad(mlp + bias, ((0, 8), (0, 0))).reshape(48, 12, 128).transpose(1, 0, 2)
    s_pack = jnp.concatenate([attn, out0[None], out1[None], mlp]).reshape(2, 9, 48, 128)
    first = jnp.pad(proj, ((0, 0), (0, 64))).reshape(6, 16, 128)
    conv_t = conv.reshape(144, 16).T
    second = jnp.stack(
        [
            conv_t[:, :128],
            head[:, :128],
            jnp.pad(jnp.concatenate([conv_t[:, 128:], head[:, 128:]], axis=1), ((0, 0), (0, 48))),
        ]
    )
    third = jnp.pad(patch.reshape(3, 14, 14, 40).transpose(2, 0, 1, 3), ((0, 1), (0, 0), (0, 0), (0, 0)))
    third = jnp.pad(third.reshape(5, 126, 40), ((0, 0), (0, 2), (0, 8)))
    third = third.transpose(0, 2, 1).reshape(15, 16, 128)
    fourth = jnp.pad(vit, ((0, 8), (0, 0))).reshape(48, 8, 128).transpose(1, 0, 2).reshape(24, 16, 128)
    r_pack = jnp.concatenate([first, second, third, fourth]).reshape(3, 16, 16, 128)
    return s_pack, r_pack


def run_step(packs, fetch, grad_shape, small, consts):
    vm, dma = pltpu.VMEM, pltpu.SemaphoreType.DMA
    scratch = [
        vm((512, 3072), BF16), vm((512, 3072), BF16),
        vm((2, NZ, 2, 9, 48, 128), BF16), vm((3, 16, NF, 16, 128), BF16),
        vm((3072, 128), BF16), vm((48, 2304), BF16), vm((2, 48, 128), BF16), vm((2, 48, 128), BF16),
        vm((512, LANES), F32), vm((512, LANES), F32), vm((2, 512, 128), F32),
        vm((2, 8, 512), F32), vm((2, NS, 8, 512), F32),
        vm((256, LANES), BF16), vm((512, 1024), BF16), vm((256, 512), BF16), vm((512, 256), BF16),
        vm((2, 2, 80, 128), F32), vm((2, 2, 80, 128), F32),
        vm((2, WIDE), F32), vm((NS, 2, WIDE), F32), vm((32, WIDE), F32),
        vm((NS, 4, WIDE), F32), vm((NS, 4, WIDE), F32),
        vm((3, 1, WIDE), F32), vm((3, NS, 1, WIDE), F32),
        vm((4, WIDE), F32), vm((NS, 4, WIDE), F32),
        vm((2, 16, 128), F32), vm((2, 16, 128), F32),
        vm((16, 16, 768), F32), vm((16, 16, 768), BF16), vm((16, 16, 768), BF16),
        vm((NF, 4, 128), F32), vm((NF, 4, 128), F32), vm((16, 4, 128), F32),
        dma((12, NS - 1)), dma((12, NS - 1)), dma((1,)),
        dma((3,)), dma((3,)), dma((3, NS - 1)), dma((3, NS - 1)), dma((3,)), dma((3,)),
        dma((4,)), dma((2,)), dma((16,)), dma((16,)), dma((2,)),
        dma((15,)), dma((15,)), dma((31,)), dma((31,)), dma((15,)), dma((15,)),
    ]
    hidden, mods, noisy, sigma, proj_bias, vecs, text, chan, head_bias = small
    return pl.pallas_call(
        functools.partial(step_kernel, fetch),
        out_shape=[jax.ShapeDtypeStruct(grad_shape, F32), jax.ShapeDtypeStruct((8, 128), F32)],
        in_specs=[ANY] + ([ANY] * 2 if fetch else [VMEM] * 2) + [VMEM] * 2 + [SMEM] + [VMEM] * 15,
        out_specs=[VMEM, VMEM],
        scratch_shapes=scratch,
        compiler_params=pltpu.CompilerParams(
            collective_id=0, has_side_effects=True, vmem_limit_bytes=60 * 1024 * 1024
        ),
        name="step",
    )(hidden, *packs, mods, noisy, sigma, proj_bias, vecs, text, chan, head_bias, *consts)


def flow_sigma(step_index):
    remain = 1.0 - step_index.astype(F32) / STEPS
    return 3.0 * remain / (1.0 + 2.0 * remain)


def prepare(
    hidden, modulation, noisy, step_index, proj_bias, conv_bias, norm_gain, norm_shift, head_bias,
    position, class_token, vit_gain, vit_shift, attn_out_bias, mlp_out_bias, text_embed,
):
    stack = jnp.concatenate(
        [
            class_token[None], vit_gain, vit_shift, attn_out_bias[None], mlp_out_bias[None],
            jnp.zeros((5, WIDTH), F32), position.astype(F32),
        ]
    )
    chan = jnp.concatenate(
        [conv_bias[None], norm_gain[None], norm_shift[None], jnp.zeros((5, 512), F32)]
    )
    return (
        hidden.reshape(512, 3072), modulation[0], noisy.reshape(512, 64),
        flow_sigma(step_index).reshape(1, 1), proj_bias[None], widen(stack), text_embed, chan,
        jnp.broadcast_to(
            jnp.pad(
                jnp.concatenate([head_bias[:128], jnp.zeros((16,), F32), head_bias[128:]]), (0, 48)
            ),
            (8, 256),
        ),
    )


def local(
    hidden, modulation, noisy, step_index, proj_weight, proj_bias, conv_weight, conv_bias,
    norm_gain, norm_shift, head_weight, head_bias, patch_weight, position, class_token,
    vit_gain, vit_shift, attn_in, attn_out, attn_out_bias, mlp_in, mlp_in_bias, mlp_out,
    mlp_out_bias, vit_proj, text_embed,
):
    packs = pack_weights(
        proj_weight, conv_weight, head_weight, patch_weight, attn_in, attn_out, mlp_in,
        mlp_in_bias, mlp_out, vit_proj,
    )
    small = prepare(
        hidden, modulation, noisy, step_index, proj_bias, conv_bias, norm_gain, norm_shift,
        head_bias, position, class_token, vit_gain, vit_shift, attn_out_bias, mlp_out_bias,
        text_embed,
    )
    grad, score = run_step(packs, True, (96, 64), small, constants())
    return grad, score[0, 0:1]


def solution(mesh):
    placed = (
        P(("fsdp", "grp"), "slab", None, None),
        P(("fsdp", "grp"), None, None),
        P(("fsdp", "grp"), "slab", None, None),
        P(("fsdp", "grp")),
        P("fsdp", None),
        P(),
        P(None, None, None, "fsdp"),
        P(),
        P(),
        P(),
        P("fsdp", None),
        P(),
        P(None, "fsdp"),
        P("slab", None),
        P(),
        P(),
        P(),
        P("fsdp", "slab"),
        P("slab", "fsdp"),
        P(),
        P(None, ("fsdp", "slab")),
        P(("fsdp", "slab")),
        P(("fsdp", "slab"), None),
        P(),
        P("fsdp", None),
        P(("fsdp", "grp"), None),
    )
    return jax.shard_map(
        local,
        mesh=mesh,
        in_specs=placed,
        out_specs=(P("fsdp", None), P(("fsdp", "grp"))),
        check_vma=False,
    )
```

time: 1650 us -> 197 us (0.12)
  waiting for transfers between devices: 960 us -> 0 us
  blocking collectives: 499 us -> 0 us
  Pallas kernels: 0 us -> 184 us
  local copies, waits for them, and re-layouts: 78.1 us -> 7.94 us
  matrix products: 45 us -> 0 us
  between operations: 28.8 us -> 1.85 us
  other arithmetic: 24.1 us -> 3.14 us
    unnamed x8 -> x0, waiting for transfers between devices: 664 us -> none
    all_gather x5 -> x0, blocking collectives: 295 us -> none  [the longest x1 72.7 us: local(): lax.all_gather(proj_weight, 'fsdp', axis=0, tiled=True)]
    all_gather x5 -> x0, waiting for transfers between devices: 245 us -> none  [the longest x1 130 us: local(): proj_rows_full = lax.all_gather(vit_proj, 'fsdp', axis=0, tiled=True)]
    pallas_call x0 -> x1, Pallas kernels: none -> 184 us  [run_step(): pl.pallas_call(functools.partial(step_kernel, fetch), out_shape=[jax.Shap...]
    psum x6 -> x0, blocking collectives: 145 us -> none  [the longest x1 68.1 us: local(): proj_grad = lax.psum(row_share, ('grp', 'slab'))]
    unnamed x1 -> x0, blocking collectives: 59.4 us -> none
    convert_element_type x13 -> x0, local copies, waits for them, and re-layouts: 57.4 us -> none  [the longest x2 27.2 us: local(): pixels = cells_to_pixels(cell_vals).astype(jnp.bfloat16)]
    reduce_scatter x1 -> x0, waiting for transfers between devices: 45 us -> none  [local(): lax.psum_scatter(spread.astype(jnp.bfloat16), 'slab', scatter_dimension=1...]
  transfers between devices with their start and end apart: 15 -> 0, of which waited for: 6 -> 0; matrix products, arithmetic and copies ran while one was open for 5% -> 0% of each run, Pallas kernels for 0% -> 0%
where the time goes in v1:
time: 197 us
  Pallas kernels  184 us (93%)
  local copies, waits for them, and re-layouts  7.94 us (4%)
  other arithmetic  3.14 us (2%)
    pallas_call x1, Pallas kernels, run_step(): pl.pallas_call(functools.partial(step_kernel, fetch), out_shape=[jax.Shap...  184 us

profile of v1, /device:TPU:1, one launch (start us, length us, event | category | flops | bytes accessed | tf_op | source)
XLA Modules:
  0.0 196.6 jit_solution(1489462208938361155)
XLA Ops:
  0.6 0.9 fusion.4
  1.5 0.1 pad_bitcast_fusion.3
  1.6 0.9 pad_maximum_fusion.1
  2.5 0.2 copy.64
  2.9 0.7 bitcast_add_fusion
  3.6 0.1 pad.57
  3.7 0.2 copy.56
  3.9 0.7 pad_maximum_fusion
  4.6 0.1 copy.57
  4.9 0.1 constant_dynamic-update-slice_fusion.2
  5.0 0.2 copy.59
  5.5 0.1 copy.61
  6.4 0.1 concatenate.40
  6.5 0.1 concatenate.41
  6.7 0.1 concatenate.42
  6.8 0.1 concatenate.43
  6.9 0.1 concatenate.44
  7.0 0.4 reshape.84
  7.6 1.2 reshape.83.vecs
  8.9 0.7 maximum_maximum_fusion.chan
  9.6 0.6 broadcast_in_dim.42.head_bias
  10.2 183.7 %step.1 = (f32[96,64]{1,0:T(8,128)}, f32[8,128]{1,0:T(8,128)}) custom-call(bf16[512,3072]{1,0:T(8,128)(2,1)} %bitcast.53, bf16[2,9,48,128]{3,2,1,0:T(8,128)(2,1)} %bitcast.56, bf16[3,16,16,128]{3,2,1,0:T(8,128)(2,1)} %bitcast.61, bf16[2,3072]{1,0:T(2,128)(2,1)} %bitcast.70, bf16[512,64]{1,0:T(8,128)(2,1)} %bitcast.63, f32[1,1]{1,0:T(1,128)} %bitcast.26.sigma_ref, ...), custom_call_target="tpu_custom_call" | custom-call | tf_op jit(solution)/shard_map/step/pallas_call | solution.py:899
  193.9 1.5 copy.63
  195.4 1.2 slice.35
  (69 shorter events, 0.9 us)
Async XLA Ops:
  2.5 1.4 copy-start.4
  2.7 1.9 copy-start.5
  2.7 1.9 copy-start.9
  2.8 2.0 %copy-start.8 = (bf16[16,192]{1,0:T(8,128)(2,1)S(1)}, bf16[16,192]{1,0:T(8,128)(2,1)}, u32[]{:S(2)}) copy-start(bf16[16,192]{1,0:T(8,128)(2,1)} %param.46) | copy-start | bytes 18436
  2.8 2.0 %slice-start = ((bf16[16,192]{1,0:T(8,128)(2,1)}), bf16[16,64]{1,0:T(8,128)(2,1)S(1)}, s32[]{:S(2)}) async-start(bf16[16,192]{1,0:T(8,128)(2,1)} %param.46), calls=%async_computation | async-start | bytes 8192 | tf_op jit(solution)/shard_map/slice | solution.py:865
  2.8 2.1 %copy-start.3 = (bf16[588,40]{0,1:T(8,128)(2,1)S(1)}, bf16[588,40]{0,1:T(8,128)(2,1)}, u32[]{:S(2)}) copy-start(bf16[588,40]{0,1:T(8,128)(2,1)} %param.48) | copy-start | bytes 141124
  3.8 1.8 copy-start.2
  4.8 1.6 copy-start.10
  4.8 1.7 copy-start.6
  5.1 1.5 copy-start.7
  5.2 1.6 copy-start.11
  5.2 1.7 copy-start.12
  5.2 1.8 copy-start.1
  5.7 1.9 copy-start
  7.5 1.4 copy-start.13
  7.5 1.4 copy-start.14
  7.5 1.4 copy-start.15
  7.5 2.0 %copy-start.16 = (f32[192]{0:T(256)S(1)}, f32[192]{0:T(256)}, u32[]{:S(2)}) copy-start(f32[192]{0:T(256)} %param.47) | copy-start | bytes 2308
  7.5 2.0 %slice-start.1 = ((f32[192]{0:T(256)}), f32[128]{0:T(128)S(1)}, s32[]{:S(2)}) async-start(f32[192]{0:T(256)} %param.47), calls=%async_computation.1 | async-start | bytes 1024 | tf_op jit(solution)/shard_map/slice | solution.py:935

commit v2 on v1

--- a/solution.py
+++ b/solution.py
@@ -46,8 +46,10 @@
     return high, (values - high.astype(F32)).astype(BF16)
 
 
-def three(product, a, b):
-    return product(a[0], b[0]) + (product(a[1], b[0]) + product(a[0], b[1]))
+def thirds(values):
+    high, rest = halves(values)
+    middle = (values - high.astype(F32) - rest.astype(F32)).astype(BF16)
+    return [high, rest, middle]
 
 
 def remote(source, dest, send, recv, target):
@@ -77,8 +79,9 @@
 
 
 class Weights:
-    def __init__(self, s_in, r_in, s_buf, r_buf, sems):
-        self.s_in, self.r_in, self.s_buf, self.r_buf = s_in, r_in, s_buf, r_buf
+    def __init__(self, a_in, b_in, r_in, a_buf, b_buf, r_buf, sems):
+        self.ins, self.r_in = (a_in, b_in), r_in
+        self.a_buf, self.b_buf, self.r_buf = a_buf, b_buf, r_buf
         (self.z_send, self.z_recv, self.sh_send, self.sh_recv, self.fw_send, self.fw_recv,
          self.loc, self.pair_sem, self.ring_send, self.ring_recv, self.core_sem) = sems
         self.f = lax.axis_index("fsdp")
@@ -87,19 +90,19 @@
         self.w = self.g * NS + self.s
         self.z, self.half = self.f // 2, lax.rem(self.f, 2)
         self.core = {"grp": 1 - self.g}
-        self.sent = []
+
+    def r_own(self, slot):
+        return pltpu.make_async_copy(
+            self.r_in.at[slot, self.w], self.r_buf.at[slot, self.w, self.f], self.loc.at[slot]
+        )
 
     def r_start(self, slot):
-        source = self.r_in.at[slot, self.w]
-        mine = pltpu.make_async_copy(
-            source, self.r_buf.at[slot, self.w, self.f], self.loc.at[slot]
-        )
-        mine.start()
+        self.r_own(slot).start()
 
         def send(d, carry):
             target = {"fsdp": lax.rem(self.f + d, NF)}
             remote(
-                source, self.r_buf.at[slot, self.w, self.f],
+                self.r_in.at[slot, self.w], self.r_buf.at[slot, self.w, self.f],
                 self.z_send.at[slot], self.z_recv.at[slot], target,
             ).start()
             return carry
@@ -108,11 +111,10 @@
 
     def r_share(self, slot):
         block = self.r_buf.at[slot, self.w]
-        many = self.r_buf.at[slot, self.w, pl.ds(0, NF - 1)]
-        remote(many, many, self.z_send.at[slot], self.z_recv.at[slot], self.core).wait_recv()
-        pltpu.make_async_copy(
-            self.r_in.at[slot, self.w], self.r_buf.at[slot, self.w, self.f], self.loc.at[slot]
-        ).wait()
+        if slot < 2:
+            many = self.r_buf.at[slot, self.w, pl.ds(0, NF - 1)]
+            remote(many, many, self.z_send.at[slot], self.z_recv.at[slot], self.core).wait_recv()
+            self.r_own(slot).wait()
         for d in range(1, NS):
             remote(
                 block, block, self.sh_send.at[slot, d - 1], self.sh_recv.at[slot, d - 1],
@@ -132,63 +134,100 @@
         many = self.r_buf.at[slot, pl.ds((1 - self.g) * NS, NS)]
         remote(many, many, self.fw_send.at[slot], self.fw_recv.at[slot], self.core).wait_recv()
 
-    def s_pair(self):
-        dest = self.s_buf.at[self.g, self.z, self.half]
-        return remote(
-            self.s_in.at[self.g], dest, self.pair_sem.at[0], self.pair_sem.at[1],
-            {"fsdp": self.z * 2 + 1 - self.half},
-        ), pltpu.make_async_copy(self.s_in.at[self.g], dest, self.loc.at[3])
-
-    def s_start(self):
-        for copy in self.s_pair():
+    def view(self, kind, z):
+        z = lax.rem(z, NZ)
+        if kind == 0:
+            return self.a_buf.at[self.g, z]
+        if kind == 1:
+            return self.r_buf.at[2, self.w, pl.ds(2 * z, 2)]
+        return self.b_buf.at[self.g, z]
+
+    def own(self):
+        return [
+            pltpu.make_async_copy(
+                self.ins[0].at[self.g], self.a_buf.at[self.g, self.z, self.half], self.loc.at[3]
+            ),
+            self.r_own(2),
+            pltpu.make_async_copy(self.ins[1].at[self.g], self.b_buf.at[self.g, self.z], self.loc.at[4]),
+        ]
+
+    def pair(self):
+        other = {"fsdp": self.z * 2 + 1 - self.half}
+        return [
+            remote(
+                self.ins[0].at[self.g], self.a_buf.at[self.g, self.z, self.half],
+                self.pair_sem.at[0, 0], self.pair_sem.at[0, 1], other,
+            ),
+            remote(
+                self.r_in.at[2, self.w], self.r_buf.at[2, self.w, self.f],
+                self.pair_sem.at[1, 0], self.pair_sem.at[1, 1], other,
+            ),
+        ]
+
+    def start(self):
+        for copy in self.pair() + self.own():
             copy.start()
 
-    def s_step(self, step, way):
+    def step(self, kind, step, way):
         sign = NZ - 1 if way == 0 else 1
-        block = self.s_buf.at[self.g, lax.rem(self.z + sign * step, NZ)]
+        block = self.view(kind, self.z + sign * step)
         hop = 1 if way == 0 else NZ - 1
         target = {"fsdp": lax.rem(self.z + hop, NZ) * 2 + self.half}
         slot = way * 8 + step
-        return remote(block, block, self.ring_send.at[slot], self.ring_recv.at[slot], target)
-
-    def s_share(self, block):
-        block = self.s_buf.at[self.g, lax.rem(block, NZ)]
-        remote(block, block, self.core_sem.at[0], self.core_sem.at[1], self.core).start()
-
-    def s_pump(self, step):
+        return remote(
+            block, block, self.ring_send.at[kind, slot], self.ring_recv.at[kind, slot], target
+        )
+
+    def share(self, kind, z):
+        if kind == 1:
+            return
+        block, k = self.view(kind, z), kind // 2
+        remote(block, block, self.core_sem.at[k, 0], self.core_sem.at[k, 1], self.core).start()
+
+    def pump(self, kinds, step):
         steps = (NZ // 2, NZ // 2 - 1)
-        if step == 0:
-            pair, own = self.s_pair()
-            own.wait()
-            pair.wait_recv()
-            self.s_share(self.z)
-        for way in (0, 1):
-            if 0 < step <= steps[way]:
-                self.s_step(step - 1, way).wait_recv()
-            if step < steps[way]:
-                self.s_step(step, way).start()
-            if 0 < step <= steps[way]:
-                self.s_share(self.z + (NZ - step if way == 0 else step))
-
-    def s_done(self):
-        theirs, mine = self.s_buf.at[1 - self.g], self.s_buf.at[self.g]
-        remote(theirs, theirs, self.core_sem.at[0], self.core_sem.at[1], self.core).wait_recv()
-        remote(mine, mine, self.core_sem.at[0], self.core_sem.at[1], self.core).wait_send()
-        self.s_pair()[0].wait_send()
-        for way, steps in ((0, NZ // 2), (1, NZ // 2 - 1)):
-            for step in range(steps):
-                self.s_step(step, way).wait_send()
-
-    def r_finish(self, slot):
-        many = self.r_buf.at[slot, self.w, pl.ds(0, NF - 1)]
-        remote(many, many, self.z_send.at[slot], self.z_recv.at[slot], self.core).wait_send()
-        block = self.r_buf.at[slot, self.w]
-        for d in range(1, NS):
-            remote(
-                block, block, self.sh_send.at[slot, d - 1], self.sh_recv.at[slot, d - 1], self.core
-            ).wait_send()
-        many = self.r_buf.at[slot, pl.ds(self.g * NS, NS)]
-        remote(many, many, self.fw_send.at[slot], self.fw_recv.at[slot], self.core).wait_send()
+        for kind in kinds:
+            if step == 0:
+                self.own()[kind].wait()
+                if kind < 2:
+                    self.pair()[kind].wait_recv()
+            for way in (0, 1):
+                if 0 < step <= steps[way]:
+                    self.step(kind, step - 1, way).wait_recv()
+                if step < steps[way]:
+                    self.step(kind, step, way).start()
+            if step == 0:
+                self.share(kind, self.z)
+            for way in (0, 1):
+                if 0 < step <= steps[way]:
+                    self.share(kind, self.z + (NZ - step if way == 0 else step))
+
+    def landed(self, kind):
+        buffer, k = (self.a_buf, self.b_buf)[kind // 2], kind // 2
+        theirs = buffer.at[1 - self.g]
+        remote(theirs, theirs, self.core_sem.at[k, 0], self.core_sem.at[k, 1], self.core).wait_recv()
+
+    def finish(self):
+        for k, buffer in enumerate((self.a_buf, self.b_buf)):
+            mine = buffer.at[self.g]
+            remote(mine, mine, self.core_sem.at[k, 0], self.core_sem.at[k, 1], self.core).wait_send()
+        for copy in self.pair():
+            copy.wait_send()
+        for kind in range(3):
+            for way, steps in ((0, NZ // 2), (1, NZ // 2 - 1)):
+                for step in range(steps):
+                    self.step(kind, step, way).wait_send()
+        for slot in range(3):
+            if slot < 2:
+                many = self.r_buf.at[slot, self.w, pl.ds(0, NF - 1)]
+                remote(many, many, self.z_send.at[slot], self.z_recv.at[slot], self.core).wait_send()
+            block = self.r_buf.at[slot, self.w]
+            for d in range(1, NS):
+                remote(
+                    block, block, self.sh_send.at[slot, d - 1], self.sh_recv.at[slot, d - 1], self.core
+                ).wait_send()
+            many = self.r_buf.at[slot, pl.ds(self.g * NS, NS)]
+            remote(many, many, self.fw_send.at[slot], self.fw_recv.at[slot], self.core).wait_send()
 
 
 def greet(targets):
@@ -207,11 +246,23 @@
     return found
 
 
+def pair_targets(f, s):
+    z, half = f // 2, lax.rem(f, 2)
+    found = []
+    for h in range(2):
+        there = z * 2 + lax.rem(half + h, 2)
+        for d in range(NS):
+            if h or d:
+                found.append((h * NS + d - 1, {"fsdp": there, "slab": lax.rem(s + d, NS)}))
+    return found
+
+
 def greet_all():
     f, g, s = lax.axis_index("fsdp"), lax.axis_index("grp"), lax.axis_index("slab")
     greet(
         [target for _, target in block_targets(g, s)]
         + [{"fsdp": lax.rem(f + d, NF)} for d in range(1, NF)]
+        + [target for _, target in pair_targets(f, s)[NS:]]
     )
 
 
@@ -255,15 +306,17 @@
 
 
 def step_kernel(
-    fetch, hidden, s_in, r_in, mods, noisy, sigma_ref, proj_bias, vecs, text, chan, head_bias,
-    perm, perm_t, inter, tth, ttl, rmh, rml, ph0, ph1, lane_rows,
+    fetch, hidden, a_in, b_in, r_in, mods, noisy, sigma_ref, proj_bias, vecs, text, chan, head_bias,
+    perm, perm_t, inter, columns_w, rows_w, ph0, ph1, lane_rows,
     grad_out, score_out,
-    hid, mod, s_buf, r_buf, proj_full, ext, halo_out, halo_in, nrm, dnrm, acc, stat_out, stat_in,
+    hid, mod, a_buf, b_buf, r_buf, proj_full, ext, halo_out, halo_in, nrm, dnrm, acc, stat_out, stat_in,
     cols_buf, pix, head_t, head_p, edge_out, edge_in, kd_out, kd_in, dirs, u_out, u_in,
-    row_out, row_in, vd_out, vd_in, rim_out, rim_in, gsplit, mine, landed, terms, arrived, collected,
+    row_out, row_in, text_in, vd_out, vd_in, rim_out, rim_in, gsplit, mine, landed, terms, arrived, collected,
     x_send, x_recv, hid_sem, *sems,
 ):
     s = lax.axis_index("slab")
+    f = lax.axis_index("fsdp")
+    half = lax.rem(f, 2)
     low, high = s > 0, s < NS - 1
     low_f, high_f = jnp.where(low, 1.0, 0.0), jnp.where(high, 1.0, 0.0)
     before, after = {"slab": lax.rem(s + NS - 1, NS)}, {"slab": lax.rem(s + 1, NS)}
@@ -303,20 +356,28 @@
 
     if fetch:
         greet_all()
-        weights = Weights(s_in, r_in, s_buf, r_buf, sems[:11])
+        weights = Weights(a_in, b_in, r_in, a_buf, b_buf, r_buf, sems[:11])
         weights.r_start(0)
-        weights.s_start()
+        weights.start()
         weights.r_start(1)
-        weights.r_start(2)
     else:
-        greet([{"slab": lax.rem(s + d, NS)} for d in range(1, NS)])
-        s_buf[...] = s_in[...]
+        greet([target for _, target in pair_targets(f, s)])
+        a_buf[...] = a_in[...]
+        b_buf[...] = b_in[0]
         r_buf[...] = r_in[...]
         weights = None
-
-    def pump(step):
+    words_copy = remote(
+        text, text_in.at[half], x_send.at[12, 0], x_recv.at[12, 0], {"fsdp": f + 1 - 2 * half}
+    )
+    words_copy.start()
+    live.append(words_copy)
+    text_in[half] = text[...]
+
+    def pump(*steps):
         if weights is not None:
-            weights.s_pump(step)
+            for kinds, step in zip(((0, 1), (2,)), steps):
+                if step is not None:
+                    weights.pump(kinds, step)
 
     hid_copy.wait()
     scale = 1.0 + mods[1:2].astype(F32)
@@ -324,7 +385,7 @@
 
     def modulate(lo, hi):
         def body(i, carry):
-            rows = pl.ds(pl.multiple_of(i * 16, 16), 16)
+            rows = pl.ds(pl.multiple_of(i * 32, 32), 32)
             values = hid[rows, :].astype(F32)
             average = jnp.mean(values, axis=-1, keepdims=True)
             centered = values - average
@@ -335,25 +396,27 @@
 
         lax.fori_loop(lo, hi, body, 0)
 
-    modulate(0, 16)
-    pump(0)
-    modulate(16, 32)
+    modulate(0, 6)
+    pump(0, 0)
+    modulate(6, 16)
+    pump(1)
     if weights is not None:
         weights.r_share(0)
-        weights.s_pump(1)
+        pump(2, 1)
         weights.r_core(0)
+        pump(3)
         weights.r_done(0)
 
     def blocks(first, count):
         parts = [r_buf[n // 16, n % 16] for n in range(first, first + count)]
         return jnp.concatenate(parts, axis=1).reshape(NF * 16 * count, 128)
 
-    def s_unit(index):
-        return s_buf[index // 9, :, :, index % 9].reshape(WIDE, 128)
-
-    for f in range(NF):
+    def a_unit(index):
+        return a_buf[index // 3, :, :, index % 3].reshape(WIDE, 128)
+
+    for k in range(NF):
         for n in range(6):
-            proj_full[96 * f + 16 * n : 96 * f + 16 * n + 16, :] = r_buf[0, n, f]
+            proj_full[96 * k + 16 * n : 96 * k + 16 * n + 16, :] = r_buf[0, n, k]
     velocity = nn(mod[...], proj_full[...])[:, :64] + proj_bias[...]
     clean = noisy[...].astype(F32) - sigma * velocity
     lat_tok = (clean / LAT_SCALE + LAT_SHIFT).astype(BF16)
@@ -380,9 +443,13 @@
     halo_out[0] = ext[:, 2048:2176]
     halo_out[1] = ext[:, 128:256]
     copies = to_sides(0, halo_out, halo_in)
-    identity = (iota((512, 512), 0) == iota((512, 512), 1)).astype(F32)
-    same = (iota((512, 512), 0) // 16 == iota((512, 512), 1) // 16).astype(F32)
-    chan_cols = nt(identity, chan[...], HIGH)
+    same = (iota((512, 512), 0) // 16 == iota((512, 512), 1) // 16).astype(BF16)
+
+    def columns_of(rows):
+        width = rows.shape[1]
+        return jnp.transpose(jnp.concatenate([rows, jnp.zeros((120, width), F32)], axis=0))
+
+    chan_cols = columns_of(chan[...])
     conv_bias, gain, gshift = chan_cols[:, 0:1], chan_cols[:, 1:2], chan_cols[:, 2:3]
     eye = (iota((128, 128), 0) == iota((128, 128), 1)).astype(BF16)
     conv0 = r_buf[0, 6].reshape(512, 128)
@@ -393,21 +460,11 @@
         lax.dot_general(ph0[...], head0, (((0,), (1,)), ((), ())), preferred_element_type=F32)
         + lax.dot_general(ph1[...], tail, (((0,), (1,)), ((), ())), preferred_element_type=F32)
     ).astype(BF16)
-    bias_cols = nt(
-        lax.dot_general(
-            ph0[...].astype(F32), eye.astype(F32), (((0,), (0,)), ((), ())),
-            preferred_element_type=F32,
-        ),
-        head_bias[:, 0:128], HIGH,
-    ) + nt(
-        lax.dot_general(
-            ph1[...].astype(F32), eye.astype(F32), (((0,), (0,)), ((), ())),
-            preferred_element_type=F32,
-        ),
-        head_bias[:, 128:256], HIGH,
-    )
-    head_col = bias_cols[:, 0:1]
-    pump(2)
+    bias_row = nn(head_bias[:, 0:128], ph0[...].astype(F32), HIGH) + nn(
+        head_bias[:, 128:256], ph1[...].astype(F32), HIGH
+    )
+    head_col = columns_of(bias_row)[:, 0:1]
+    pump(4, 2)
     landed_all(copies)
     ext[:, 0:128] = (halo_in[0].astype(F32) * low_f).astype(BF16)
     ext[:, 2176:2304] = (halo_in[1].astype(F32) * high_f).astype(BF16)
@@ -427,26 +484,29 @@
     lax.fori_loop(0, 8, conv_chunk, 0)
 
     def group_totals(kind, step=None):
-        ones = jnp.ones((8, 128), F32)
-        first, second = nt(ones, acc[0], HIGH), nt(ones, acc[1], HIGH)
+        ones = jnp.ones((8, 128), BF16)
+        first, second = [
+            nt(ones, part[0]) + (nt(ones, part[1]) + nt(ones, part[2]))
+            for part in (thirds(acc[0]), thirds(acc[1]))
+        ]
         k = kind - 1
         stat_out[k] = jnp.where(iota((8, 512), 0) == 0, first, second)
         copies = to_all(kind, stat_out.at[k], stat_in.at[k])
         stat_in[k, s] = stat_out[k]
         if step is not None:
-            pump(step)
+            pump(*step)
         landed_all(copies)
         total = stat_in[k, 0]
         for index in range(1, NS):
             total = total + stat_in[k, index]
-        columns = nt(same, total, HIGH)
+        sums = nn(jnp.concatenate(thirds(total), axis=0), same)
+        columns = columns_of(sums[0:8] + (sums[8:16] + sums[16:24]))
         return columns[:, 0:1] * (1.0 / CELLS), columns[:, 1:2] * (1.0 / CELLS)
 
-    average, square = group_totals(1, 3)
+    average, square = group_totals(1, (5, 3))
     inverse = 1.0 / jnp.sqrt(square - average * average + 1e-06)
     if weights is not None:
         weights.r_share(1)
-        weights.r_share(2)
 
     def head_chunk(i, carry):
         at = pl.multiple_of(i * 256, 256)
@@ -464,20 +524,17 @@
         return carry
 
     lax.fori_loop(0, 8, head_chunk, 0)
-    pump(4)
-    narrow = halves(nt(tth[...], pix[...]) + nt(ttl[...], pix[...]))
+    pump(6, 4)
+    narrow = nt(columns_w[...], pix[...]).astype(BF16)
     raw = jnp.zeros((80, 512), F32)
     for m in range(3):
-        part = [half[80 * m : 80 * m + 80] for half in narrow]
-        table = [rmh[512 * m : 512 * m + 512, :], rml[512 * m : 512 * m + 512, :]]
-        raw = raw + three(nn, part, table)
+        raw = raw + nn(narrow[128 * m : 128 * m + 80], rows_w[512 * m : 512 * m + 512, :])
     edge_out[0, 0] = raw[:, 256:384]
     edge_out[0, 1] = raw[:, 384:512]
     copies = to_sides(2 + 1, edge_out.at[0], edge_in.at[0])
-    pump(5)
+    pump(7, 5)
     if weights is not None:
         weights.r_core(1)
-        weights.s_pump(6)
     corr0 = jnp.where(low, 1.0, lane_rows[0:1, :])
     corr1 = jnp.where(high, 1.0, lane_rows[1:2, :])
     img_scale, img_shift = lane_rows[2:3, :], lane_rows[3:4, :]
@@ -501,22 +558,16 @@
     mask = (inner < 40).astype(F32)
     gains = [vecs[1 + i : 2 + i, :] for i in range(4)]
     shifts = [vecs[5 + i : 6 + i, :] for i in range(4)]
-    hat0, inv0 = norm_stats(embedded, mask, 1e-05)
-    hat1, inv1 = norm_stats(hat0 * gains[0] + shifts[0], mask, 1e-05)
-    unit = hat1 * gains[1] + shifts[1]
-    unit_b = unit.astype(BF16)
-    unit = unit_b.astype(F32)
+    pump(8, 6)
     if weights is not None:
-        weights.s_pump(7)
-        weights.r_core(2)
-        weights.s_pump(8)
-        weights.s_done()
+        weights.r_share(2)
+        weights.landed(0)
 
     class_hat, _ = norm_stats(vecs[0:1, :], mask, 1e-05)
     class_pre = class_hat * gains[0] + shifts[0]
     class_hat, _ = norm_stats(class_pre, mask, 1e-05)
     class_unit = jnp.broadcast_to(class_hat * gains[1] + shifts[1], (8, WIDE)).astype(BF16)
-    attn = [s_unit(i) for i in range(4)]
+    attn = [a_unit(i) for i in range(4)]
     class_qkv = jnp.concatenate([nn(class_unit, attn[i]) for i in range(4)], axis=1)
     class_qkv = class_qkv.astype(BF16).astype(F32)
     place512 = iota((8, 512), 1)
@@ -534,6 +585,12 @@
     kd_out[...] = key_dir[0:2]
     copies = to_all(4, kd_out, kd_in)
     kd_in[s] = key_dir[0:2]
+    hat0, inv0 = norm_stats(embedded, mask, 1e-05)
+    hat1, inv1 = norm_stats(hat0 * gains[0] + shifts[0], mask, 1e-05)
+    unit = hat1 * gains[1] + shifts[1]
+    unit_b = unit.astype(BF16)
+    unit = unit_b.astype(F32)
+    pump(None, 7)
     landed_all(copies)
     for index in range(NS):
         dirs[2 * index : 2 * index + 2, :] = kd_in[index]
@@ -545,6 +602,9 @@
         u_out[index, 2:4] = sums[2 * index : 2 * index + 2]
     copies = to_all(5, u_out, u_in, swap=True)
     u_in[s] = u_out[s]
+    pump(None, 8)
+    if weights is not None:
+        weights.r_core(2)
     landed_all(copies)
     total = u_in[0]
     for index in range(1, NS):
@@ -557,66 +617,90 @@
     heads3 = jnp.where(val_at[1:2, 384:512], second[1:2] + class_exp[1:2] * class_qkv[0:1, 384:512], 0.0)
     heads1 = heads1 / denominator[0:1]
     heads3 = heads3 / denominator[1:2]
-    rows1 = s_unit(4)
-    rows3 = s_unit(5)
+    rows1 = a_unit(4)
+    rows3 = a_unit(5)
 
     def wide8(row):
-        return jnp.broadcast_to(row, (8, row.shape[1])).astype(BF16)
+        if row.shape[0] == 1:
+            return jnp.broadcast_to(row, (8, row.shape[1])).astype(BF16)
+        return jnp.concatenate([row, jnp.zeros((6, row.shape[1]), F32)], axis=0).astype(BF16)
+
+    def mine_of(rows):
+        return jnp.where(half == 0, rows[0:1], rows[1:2])
 
     attn_part = nt(wide8(heads1), rows1) + nt(wide8(heads3), rows3)
 
-    def slab_sum(kind, k, row):
-        row_out[k] = row[0:1]
-        copies = to_all(kind, row_out.at[k], row_in.at[k])
-        row_in[k, s] = row[0:1]
+    def pair_sum(kind, k, rows):
+        row_out[k] = rows[0:2]
+        copies = [
+            remote(
+                row_out.at[k], row_in.at[k, half, s], x_send.at[kind, index], x_recv.at[kind, index],
+                target,
+            )
+            for index, target in pair_targets(f, s)
+        ]
+        for copy in copies:
+            copy.start()
+        live.extend(copies)
+        row_in[k, half, s] = row_out[k]
         landed_all(copies)
-        total = row_in[k, 0]
-        for index in range(1, NS):
-            total = total + row_in[k, index]
-        return total
-
-    block_mid = class_pre + slab_sum(6, 0, attn_part) + vecs[9:10, :]
+        sums = []
+        for h in range(2):
+            total = row_in[k, h, 0]
+            for index in range(1, NS):
+                total = total + row_in[k, h, index]
+            sums.append(total)
+        return sums
+
+    sums = pair_sum(6, 0, attn_part)
+    block_mid = class_pre + jnp.concatenate([sums[0][0:1], sums[1][0:1]], axis=0) + vecs[9:10, :]
     hat2, inv2 = norm_stats(block_mid, mask, 1e-05)
     mlp_input = hat2 * gains[2] + shifts[2]
     mlp_input = wide8(jnp.where(lane == 40, 1.0, mlp_input))
-    hidden_units = [s_unit(6 + i) for i in range(12)]
+    if weights is not None:
+        weights.landed(2)
+    hidden_units = [b_buf[i // 6, :, i % 6].reshape(WIDE // 2, 128) for i in range(12)]
+    unit_at = lax.rem(iota((1, WIDE // 2), 1), 48) < 20
     preact = nt(mlp_input[:, 0:128], hidden_units[0])
     for i in range(1, 12):
         preact = preact + nt(mlp_input[:, 128 * i : 128 * i + 128], hidden_units[i])
-    preact = jnp.where(inner < 20, preact, 0.0)
+    preact = jnp.where(unit_at, preact, 0.0)
     cdf = 0.5 * (1.0 + lax.erf(preact * 0.7071067811865476))
     active = preact * cdf
     active = pltpu.roll(active, 20, 1).astype(BF16)
     mlp_part = jnp.concatenate([nn(active, hidden_units[i]) for i in range(12)], axis=1)
-    block_out = block_mid + slab_sum(7, 1, mlp_part) + vecs[10:11, :]
+    sums = pair_sum(7, 1, mlp_part)
+    block_out = block_mid + (sums[0] + sums[1]) + vecs[10:11, :]
     hat3, inv3 = norm_stats(block_out, mask, 1e-05)
     post = wide8(hat3 * gains[3] + shifts[3])
     if weights is not None:
         weights.r_done(2)
     vit = [blocks(24 + 3 * u, 3) for u in range(8)]
-    embed = jnp.concatenate([nn(post, vit[u]) for u in range(8)], axis=1)[0:1]
-    words = text[...]
+    embed = jnp.concatenate([nn(post, vit[u]) for u in range(8)], axis=1)[0:2]
+    words_copy.wait_recv()
+    words = jnp.concatenate([text_in[0], text_in[1]], axis=0)
     dots = jnp.sum(embed * words, axis=-1, keepdims=True)
     size_e = jnp.sum(embed * embed, axis=-1, keepdims=True) + 1e-06
     size_t = jnp.sum(words * words, axis=-1, keepdims=True) + 1e-06
     sizes = jnp.sqrt(size_e) * jnp.sqrt(size_t)
     score = 100.0 * dots / sizes
-    score_out[...] = jnp.broadcast_to(score, (8, 128))
+    score_out[...] = jnp.broadcast_to(mine_of(score), (8, 128))
     d_embed = wide8((-1.0 / 64.0) * (100.0 * words / sizes - score * embed / size_e))
     d_post = nt(d_embed[:, 0:128], vit[0])
     for u in range(1, 8):
         d_post = d_post + nt(d_embed[:, 128 * u : 128 * u + 128], vit[u])
-    d_second = norm_back(d_post[0:1], hat3, inv3, gains[3])
+    d_second = norm_back(d_post[0:2], hat3, inv3, gains[3])
     d_second_b = wide8(d_second)
     d_active = nt(d_second_b[:, 0:128], hidden_units[0])
     for i in range(1, 12):
         d_active = d_active + nt(d_second_b[:, 128 * i : 128 * i + 128], hidden_units[i])
-    d_active = pltpu.roll(d_active, WIDE - 20, 1)
+    d_active = pltpu.roll(d_active, WIDE // 2 - 20, 1)
     slope = cdf + preact * jnp.exp(-0.5 * preact * preact) * 0.3989422804014327
-    d_pre = jnp.where(inner < 20, d_active * slope, 0.0).astype(BF16)
+    d_pre = jnp.where(unit_at, d_active * slope, 0.0).astype(BF16)
     input_part = jnp.concatenate([nn(d_pre, hidden_units[i]) for i in range(12)], axis=1)
-    d_input = slab_sum(8, 2, input_part)
-    d_first = wide8(d_second + norm_back(d_input, hat2, inv2, gains[2]))
+    sums = pair_sum(8, 2, input_part)
+    d_first = d_second + norm_back(sums[0] + sums[1], hat2, inv2, gains[2])
+    d_first = wide8(mine_of(d_first))
     d_heads1 = nn(d_first, rows1).astype(BF16)
     d_heads3 = nn(d_first, rows3).astype(BF16)
     value0 = nt(jnp.where(val_at[0:1, 128:256], d_heads1.astype(F32), 0.0).astype(BF16), attn[1])
@@ -655,25 +739,27 @@
     edge_out[1, 1] = d_top
     copies = to_sides(10, edge_out.at[1], edge_in.at[1])
     landed_all(copies)
-    d_raw = halves(
-        jnp.concatenate(
-            [d_top * corr0, d_bottom * corr1, edge_in[1, 1] * high_f, edge_in[1, 0] * low_f], axis=1
-        )
-    )
-    d_narrow = []
-    for m in range(3):
-        table = [rmh[512 * m : 512 * m + 512, :], rml[512 * m : 512 * m + 512, :]]
-        d_narrow.append(halves(three(nt, table, d_raw)))
-    for x in range(8):
-        d_pix = jnp.zeros((512, 128), F32)
-        for m in range(3):
-            table = [
-                t[80 * m : 80 * m + 80, 128 * x : 128 * x + 128] for t in (tth, ttl)
-            ]
-            d_pix = d_pix + three(nn, d_narrow[m], table)
-        d_pix = d_pix.astype(BF16)
-        for r in range(16):
-            cols_buf[32 * x : 32 * x + 32, 128 * r : 128 * r + 128] = d_pix[32 * r : 32 * r + 32]
+    d_raw = jnp.concatenate(
+        [
+            jnp.concatenate(
+                [d_top * corr0, d_bottom * corr1, edge_in[1, 1] * high_f, edge_in[1, 0] * low_f],
+                axis=1,
+            ),
+            jnp.zeros((48, 512), F32),
+        ],
+        axis=0,
+    ).astype(BF16)
+    d_narrow = jnp.concatenate(
+        [nt(rows_w[512 * m : 512 * m + 512, :], d_raw) for m in range(3)], axis=1
+    ).astype(BF16)
+    for k in range(4):
+        d_pix = nn(d_narrow, columns_w[:, 256 * k : 256 * k + 256]).astype(BF16)
+        for x in range(2):
+            rows = slice(64 * k + 32 * x, 64 * k + 32 * x + 32)
+            for r in range(16):
+                cols_buf[rows, 128 * r : 128 * r + 128] = d_pix[
+                    32 * r : 32 * r + 32, 128 * x : 128 * x + 128
+                ]
     acc[...] = jnp.zeros_like(acc)
 
     def head_back(i, carry):
@@ -755,8 +841,7 @@
     for copy in live:
         copy.wait_send()
     if weights is not None:
-        for slot in range(3):
-            weights.r_finish(slot)
+        weights.finish()
         mine[...] = gsplit[...].astype(BF16)
         reduce_gradient(mine, landed, terms, arrived, collected, sems[11:])
         whole = jnp.concatenate([collected[w] for w in range(2 * NS)], axis=0)
@@ -771,12 +856,6 @@
     places = np.arange(in_count) + 0.5
     weights = np.maximum(0.0, 1.0 - np.abs(places[None, :] - centers[:, None]) / stretch)
     return weights / weights.sum(axis=1, keepdims=True)
-
-
-def split_const(values):
-    high = values.astype(np.float32).astype(jnp.bfloat16)
-    rest = (values - high.astype(np.float64)).astype(jnp.bfloat16)
-    return jnp.asarray(high), jnp.asarray(rest)
 
 
 def constants():
@@ -794,7 +873,7 @@
                     if 0 <= at < 128:
                         inter[q, i2, j, i2, b, at] = 1
     table = resize_table(224, 1024)
-    columns = np.zeros((3, 5, 16, 8, 128))
+    columns = np.zeros((3, 8, 16, 8, 128))
     for m in range(3):
         for u in range(5):
             if 3 * u + m < 14:
@@ -831,12 +910,11 @@
                     ph[0, k, x, 8 * c + y] = 1
                 else:
                     ph[1, 16 + k - 128, x, 8 * c + y] = 1
-    tth, ttl = split_const(columns.reshape(240, 1024))
-    rmh, rml = split_const(rows.reshape(1536, 512))
     one = lambda v: jnp.asarray(v.astype(jnp.bfloat16))
     ph = ph.reshape(2, 128, 256)
     return (
-        one(perm), one(perm.T), one(inter.reshape(256, 768)), tth, ttl, rmh, rml,
+        one(perm), one(perm.T), one(inter.reshape(256, 768)),
+        one(columns.reshape(384, 1024)), one(rows.reshape(1536, 512)),
         one(ph[0]), one(ph[1]), jnp.asarray(lanes.astype(np.float32)),
     )
 
@@ -855,7 +933,8 @@
     mlp = widen(jnp.concatenate([mlp_in.T, mlp_out]))
     bias = jnp.pad(mlp_bias[:, None], ((0, 20), (40, WIDE - 41)))
     mlp = jnp.pad(mlp + bias, ((0, 8), (0, 0))).reshape(48, 12, 128).transpose(1, 0, 2)
-    s_pack = jnp.concatenate([attn, out0[None], out1[None], mlp]).reshape(2, 9, 48, 128)
+    a_pack = jnp.concatenate([attn, out0[None], out1[None]]).reshape(2, 3, 48, 128)
+    b_pack = mlp.reshape(2, 6, 48, 128)
     first = jnp.pad(proj, ((0, 0), (0, 64))).reshape(6, 16, 128)
     conv_t = conv.reshape(144, 16).T
     second = jnp.stack(
@@ -870,14 +949,14 @@
     third = third.transpose(0, 2, 1).reshape(15, 16, 128)
     fourth = jnp.pad(vit, ((0, 8), (0, 0))).reshape(48, 8, 128).transpose(1, 0, 2).reshape(24, 16, 128)
     r_pack = jnp.concatenate([first, second, third, fourth]).reshape(3, 16, 16, 128)
-    return s_pack, r_pack
+    return a_pack, b_pack, r_pack
 
 
 def run_step(packs, fetch, grad_shape, small, consts):
     vm, dma = pltpu.VMEM, pltpu.SemaphoreType.DMA
     scratch = [
         vm((512, 3072), BF16), vm((512, 3072), BF16),
-        vm((2, NZ, 2, 9, 48, 128), BF16), vm((3, 16, NF, 16, 128), BF16),
+        vm((2, NZ, 2, 3, 48, 128), BF16), vm((2, NZ, 6, 48, 128), BF16), vm((3, 16, NF, 16, 128), BF16),
         vm((3072, 128), BF16), vm((48, 2304), BF16), vm((2, 48, 128), BF16), vm((2, 48, 128), BF16),
         vm((512, LANES), F32), vm((512, LANES), F32), vm((2, 512, 128), F32),
         vm((2, 8, 512), F32), vm((2, NS, 8, 512), F32),
@@ -885,21 +964,21 @@
         vm((2, 2, 80, 128), F32), vm((2, 2, 80, 128), F32),
         vm((2, WIDE), F32), vm((NS, 2, WIDE), F32), vm((32, WIDE), F32),
         vm((NS, 4, WIDE), F32), vm((NS, 4, WIDE), F32),
-        vm((3, 1, WIDE), F32), vm((3, NS, 1, WIDE), F32),
+        vm((3, 2, WIDE), F32), vm((3, 2, NS, 2, WIDE), F32), vm((2, 1, 1024), F32),
         vm((4, WIDE), F32), vm((NS, 4, WIDE), F32),
         vm((2, 16, 128), F32), vm((2, 16, 128), F32),
         vm((16, 16, 768), F32), vm((16, 16, 768), BF16), vm((16, 16, 768), BF16),
         vm((NF, 4, 128), F32), vm((NF, 4, 128), F32), vm((16, 4, 128), F32),
-        dma((12, NS - 1)), dma((12, NS - 1)), dma((1,)),
+        dma((13, 15)), dma((13, 15)), dma((1,)),
         dma((3,)), dma((3,)), dma((3, NS - 1)), dma((3, NS - 1)), dma((3,)), dma((3,)),
-        dma((4,)), dma((2,)), dma((16,)), dma((16,)), dma((2,)),
+        dma((5,)), dma((2, 2)), dma((3, 16)), dma((3, 16)), dma((2, 2)),
         dma((15,)), dma((15,)), dma((31,)), dma((31,)), dma((15,)), dma((15,)),
     ]
     hidden, mods, noisy, sigma, proj_bias, vecs, text, chan, head_bias = small
     return pl.pallas_call(
         functools.partial(step_kernel, fetch),
         out_shape=[jax.ShapeDtypeStruct(grad_shape, F32), jax.ShapeDtypeStruct((8, 128), F32)],
-        in_specs=[ANY] + ([ANY] * 2 if fetch else [VMEM] * 2) + [VMEM] * 2 + [SMEM] + [VMEM] * 15,
+        in_specs=[ANY] + ([ANY] * 3 if fetch else [VMEM] * 3) + [VMEM] * 2 + [SMEM] + [VMEM] * 13,
         out_specs=[VMEM, VMEM],
         scratch_shapes=scratch,
         compiler_params=pltpu.CompilerParams(

time: 197 us -> 200 us (1.015)
  local copies, waits for them, and re-layouts: 7.94 us -> 13.9 us
  Pallas kernels: 184 us -> 182 us
    unnamed x50 -> x44, local copies, waits for them, and re-layouts: 2.01 us -> 5.08 us
where the time goes in v2:
time: 200 us; the launch traced here: 199 us
  Pallas kernels  182 us (91%)
  local copies, waits for them, and re-layouts  13.9 us (7%)
    pallas_call x1, Pallas kernels, run_step(): pl.pallas_call(functools.partial(step_kernel, fetch), out_shape=[jax.Shap...  182 us
    unnamed x44, local copies, waits for them, and re-layouts  5.08 us

profile of v2, /device:TPU:1, one launch (start us, length us, event | category | flops | bytes accessed | tf_op | source)
XLA Modules:
  0.0 199.0 jit_solution(9451079268131690981)
XLA Ops:
  0.7 0.9 fusion.4
  1.6 0.1 pad_bitcast_fusion.3
  1.7 0.8 bitcast_bitcast_fusion
  2.4 0.6 pad_maximum_fusion.1
  3.1 0.8 copy.63
  3.9 0.8 copy.55
  4.8 0.7 constant_dynamic-update-slice_fusion.3
  5.5 0.7 slice.32
  6.2 0.1 constant_dynamic-update-slice_fusion.2
  6.3 1.0 copy.57
  7.5 0.1 copy.59
  7.7 0.9 pad_bitcast_fusion.1
  9.5 0.1 concatenate.41
  9.6 0.1 concatenate.42
  10.0 0.4 reshape.88
  10.6 1.2 reshape.87.vecs
  11.8 0.2 copy.62
  12.2 0.1 pad.57
  12.2 0.8 copy.54
  13.2 0.7 maximum_maximum_fusion.chan
  13.9 0.6 broadcast_in_dim.42.head_bias
  14.5 181.8 %step.1 = (f32[96,64]{1,0:T(8,128)}, f32[8,128]{1,0:T(8,128)}) custom-call(bf16[512,3072]{1,0:T(8,128)(2,1)} %bitcast.55, bf16[2,3,48,128]{3,2,1,0:T(8,128)(2,1)} %bitcast.62, bf16[2,6,48,128]{3,2,1,0:T(8,128)(2,1)} %bitcast.59, bf16[3,16,16,128]{3,2,1,0:T(8,128)(2,1)} %bitcast.63, bf16[2,3072]{1,0:T(2,128)(2,1)} %bitcast.72, bf16[512,64]{1,0:T(8,128)(2,1)} %bitcast.65, ...), custom_call_target="tpu_custom_call" | custom-call | tf_op jit(solution)/shard_map/step/pallas_call | solution.py:978
  196.4 1.5 copy.61
  197.9 1.2 slice.35
  (62 shorter events, 1.1 us)
Async XLA Ops:
  0.6 8.7 %copy-start.6 = (f32[1280]{0:T(1024)S(1)}, f32[1280]{0:T(1024)}, u32[]{:S(2)}) copy-start(f32[1280]{0:T(1024)} %param.48) | copy-start | bytes 15364
  0.6 8.8 %copy-start.4 = (f32[4,1280]{1,0:T(4,128)S(1)}, f32[4,1280]{1,0:T(4,128)}, u32[]{:S(2)}) copy-start(f32[4,1280]{1,0:T(4,128)} %param.49) | copy-start | bytes 61444
  0.7 9.0 %copy-start.5 = (f32[4,1280]{1,0:T(4,128)S(1)}, f32[4,1280]{1,0:T(4,128)}, u32[]{:S(2)}) copy-start(f32[4,1280]{1,0:T(4,128)} %param.50) | copy-start | bytes 61444
  0.7 9.1 %copy-start.7 = (f32[1280]{0:T(1024)S(1)}, f32[1280]{0:T(1024)}, u32[]{:S(2)}) copy-start(f32[1280]{0:T(1024)} %param.53) | copy-start | bytes 15364
  0.7 9.2 %copy-start.8 = (f32[1280]{0:T(1024)S(1)}, f32[1280]{0:T(1024)}, u32[]{:S(2)}) copy-start(f32[1280]{0:T(1024)} %param.57) | copy-start | bytes 15364
  0.7 9.3 %copy-start.1 = (bf16[32,1280]{1,0:T(8,128)(2,1)S(1)}, bf16[32,1280]{1,0:T(8,128)(2,1)}, u32[]{:S(2)}) copy-start(bf16[32,1280]{1,0:T(8,128)(2,1)} %param.47) | copy-start | bytes 245764
  7.5 4.2 %copy-start.2 = (bf16[20,1280]{1,0:T(8,128)(2,1)S(1)}, bf16[20,1280]{1,0:T(8,128)(2,1)}, u32[]{:S(2)}) copy-start(bf16[20,1280]{1,0:T(8,128)(2,1)} %param.56) | copy-start | bytes 153604
  7.5 4.2 %copy-start.3 = (bf16[1280,20]{0,1:T(8,128)(2,1)S(1)}, bf16[1280,20]{0,1:T(8,128)(2,1)}, u32[]{:S(2)}) copy-start(bf16[1280,20]{0,1:T(8,128)(2,1)} %param.54) | copy-start | bytes 153604
  8.7 3.4 %copy-start = (bf16[48,16,128]{2,1,0:T(8,128)(2,1)}, bf16[48,16,128]{2,1,0:T(8,128)(2,1)S(1)}, u32[]{:S(2)}) copy-start(bf16[48,16,128]{2,1,0:T(8,128)(2,1)S(1)} %constant_dynamic-update-slice_fusion) | copy-start | bytes 589828
  9.5 2.6 %copy-start.13 = (bf16[20]{0:T(256)(128)(2,1)S(1)}, bf16[20]{0:T(256)(128)(2,1)}, u32[]{:S(2)}) copy-start(bf16[20]{0:T(256)(128)(2,1)} %param.55) | copy-start | bytes 124
  10.4 2.7 %copy-start.9 = (f32[512]{0:T(512)S(1)}, f32[512]{0:T(512)}, u32[]{:S(2)}) copy-start(f32[512]{0:T(512)} %param.43) | copy-start | bytes 6148
  10.4 2.7 %copy-start.10 = (f32[512]{0:T(512)S(1)}, f32[512]{0:T(512)}, u32[]{:S(2)}) copy-start(f32[512]{0:T(512)} %param.42) | copy-start | bytes 6148
  10.5 2.7 %copy-start.11 = (f32[512]{0:T(512)S(1)}, f32[512]{0:T(512)}, u32[]{:S(2)}) copy-start(f32[512]{0:T(512)} %param.41) | copy-start | bytes 6148
  10.5 3.4 %copy-start.12 = (f32[192]{0:T(256)S(1)}, f32[192]{0:T(256)}, u32[]{:S(2)}) copy-start(f32[192]{0:T(256)} %param.45) | copy-start | bytes 2308
  10.5 3.4 %slice-start = ((f32[192]{0:T(256)}), f32[128]{0:T(128)S(1)}, s32[]{:S(2)}) async-start(f32[192]{0:T(256)} %param.45), calls=%async_computation | async-start | bytes 1024 | tf_op jit(solution)/shard_map/slice | solution.py:1014

commit v3 on v2

--- a/solution.py
+++ b/solution.py
@@ -79,9 +79,9 @@
 
 
 class Weights:
-    def __init__(self, a_in, b_in, r_in, a_buf, b_buf, r_buf, sems):
-        self.ins, self.r_in = (a_in, b_in), r_in
-        self.a_buf, self.b_buf, self.r_buf = a_buf, b_buf, r_buf
+    def __init__(self, c_own, p_own, a_own, b_own, c_buf, p_buf, a_buf, b_buf, sems):
+        self.c_own, self.p_own, self.owns = c_own, p_own, (a_own, b_own)
+        self.c_buf, self.p_buf, self.bufs = c_buf, p_buf, (a_buf, b_buf)
         (self.z_send, self.z_recv, self.sh_send, self.sh_recv, self.fw_send, self.fw_recv,
          self.loc, self.pair_sem, self.ring_send, self.ring_recv, self.core_sem) = sems
         self.f = lax.axis_index("fsdp")
@@ -90,83 +90,107 @@
         self.w = self.g * NS + self.s
         self.z, self.half = self.f // 2, lax.rem(self.f, 2)
         self.core = {"grp": 1 - self.g}
-
-    def r_own(self, slot):
-        return pltpu.make_async_copy(
-            self.r_in.at[slot, self.w], self.r_buf.at[slot, self.w, self.f], self.loc.at[slot]
-        )
-
-    def r_start(self, slot):
-        self.r_own(slot).start()
-
+        self.inside = self.f // 16 == self.g
+
+    def to_fsdp(self, source, dest, k):
         def send(d, carry):
             target = {"fsdp": lax.rem(self.f + d, NF)}
-            remote(
-                self.r_in.at[slot, self.w], self.r_buf.at[slot, self.w, self.f],
-                self.z_send.at[slot], self.z_recv.at[slot], target,
-            ).start()
+            remote(source, dest, self.z_send.at[k], self.z_recv.at[k], target).start()
             return carry
 
         lax.fori_loop(1, NF, send, 0)
 
-    def r_share(self, slot):
-        block = self.r_buf.at[slot, self.w]
-        if slot < 2:
-            many = self.r_buf.at[slot, self.w, pl.ds(0, NF - 1)]
-            remote(many, many, self.z_send.at[slot], self.z_recv.at[slot], self.core).wait_recv()
-            self.r_own(slot).wait()
+    def c_copy(self):
+        return pltpu.make_async_copy(
+            self.c_own.at[self.s], self.c_buf.at[self.s, self.f], self.loc.at[0]
+        )
+
+    def c_start(self):
+        @pl.when(self.inside)
+        def _():
+            self.c_copy().start()
+            self.to_fsdp(self.c_own.at[self.s], self.c_buf.at[self.s, self.f], 0)
+
+    def c_part(self, n):
+        return self.c_buf.at[n, pl.ds(16 * self.g, 16)]
+
+    def c_share(self):
+        @pl.when(self.inside)
+        def _():
+            self.c_copy().wait()
+            many = self.c_buf.at[self.s, pl.ds(16 * self.g, 15)]
+            remote(many, many, self.z_send.at[0], self.z_recv.at[0], self.core).wait_recv()
+
+        @pl.when(jnp.logical_not(self.inside))
+        def _():
+            many = self.c_part(self.s)
+            remote(many, many, self.z_send.at[0], self.z_recv.at[0], self.core).wait_recv()
+
         for d in range(1, NS):
-            remote(
-                block, block, self.sh_send.at[slot, d - 1], self.sh_recv.at[slot, d - 1],
-                {"slab": lax.rem(self.s + d, NS)},
-            ).start()
-
-    def r_core(self, slot):
+            self.share_copy(0, d, self.c_part(self.s)).start()
+
+    def share_copy(self, k, d, block):
+        return remote(
+            block, block, self.sh_send.at[k, d - 1], self.sh_recv.at[k, d - 1],
+            {"slab": lax.rem(self.s + d, NS)},
+        )
+
+    def core_copy(self, k, block):
+        return remote(block, block, self.fw_send.at[k], self.fw_recv.at[k], self.core)
+
+    def c_core(self):
         for d in range(1, NS):
-            block = self.r_buf.at[slot, self.g * NS + lax.rem(self.s + NS - d, NS)]
-            remote(
-                block, block, self.sh_send.at[slot, d - 1], self.sh_recv.at[slot, d - 1], self.core
-            ).wait_recv()
-        many = self.r_buf.at[slot, pl.ds(self.g * NS, NS)]
-        remote(many, many, self.fw_send.at[slot], self.fw_recv.at[slot], self.core).start()
-
-    def r_done(self, slot):
-        many = self.r_buf.at[slot, pl.ds((1 - self.g) * NS, NS)]
-        remote(many, many, self.fw_send.at[slot], self.fw_recv.at[slot], self.core).wait_recv()
+            self.share_copy(0, d, self.c_part(lax.rem(self.s + NS - d, NS))).wait_recv()
+        self.core_copy(0, self.c_buf.at[:, pl.ds(16 * self.g, 16)]).start()
+
+    def c_done(self):
+        self.core_copy(0, self.c_buf.at[:, pl.ds(16 - 16 * self.g, 16)]).wait_recv()
+
+    def p_copy(self):
+        return pltpu.make_async_copy(
+            self.p_own.at[self.w], self.p_buf.at[self.w, self.f], self.loc.at[1]
+        )
+
+    def p_start(self):
+        self.p_copy().start()
+        self.to_fsdp(self.p_own.at[self.w], self.p_buf.at[self.w, self.f], 1)
+
+    def p_ready(self):
+        many = self.p_buf.at[self.w, pl.ds(0, NF - 1)]
+        remote(many, many, self.z_send.at[1], self.z_recv.at[1], self.core).wait_recv()
+        self.p_copy().wait()
+
+    def p_share(self, *pieces):
+        for d in pieces:
+            self.share_copy(1, d, self.p_buf.at[self.w]).start()
+
+    def p_core(self):
+        for d in range(1, NS):
+            block = self.p_buf.at[self.g * NS + lax.rem(self.s + NS - d, NS)]
+            self.share_copy(1, d, block).wait_recv()
+        self.core_copy(1, self.p_buf.at[pl.ds(self.g * NS, NS)]).start()
+
+    def p_done(self):
+        self.core_copy(1, self.p_buf.at[pl.ds((1 - self.g) * NS, NS)]).wait_recv()
 
     def view(self, kind, z):
-        z = lax.rem(z, NZ)
-        if kind == 0:
-            return self.a_buf.at[self.g, z]
-        if kind == 1:
-            return self.r_buf.at[2, self.w, pl.ds(2 * z, 2)]
-        return self.b_buf.at[self.g, z]
-
-    def own(self):
-        return [
-            pltpu.make_async_copy(
-                self.ins[0].at[self.g], self.a_buf.at[self.g, self.z, self.half], self.loc.at[3]
-            ),
-            self.r_own(2),
-            pltpu.make_async_copy(self.ins[1].at[self.g], self.b_buf.at[self.g, self.z], self.loc.at[4]),
-        ]
+        return self.bufs[kind].at[self.g, lax.rem(z, NZ)]
+
+    def own(self, kind):
+        dest = self.view(kind, self.z)
+        dest = dest.at[self.half] if kind == 0 else dest
+        return pltpu.make_async_copy(self.owns[kind], dest, self.loc.at[2 + kind])
 
     def pair(self):
-        other = {"fsdp": self.z * 2 + 1 - self.half}
-        return [
-            remote(
-                self.ins[0].at[self.g], self.a_buf.at[self.g, self.z, self.half],
-                self.pair_sem.at[0, 0], self.pair_sem.at[0, 1], other,
-            ),
-            remote(
-                self.r_in.at[2, self.w], self.r_buf.at[2, self.w, self.f],
-                self.pair_sem.at[1, 0], self.pair_sem.at[1, 1], other,
-            ),
-        ]
+        return remote(
+            self.owns[0], self.bufs[0].at[self.g, self.z, self.half],
+            self.pair_sem.at[0], self.pair_sem.at[1], {"fsdp": self.z * 2 + 1 - self.half},
+        )
 
     def start(self):
-        for copy in self.pair() + self.own():
-            copy.start()
+        self.pair().start()
+        self.own(0).start()
+        self.own(1).start()
 
     def step(self, kind, step, way):
         sign = NZ - 1 if way == 0 else 1
@@ -179,62 +203,65 @@
         )
 
     def share(self, kind, z):
-        if kind == 1:
-            return
-        block, k = self.view(kind, z), kind // 2
-        remote(block, block, self.core_sem.at[k, 0], self.core_sem.at[k, 1], self.core).start()
-
-    def pump(self, kinds, step):
+        block = self.view(kind, z)
+        remote(block, block, self.core_sem.at[kind, 0], self.core_sem.at[kind, 1], self.core).start()
+
+    def pump(self, kind, step):
         steps = (NZ // 2, NZ // 2 - 1)
-        for kind in kinds:
-            if step == 0:
-                self.own()[kind].wait()
-                if kind < 2:
-                    self.pair()[kind].wait_recv()
-            for way in (0, 1):
-                if 0 < step <= steps[way]:
-                    self.step(kind, step - 1, way).wait_recv()
-                if step < steps[way]:
-                    self.step(kind, step, way).start()
-            if step == 0:
-                self.share(kind, self.z)
-            for way in (0, 1):
-                if 0 < step <= steps[way]:
-                    self.share(kind, self.z + (NZ - step if way == 0 else step))
+        if step == 0:
+            self.own(kind).wait()
+            if kind == 0:
+                self.pair().wait_recv()
+        for way in (0, 1):
+            if 0 < step <= steps[way]:
+                self.step(kind, step - 1, way).wait_recv()
+            if step < steps[way]:
+                self.step(kind, step, way).start()
+        if step == 0:
+            self.share(kind, self.z)
+        for way in (0, 1):
+            if 0 < step <= steps[way]:
+                self.share(kind, self.z + (NZ - step if way == 0 else step))
 
     def landed(self, kind):
-        buffer, k = (self.a_buf, self.b_buf)[kind // 2], kind // 2
-        theirs = buffer.at[1 - self.g]
-        remote(theirs, theirs, self.core_sem.at[k, 0], self.core_sem.at[k, 1], self.core).wait_recv()
+        theirs = self.bufs[kind].at[1 - self.g]
+        remote(
+            theirs, theirs, self.core_sem.at[kind, 0], self.core_sem.at[kind, 1], self.core
+        ).wait_recv()
 
     def finish(self):
-        for k, buffer in enumerate((self.a_buf, self.b_buf)):
-            mine = buffer.at[self.g]
-            remote(mine, mine, self.core_sem.at[k, 0], self.core_sem.at[k, 1], self.core).wait_send()
-        for copy in self.pair():
-            copy.wait_send()
-        for kind in range(3):
+        for kind in range(2):
+            mine = self.bufs[kind].at[self.g]
+            remote(
+                mine, mine, self.core_sem.at[kind, 0], self.core_sem.at[kind, 1], self.core
+            ).wait_send()
             for way, steps in ((0, NZ // 2), (1, NZ // 2 - 1)):
                 for step in range(steps):
                     self.step(kind, step, way).wait_send()
-        for slot in range(3):
-            if slot < 2:
-                many = self.r_buf.at[slot, self.w, pl.ds(0, NF - 1)]
-                remote(many, many, self.z_send.at[slot], self.z_recv.at[slot], self.core).wait_send()
-            block = self.r_buf.at[slot, self.w]
-            for d in range(1, NS):
-                remote(
-                    block, block, self.sh_send.at[slot, d - 1], self.sh_recv.at[slot, d - 1], self.core
-                ).wait_send()
-            many = self.r_buf.at[slot, pl.ds(self.g * NS, NS)]
-            remote(many, many, self.fw_send.at[slot], self.fw_recv.at[slot], self.core).wait_send()
+        self.pair().wait_send()
+
+        @pl.when(self.inside)
+        def _():
+            many = self.c_buf.at[self.s, pl.ds(0, NF - 1)]
+            remote(many, many, self.z_send.at[0], self.z_recv.at[0], self.core).wait_send()
+
+        many = self.p_buf.at[self.w, pl.ds(0, NF - 1)]
+        remote(many, many, self.z_send.at[1], self.z_recv.at[1], self.core).wait_send()
+        for d in range(1, NS):
+            self.share_copy(0, d, self.c_part(self.s)).wait_send()
+            self.share_copy(1, d, self.p_buf.at[self.w]).wait_send()
+        self.core_copy(0, self.c_buf.at[:, pl.ds(16 * self.g, 16)]).wait_send()
+        self.core_copy(1, self.p_buf.at[pl.ds(self.g * NS, NS)]).wait_send()
 
 
 def greet(targets):
     barrier = pltpu.get_barrier_semaphore()
     for target in targets:
         pl.semaphore_signal(barrier, inc=1, device_id=target, device_id_type=MESH)
-    pl.semaphore_wait(barrier, len(targets))
+
+
+def greeted(targets):
+    pl.semaphore_wait(pltpu.get_barrier_semaphore(), len(targets))
 
 
 def block_targets(g, s):
@@ -257,9 +284,9 @@
     return found
 
 
-def greet_all():
+def all_targets():
     f, g, s = lax.axis_index("fsdp"), lax.axis_index("grp"), lax.axis_index("slab")
-    greet(
+    return (
         [target for _, target in block_targets(g, s)]
         + [{"fsdp": lax.rem(f + d, NF)} for d in range(1, NF)]
         + [target for _, target in pair_targets(f, s)[NS:]]
@@ -305,13 +332,70 @@
         copy.wait()
 
 
+def pack_tiles(
+    g, s, proj_in, conv_in, tail_in, head_in, patch_in, attn_in, back_in, up_in, bias_in, down_in,
+    vit_in, patch_perm, wide_w, fill, c_own, p_own, a_own, b_own,
+):
+    proj = proj_in[...].astype(F32)
+    proj = jnp.concatenate([proj[0:48], proj[48:96]], axis=1).astype(BF16)
+    for n in range(3):
+        c_own[n] = proj[16 * n : 16 * n + 16]
+    c_own[3] = conv_in[:, 0:128]
+    c_own[4] = head_in[:, 0:128]
+    c_own[5] = tail_in[...]
+    patch = nn(patch_in[...], patch_perm[...])
+    patch = jnp.concatenate([patch, jnp.zeros((8, 640), F32)], axis=0).astype(BF16)
+    for u in range(5):
+        for rb in range(3):
+            n = 3 * u + rb
+            block = patch[16 * rb : 16 * rb + 16, 128 * u : 128 * u + 128]
+            if n < 2:
+                c_own[6 + n] = block
+            else:
+                p_own[n - 2] = block
+    for n in range(13, 16):
+        p_own[n] = jnp.zeros((16, 128), BF16)
+
+    def tall(rows, lanes):
+        values = rows.astype(F32)
+        more = lanes - values.shape[1]
+        if more:
+            values = jnp.concatenate([values, jnp.zeros((40, more), F32)], axis=1)
+        return jnp.concatenate([values, jnp.zeros((8, lanes), F32)], axis=0)
+
+    attn = tall(attn_in[...], 512)
+    back = tall(back_in[...], 256)
+    vit = tall(vit_in[:, pl.ds(pl.multiple_of(128 * s, 128), 128)], 128)
+    tiles = [attn[:, 128 * u : 128 * u + 128] for u in range(4)] + [back[:, 0:128], back[:, 128:256]]
+    for u in range(3):
+        a_own[48 * u : 48 * u + 48, :] = jnp.where(g == 0, tiles[u], tiles[3 + u]).astype(BF16)
+    last = jnp.concatenate([vit[32:48], jnp.zeros((16, 128), F32)], axis=0)
+    a_own[144:176, :] = jnp.where(g == 0, vit[0:32], last).astype(BF16)
+    fill[0:20, :] = up_in[...].astype(F32)
+    fill[20:40, :] = down_in[...].astype(F32)
+    fill[40:48, :] = jnp.zeros((8, WIDTH), F32)
+    values = fill[...].astype(BF16)
+    wide = jnp.concatenate([nn(values[:, 0:640], wide_w[...]), nn(values[:, 640:1280], wide_w[...])], axis=1)
+    bias = jnp.where(
+        iota((48, 20), 0) == iota((48, 20), 1), jnp.broadcast_to(bias_in[...].astype(F32), (48, 20)), 0.0
+    )
+    bias = jnp.sum(bias, axis=1, keepdims=True)
+    wide = jnp.where(iota((48, WIDE), 1) == 40, bias, wide)
+    wide = jnp.where(g == 0, wide[:, 0:768], wide[:, 768:1536]).astype(BF16)
+    for u in range(6):
+        b_own[u] = wide[:, 128 * u : 128 * u + 128]
+
+
 def step_kernel(
-    fetch, hidden, a_in, b_in, r_in, mods, noisy, sigma_ref, proj_bias, vecs, text, chan, head_bias,
-    perm, perm_t, inter, columns_w, rows_w, ph0, ph1, lane_rows,
+    fetch, hidden, shards, mods, noisy, sigma_ref, proj_bias, class_in, gain_in, shift_in,
+    back_bias, down_bias, position_in, text, conv_b_in, norm_g_in, norm_s_in, head_b_in,
+    perm, perm_t, inter, columns_w, rows_w, ph0, ph1, lane_rows, patch_perm, wide_w,
     grad_out, score_out,
-    hid, mod, a_buf, b_buf, r_buf, proj_full, ext, halo_out, halo_in, nrm, dnrm, acc, stat_out, stat_in,
+    hid, mod, c_own, p_own, a_own, b_own, c_buf, p_buf, a_buf, b_buf, vecs, fill,
+    proj_full, ext, halo_out, halo_in, nrm, dnrm, acc, stat_out, stat_in,
     cols_buf, pix, head_t, head_p, edge_out, edge_in, kd_out, kd_in, dirs, u_out, u_in,
-    row_out, row_in, text_in, vd_out, vd_in, rim_out, rim_in, gsplit, mine, landed, terms, arrived, collected,
+    row_out, row_in, text_in, emb_out, emb_in, vd_out, vd_in, rim_out, rim_in, gsplit, mine, landed,
+    terms, arrived, collected,
     x_send, x_recv, hid_sem, *sems,
 ):
     s = lax.axis_index("slab")
@@ -354,32 +438,9 @@
         for copy in copies:
             copy.wait_recv()
 
-    if fetch:
-        greet_all()
-        weights = Weights(a_in, b_in, r_in, a_buf, b_buf, r_buf, sems[:11])
-        weights.r_start(0)
-        weights.start()
-        weights.r_start(1)
-    else:
-        greet([target for _, target in pair_targets(f, s)])
-        a_buf[...] = a_in[...]
-        b_buf[...] = b_in[0]
-        r_buf[...] = r_in[...]
-        weights = None
-    words_copy = remote(
-        text, text_in.at[half], x_send.at[12, 0], x_recv.at[12, 0], {"fsdp": f + 1 - 2 * half}
-    )
-    words_copy.start()
-    live.append(words_copy)
-    text_in[half] = text[...]
-
-    def pump(*steps):
-        if weights is not None:
-            for kinds, step in zip(((0, 1), (2,)), steps):
-                if step is not None:
-                    weights.pump(kinds, step)
-
-    hid_copy.wait()
+    targets = all_targets() if fetch else [target for _, target in pair_targets(f, s)]
+    greet(targets)
+
     scale = 1.0 + mods[1:2].astype(F32)
     shift = mods[0:1].astype(F32)
 
@@ -396,27 +457,75 @@
 
         lax.fori_loop(lo, hi, body, 0)
 
-    modulate(0, 6)
-    pump(0, 0)
-    modulate(6, 16)
-    pump(1)
+    if fetch:
+        weights = Weights(c_own, p_own, a_own, b_own, c_buf, p_buf, a_buf, b_buf, sems[:11])
+        pack_tiles(
+            weights.g, s, *shards, patch_perm, wide_w, fill, c_own, p_own, a_own, b_own
+        )
+    else:
+        weights = None
+        for ref, given in zip((c_buf, p_buf, a_buf, b_buf), shards):
+            ref[...] = given[...]
+    hid_copy.wait()
+    modulate(0, 8)
+    greeted(targets)
+    if fetch:
+        weights.c_start()
+        weights.start()
+        weights.p_start()
+    words_copy = remote(
+        text, text_in.at[half], x_send.at[12, 0], x_recv.at[12, 0], {"fsdp": f + 1 - 2 * half}
+    )
+    words_copy.start()
+    live.append(words_copy)
+    text_in[half] = text[...]
+
+    def pump(*steps):
+        if weights is not None:
+            for kind, step in enumerate(steps):
+                if step is not None:
+                    weights.pump(kind, step)
+
+    fill[0:1, :] = class_in[...]
+    fill[1:5, :] = gain_in[...]
+    fill[5:9, :] = shift_in[...]
+    fill[9:10, :] = back_bias[...]
+    fill[10:11, :] = down_bias[...]
+    fill[11:16, :] = jnp.zeros((5, WIDTH), F32)
+    fill[16:48, :] = position_in[...].astype(F32)
+    for k in range(2):
+        parts = jnp.concatenate(thirds(fill[:, 640 * k : 640 * k + 640]), axis=0)
+        parts = nn(parts, wide_w[...])
+        vecs[:, 768 * k : 768 * k + 768] = parts[0:48] + (parts[48:96] + parts[96:144])
+    pump(None, 0)
+    modulate(8, 12)
+    pump(0)
+    modulate(12, 16)
     if weights is not None:
-        weights.r_share(0)
+        weights.c_share()
+        pump(1)
+        weights.c_core()
         pump(2, 1)
-        weights.r_core(0)
-        pump(3)
-        weights.r_done(0)
-
-    def blocks(first, count):
-        parts = [r_buf[n // 16, n % 16] for n in range(first, first + count)]
-        return jnp.concatenate(parts, axis=1).reshape(NF * 16 * count, 128)
+        weights.c_done()
+
+    def patch_unit(u):
+        parts = []
+        for rb in range(3):
+            n = 3 * u + rb
+            parts.append(c_buf[6 + n] if n < 2 else p_buf[n - 2])
+        return jnp.concatenate(parts, axis=1).reshape(WIDE, 128)
 
     def a_unit(index):
-        return a_buf[index // 3, :, :, index % 3].reshape(WIDE, 128)
-
-    for k in range(NF):
-        for n in range(6):
-            proj_full[96 * k + 16 * n : 96 * k + 16 * n + 16, :] = r_buf[0, n, k]
+        k = index % 3
+        return a_buf[index // 3, :, :, 48 * k : 48 * k + 48].reshape(WIDE, 128)
+
+    for n in range(3):
+        both = c_buf[n].reshape(512, 128).astype(F32)
+        turned = pltpu.roll(both, 64, 1).astype(BF16)
+        for k in range(NF):
+            at = 96 * k + 16 * n
+            proj_full[at : at + 16, :] = c_buf[n, k]
+            proj_full[at + 48 : at + 64, :] = turned[16 * k : 16 * k + 16]
     velocity = nn(mod[...], proj_full[...])[:, :64] + proj_bias[...]
     clean = noisy[...].astype(F32) - sigma * velocity
     lat_tok = (clean / LAT_SCALE + LAT_SHIFT).astype(BF16)
@@ -449,23 +558,31 @@
         width = rows.shape[1]
         return jnp.transpose(jnp.concatenate([rows, jnp.zeros((120, width), F32)], axis=0))
 
-    chan_cols = columns_of(chan[...])
+    chan = jnp.concatenate(
+        [conv_b_in[...], norm_g_in[...], norm_s_in[...], jnp.zeros((5, 512), F32)], axis=0
+    )
+    chan_cols = columns_of(chan)
     conv_bias, gain, gshift = chan_cols[:, 0:1], chan_cols[:, 1:2], chan_cols[:, 2:3]
     eye = (iota((128, 128), 0) == iota((128, 128), 1)).astype(BF16)
-    conv0 = r_buf[0, 6].reshape(512, 128)
-    head0 = r_buf[0, 7].reshape(512, 128)
-    tail = r_buf[0, 8].reshape(512, 128)
+    conv0 = c_buf[3].reshape(512, 128)
+    head0 = c_buf[4].reshape(512, 128)
+    tail = c_buf[5].reshape(512, 128)
     head_p[...] = (nn(head0, ph0[...]) + nn(tail, ph1[...])).astype(BF16)
     head_t[...] = (
         lax.dot_general(ph0[...], head0, (((0,), (1,)), ((), ())), preferred_element_type=F32)
         + lax.dot_general(ph1[...], tail, (((0,), (1,)), ((), ())), preferred_element_type=F32)
     ).astype(BF16)
+    head_bias = jnp.broadcast_to(head_b_in[...], (8, 256))
     bias_row = nn(head_bias[:, 0:128], ph0[...].astype(F32), HIGH) + nn(
         head_bias[:, 128:256], ph1[...].astype(F32), HIGH
     )
     head_col = columns_of(bias_row)[:, 0:1]
-    pump(4, 2)
+    pump(3, 2)
+    if weights is not None:
+        weights.p_ready()
     landed_all(copies)
+    if weights is not None:
+        weights.p_share(1, 2, 3)
     ext[:, 0:128] = (halo_in[0].astype(F32) * low_f).astype(BF16)
     ext[:, 2176:2304] = (halo_in[1].astype(F32) * high_f).astype(BF16)
     acc[...] = jnp.zeros_like(acc)
@@ -503,10 +620,10 @@
         columns = columns_of(sums[0:8] + (sums[8:16] + sums[16:24]))
         return columns[:, 0:1] * (1.0 / CELLS), columns[:, 1:2] * (1.0 / CELLS)
 
-    average, square = group_totals(1, (5, 3))
+    average, square = group_totals(1, (4, 3))
     inverse = 1.0 / jnp.sqrt(square - average * average + 1e-06)
     if weights is not None:
-        weights.r_share(1)
+        weights.p_share(4, 5, 6, 7)
 
     def head_chunk(i, carry):
         at = pl.multiple_of(i * 256, 256)
@@ -524,7 +641,7 @@
         return carry
 
     lax.fori_loop(0, 8, head_chunk, 0)
-    pump(6, 4)
+    pump(5, 4)
     narrow = nt(columns_w[...], pix[...]).astype(BF16)
     raw = jnp.zeros((80, 512), F32)
     for m in range(3):
@@ -532,14 +649,14 @@
     edge_out[0, 0] = raw[:, 256:384]
     edge_out[0, 1] = raw[:, 384:512]
     copies = to_sides(2 + 1, edge_out.at[0], edge_in.at[0])
-    pump(7, 5)
+    pump(6, 5)
     if weights is not None:
-        weights.r_core(1)
+        weights.p_core()
     corr0 = jnp.where(low, 1.0, lane_rows[0:1, :])
     corr1 = jnp.where(high, 1.0, lane_rows[1:2, :])
     img_scale, img_shift = lane_rows[2:3, :], lane_rows[3:4, :]
     if weights is not None:
-        weights.r_done(1)
+        weights.p_done()
     landed_all(copies)
     top = (raw[:, 0:128] * corr0 + edge_in[0, 0] * low_f) * img_scale + img_shift
     bottom = (raw[:, 128:256] * corr1 + edge_in[0, 1] * high_f) * img_scale + img_shift
@@ -550,9 +667,10 @@
         ],
         axis=0,
     ).astype(BF16)
+    pump(7)
     embedded = vecs[16:48, :]
     for u in range(5):
-        embedded = embedded + nt(patches[:, 128 * u : 128 * u + 128], blocks(9 + 3 * u, 3))
+        embedded = embedded + nt(patches[:, 128 * u : 128 * u + 128], patch_unit(u))
     lane = iota((1, WIDE), 1)
     inner = lax.rem(lane, 48)
     mask = (inner < 40).astype(F32)
@@ -560,7 +678,6 @@
     shifts = [vecs[5 + i : 6 + i, :] for i in range(4)]
     pump(8, 6)
     if weights is not None:
-        weights.r_share(2)
         weights.landed(0)
 
     class_hat, _ = norm_stats(vecs[0:1, :], mask, 1e-05)
@@ -603,8 +720,6 @@
     copies = to_all(5, u_out, u_in, swap=True)
     u_in[s] = u_out[s]
     pump(None, 8)
-    if weights is not None:
-        weights.r_core(2)
     landed_all(copies)
     total = u_in[0]
     for index in range(1, NS):
@@ -658,7 +773,7 @@
     mlp_input = hat2 * gains[2] + shifts[2]
     mlp_input = wide8(jnp.where(lane == 40, 1.0, mlp_input))
     if weights is not None:
-        weights.landed(2)
+        weights.landed(1)
     hidden_units = [b_buf[i // 6, :, i % 6].reshape(WIDE // 2, 128) for i in range(12)]
     unit_at = lax.rem(iota((1, WIDE // 2), 1), 48) < 20
     preact = nt(mlp_input[:, 0:128], hidden_units[0])
@@ -673,22 +788,33 @@
     block_out = block_mid + (sums[0] + sums[1]) + vecs[10:11, :]
     hat3, inv3 = norm_stats(block_out, mask, 1e-05)
     post = wide8(hat3 * gains[3] + shifts[3])
-    if weights is not None:
-        weights.r_done(2)
-    vit = [blocks(24 + 3 * u, 3) for u in range(8)]
-    embed = jnp.concatenate([nn(post, vit[u]) for u in range(8)], axis=1)[0:2]
+    vit = jnp.concatenate([a_buf[0, :, :, 144:176], a_buf[1, :, :, 144:160]], axis=2).reshape(WIDE, 128)
+    embed = nn(post, vit)[0:2]
     words_copy.wait_recv()
     words = jnp.concatenate([text_in[0], text_in[1]], axis=0)
-    dots = jnp.sum(embed * words, axis=-1, keepdims=True)
-    size_e = jnp.sum(embed * embed, axis=-1, keepdims=True) + 1e-06
+    own_words = jnp.concatenate(
+        [text_in[k, :, pl.ds(pl.multiple_of(128 * s, 128), 128)] for k in range(2)], axis=0
+    )
+    four = jnp.concatenate([own_words, embed], axis=0)
+    exact = four.astype(BF16).astype(F32)
+    eight = nt(jnp.concatenate([exact, four - exact], axis=0).astype(BF16), vit)
+    four = eight[0:4] + eight[4:8]
+    dots = jnp.sum(embed * own_words, axis=-1, keepdims=True)
+    squares = jnp.sum(embed * embed, axis=-1, keepdims=True)
+    emb_out[0:2, :] = four[0:2]
+    emb_out[2:4, :] = jnp.where(lane == 40, dots, jnp.where(lane == 41, squares, four[2:4]))
+    copies = to_all(13, emb_out, emb_in)
+    emb_in[s] = emb_out[...]
+    landed_all(copies)
+    total = emb_in[0]
+    for index in range(1, NS):
+        total = total + emb_in[index]
+    dots, size_e = total[2:4, 40:41], total[2:4, 41:42] + 1e-06
     size_t = jnp.sum(words * words, axis=-1, keepdims=True) + 1e-06
     sizes = jnp.sqrt(size_e) * jnp.sqrt(size_t)
     score = 100.0 * dots / sizes
     score_out[...] = jnp.broadcast_to(mine_of(score), (8, 128))
-    d_embed = wide8((-1.0 / 64.0) * (100.0 * words / sizes - score * embed / size_e))
-    d_post = nt(d_embed[:, 0:128], vit[0])
-    for u in range(1, 8):
-        d_post = d_post + nt(d_embed[:, 128 * u : 128 * u + 128], vit[u])
+    d_post = (-1.0 / 64.0) * ((100.0 / sizes) * total[0:2] - (score / size_e) * total[2:4])
     d_second = norm_back(d_post[0:2], hat3, inv3, gains[3])
     d_second_b = wide8(d_second)
     d_active = nt(d_second_b[:, 0:128], hidden_units[0])
@@ -732,7 +858,7 @@
     )
     d_pre_x = norm_back(d_unit, hat1, inv1, gains[1])
     d_embedded = norm_back(d_pre_x, hat0, inv0, gains[0]).astype(BF16)
-    d_parts = [nn(d_embedded, blocks(9 + 3 * u, 3)) for u in range(5)]
+    d_parts = [nn(d_embedded, patch_unit(u)) for u in range(5)]
     d_top = jnp.concatenate([part[0:16] for part in d_parts], axis=0) * img_scale
     d_bottom = jnp.concatenate([part[16:32] for part in d_parts], axis=0) * img_scale
     edge_out[1, 0] = d_bottom
@@ -912,51 +1038,42 @@
                     ph[1, 16 + k - 128, x, 8 * c + y] = 1
     one = lambda v: jnp.asarray(v.astype(jnp.bfloat16))
     ph = ph.reshape(2, 128, 256)
+    order = np.zeros((3, 14, 14, 640))
+    for c in range(3):
+        for a in range(14):
+            for b in range(14):
+                order[c, a, b, 128 * (b // 3) + 42 * (b % 3) + 14 * c + a] = 1
+    wide = np.zeros((16, 40, 16, 48))
+    for k in range(16):
+        wide[k, np.arange(40), k, np.arange(40)] = 1
     return (
         one(perm), one(perm.T), one(inter.reshape(256, 768)),
         one(columns.reshape(384, 1024)), one(rows.reshape(1536, 512)),
         one(ph[0]), one(ph[1]), jnp.asarray(lanes.astype(np.float32)),
-    )
-
-
-def widen(values):
-    shape = values.shape[:-1]
-    view = values.reshape(shape + (32, 40))
-    return jnp.pad(view, [(0, 0)] * len(shape) + [(0, 0), (0, 8)]).reshape(shape + (WIDE,))
-
-
-def pack_weights(proj, conv, head, patch, attn_in, attn_out, mlp_in, mlp_bias, mlp_out, vit):
-    attn = jnp.pad(attn_in, ((0, 8), (0, 32))).reshape(48, 4, 128).transpose(1, 0, 2)
+        one(order.reshape(588, 640)), one(wide.reshape(640, 768)),
+    )
+
+
+def raw_shards(proj, conv, head, patch, attn_in, attn_out, mlp_in, mlp_bias, mlp_out, vit):
+    conv_t = conv.reshape(144, 16).T
+    tail = jnp.pad(jnp.concatenate([conv_t[:, 128:], head[:, 128:]], axis=1), ((0, 0), (0, 48)))
     back = attn_out.T
-    out0 = jnp.pad(back[:, :80], ((0, 8), (32, 16)))
-    out1 = jnp.pad(back[:, 80:], ((0, 8), (16, 32)))
-    mlp = widen(jnp.concatenate([mlp_in.T, mlp_out]))
-    bias = jnp.pad(mlp_bias[:, None], ((0, 20), (40, WIDE - 41)))
-    mlp = jnp.pad(mlp + bias, ((0, 8), (0, 0))).reshape(48, 12, 128).transpose(1, 0, 2)
-    a_pack = jnp.concatenate([attn, out0[None], out1[None]]).reshape(2, 3, 48, 128)
-    b_pack = mlp.reshape(2, 6, 48, 128)
-    first = jnp.pad(proj, ((0, 0), (0, 64))).reshape(6, 16, 128)
-    conv_t = conv.reshape(144, 16).T
-    second = jnp.stack(
-        [
-            conv_t[:, :128],
-            head[:, :128],
-            jnp.pad(jnp.concatenate([conv_t[:, 128:], head[:, 128:]], axis=1), ((0, 0), (0, 48))),
-        ]
-    )
-    third = jnp.pad(patch.reshape(3, 14, 14, 40).transpose(2, 0, 1, 3), ((0, 1), (0, 0), (0, 0), (0, 0)))
-    third = jnp.pad(third.reshape(5, 126, 40), ((0, 0), (0, 2), (0, 8)))
-    third = third.transpose(0, 2, 1).reshape(15, 16, 128)
-    fourth = jnp.pad(vit, ((0, 8), (0, 0))).reshape(48, 8, 128).transpose(1, 0, 2).reshape(24, 16, 128)
-    r_pack = jnp.concatenate([first, second, third, fourth]).reshape(3, 16, 16, 128)
-    return a_pack, b_pack, r_pack
-
-
-def run_step(packs, fetch, grad_shape, small, consts):
+    back = jnp.concatenate(
+        [jnp.pad(back[:, :80], ((0, 0), (32, 16))), jnp.pad(back[:, 80:], ((0, 0), (16, 32)))], axis=1
+    )
+    return (
+        proj, conv_t, tail, head, patch.T, attn_in, back, mlp_in.T, mlp_bias[None], mlp_out, vit
+    )
+
+
+def run_step(shards, fetch, grad_shape, hidden, sigma, small, consts):
     vm, dma = pltpu.VMEM, pltpu.SemaphoreType.DMA
     scratch = [
         vm((512, 3072), BF16), vm((512, 3072), BF16),
-        vm((2, NZ, 2, 3, 48, 128), BF16), vm((2, NZ, 6, 48, 128), BF16), vm((3, 16, NF, 16, 128), BF16),
+        vm((8, 16, 128), BF16), vm((16, 16, 128), BF16), vm((176, 128), BF16), vm((6, 48, 128), BF16),
+        vm((8, NF, 16, 128), BF16), vm((16, NF, 16, 128), BF16),
+        vm((2, NZ, 2, 176, 128), BF16), vm((2, NZ, 6, 48, 128), BF16),
+        vm((48, WIDE), F32), vm((48, WIDTH), F32),
         vm((3072, 128), BF16), vm((48, 2304), BF16), vm((2, 48, 128), BF16), vm((2, 48, 128), BF16),
         vm((512, LANES), F32), vm((512, LANES), F32), vm((2, 512, 128), F32),
         vm((2, 8, 512), F32), vm((2, NS, 8, 512), F32),
@@ -966,26 +1083,34 @@
         vm((NS, 4, WIDE), F32), vm((NS, 4, WIDE), F32),
         vm((3, 2, WIDE), F32), vm((3, 2, NS, 2, WIDE), F32), vm((2, 1, 1024), F32),
         vm((4, WIDE), F32), vm((NS, 4, WIDE), F32),
+        vm((4, WIDE), F32), vm((NS, 4, WIDE), F32),
         vm((2, 16, 128), F32), vm((2, 16, 128), F32),
         vm((16, 16, 768), F32), vm((16, 16, 768), BF16), vm((16, 16, 768), BF16),
         vm((NF, 4, 128), F32), vm((NF, 4, 128), F32), vm((16, 4, 128), F32),
-        dma((13, 15)), dma((13, 15)), dma((1,)),
-        dma((3,)), dma((3,)), dma((3, NS - 1)), dma((3, NS - 1)), dma((3,)), dma((3,)),
-        dma((5,)), dma((2, 2)), dma((3, 16)), dma((3, 16)), dma((2, 2)),
+        dma((14, 15)), dma((14, 15)), dma((1,)),
+        dma((2,)), dma((2,)), dma((2, NS - 1)), dma((2, NS - 1)), dma((2,)), dma((2,)),
+        dma((4,)), dma((2,)), dma((2, 16)), dma((2, 16)), dma((2, 2)),
         dma((15,)), dma((15,)), dma((31,)), dma((31,)), dma((15,)), dma((15,)),
     ]
-    hidden, mods, noisy, sigma, proj_bias, vecs, text, chan, head_bias = small
+    count = len(shards)
+
+    def kernel(hidden_ref, *refs):
+        mods, noisy, sigma_ref = refs[count : count + 3]
+        step_kernel(
+            fetch, hidden_ref, refs[:count], mods, noisy, sigma_ref, *refs[count + 3 :]
+        )
+
     return pl.pallas_call(
-        functools.partial(step_kernel, fetch),
+        kernel,
         out_shape=[jax.ShapeDtypeStruct(grad_shape, F32), jax.ShapeDtypeStruct((8, 128), F32)],
-        in_specs=[ANY] + ([ANY] * 3 if fetch else [VMEM] * 3) + [VMEM] * 2 + [SMEM] + [VMEM] * 13,
+        in_specs=[ANY] + [VMEM] * (count + 2) + [SMEM] + [VMEM] * (len(small) - 2 + len(consts)),
         out_specs=[VMEM, VMEM],
         scratch_shapes=scratch,
         compiler_params=pltpu.CompilerParams(
             collective_id=0, has_side_effects=True, vmem_limit_bytes=60 * 1024 * 1024
         ),
         name="step",
-    )(hidden, *packs, mods, noisy, sigma, proj_bias, vecs, text, chan, head_bias, *consts)
+    )(hidden, *shards, *small[:2], sigma, *small[2:], *consts)
 
 
 def flow_sigma(step_index):
@@ -994,27 +1119,16 @@
 
 
 def prepare(
-    hidden, modulation, noisy, step_index, proj_bias, conv_bias, norm_gain, norm_shift, head_bias,
+    modulation, noisy, proj_bias, conv_bias, norm_gain, norm_shift, head_bias,
     position, class_token, vit_gain, vit_shift, attn_out_bias, mlp_out_bias, text_embed,
 ):
-    stack = jnp.concatenate(
-        [
-            class_token[None], vit_gain, vit_shift, attn_out_bias[None], mlp_out_bias[None],
-            jnp.zeros((5, WIDTH), F32), position.astype(F32),
-        ]
-    )
-    chan = jnp.concatenate(
-        [conv_bias[None], norm_gain[None], norm_shift[None], jnp.zeros((5, 512), F32)]
+    padded = jnp.concatenate(
+        [head_bias[:128], jnp.zeros((16,), F32), head_bias[128:], jnp.zeros((48,), F32)]
     )
     return (
-        hidden.reshape(512, 3072), modulation[0], noisy.reshape(512, 64),
-        flow_sigma(step_index).reshape(1, 1), proj_bias[None], widen(stack), text_embed, chan,
-        jnp.broadcast_to(
-            jnp.pad(
-                jnp.concatenate([head_bias[:128], jnp.zeros((16,), F32), head_bias[128:]]), (0, 48)
-            ),
-            (8, 256),
-        ),
+        modulation[0], noisy.reshape(512, 64), proj_bias[None], class_token[None], vit_gain, vit_shift,
+        attn_out_bias[None], mlp_out_bias[None], position, text_embed, conv_bias[None],
+        norm_gain[None], norm_shift[None], padded[None],
     )
 
 
@@ -1024,16 +1138,18 @@
     vit_gain, vit_shift, attn_in, attn_out, attn_out_bias, mlp_in, mlp_in_bias, mlp_out,
     mlp_out_bias, vit_proj, text_embed,
 ):
-    packs = pack_weights(
+    shards = raw_shards(
         proj_weight, conv_weight, head_weight, patch_weight, attn_in, attn_out, mlp_in,
         mlp_in_bias, mlp_out, vit_proj,
     )
     small = prepare(
-        hidden, modulation, noisy, step_index, proj_bias, conv_bias, norm_gain, norm_shift,
-        head_bias, position, class_token, vit_gain, vit_shift, attn_out_bias, mlp_out_bias,
-        text_embed,
-    )
-    grad, score = run_step(packs, True, (96, 64), small, constants())
+        modulation, noisy, proj_bias, conv_bias, norm_gain, norm_shift, head_bias, position,
+        class_token, vit_gain, vit_shift, attn_out_bias, mlp_out_bias, text_embed,
+    )
+    grad, score = run_step(
+        shards, True, (96, 64), hidden.reshape(512, 3072), flow_sigma(step_index).reshape(1, 1),
+        small, constants(),
+    )
     return grad, score[0, 0:1]
 
 

time: 200 us -> 187 us (0.935)
  Pallas kernels: 182 us -> 171 us
  local copies, waits for them, and re-layouts: 13.9 us -> 11.7 us
    pallas_call x1, Pallas kernels: 182 us -> 171 us  [run_step(): pl.pallas_call(kernel, out_shape=[jax.ShapeDtypeStruct(grad_shape, F32),...]
    broadcast_in_dim x3 -> x4, local copies, waits for them, and re-layouts: 0.68 us -> 3.87 us  [the longest x1 1.29 us: prepare(): class_token[None]]
    reshape x6 -> x1, local copies, waits for them, and re-layouts: 3.15 us -> 0.82 us  [raw_shards(): conv_t = conv.reshape(144, 16).T]
    unnamed x44 -> x4, local copies, waits for them, and re-layouts: 5.08 us -> 2.92 us
where the time goes in v3:
time: 187 us; the launch traced here: 186 us
  Pallas kernels  171 us (91%)
  local copies, waits for them, and re-layouts  11.7 us (6%)
  other arithmetic  1.98 us (1%)
    pallas_call x1, Pallas kernels, run_step(): pl.pallas_call(kernel, out_shape=[jax.ShapeDtypeStruct(grad_shape, F32),...  171 us

profile of v3, /device:TPU:1, one launch (start us, length us, event | category | flops | bytes accessed | tf_op | source)
XLA Modules:
  0.0 186.2 jit_solution(10522199526254046791)
XLA Ops:
  1.3 0.7 slice.26
  2.0 0.7 slice.25
  2.7 0.6 pad_maximum_fusion
  3.3 0.7 slice.22
  4.0 1.3 broadcast_in_dim.32.refs_15_
  5.3 1.3 broadcast_in_dim.33.refs_18_
  6.6 1.3 broadcast_in_dim.34.refs_19_
  7.9 0.8 copy.44
  8.7 0.0 copy-start
  8.7 0.7 fusion.5.refs_2_
  9.4 0.9 fusion.6
  10.3 0.7 fusion.2.refs_6_
  10.9 1.4 copy.42.refs_0_
  12.4 0.0 copy-done
  12.4 171.2 %step.1 = (f32[96,64]{1,0:T(8,128)}, f32[8,128]{1,0:T(8,128)}) custom-call(bf16[512,3072]{1,0:T(8,128)(2,1)} %bitcast.16, bf16[96,64]{1,0:T(8,128)(2,1)} %copy.42.refs_0_, bf16[16,144]{1,0:T(8,128)(2,1)} %bitcast.21, bf16[16,128]{1,0:T(8,128)(2,1)} %fusion.5.refs_2_, bf16[16,192]{1,0:T(8,128)(2,1)} %refs_3_.1, bf16[40,588]{1,0:T(8,128)(2,1)} %bitcast.19, ...), custom_call_target="tpu_custom_call" | custom-call | tf_op jit(solution)/shard_map/step/pallas_call | solution.py:1103
  183.6 1.2 slice.27
  184.8 1.5 copy.43
  (3 shorter events, 0.0 us)
Async XLA Ops:
  8.7 3.7 %copy-start = (bf16[144,16]{0,1:T(8,128)(2,1)}, bf16[144,16]{0,1:T(8,128)(2,1)S(1)}, u32[]{:S(2)}) copy-start(bf16[144,16]{0,1:T(8,128)(2,1)S(1)} %copy.44) | copy-start | bytes 13828

commit v4 on v3

--- a/solution.py
+++ b/solution.py
@@ -333,16 +333,19 @@
 
 
 def pack_tiles(
-    g, s, proj_in, conv_in, tail_in, head_in, patch_in, attn_in, back_in, up_in, bias_in, down_in,
-    vit_in, patch_perm, wide_w, fill, c_own, p_own, a_own, b_own,
+    g, s, proj_in, conv_in, head_in, patch_in, attn_in, back_in, up_in, bias_in, down_in,
+    vit_in, patch_perm, wide_w, back_perm, tail_perm, fill, c_own, p_own, a_own, b_own,
 ):
-    proj = proj_in[...].astype(F32)
+    choose = (iota((96, 96), 0) == iota((96, 96), 1)).astype(BF16)
+    proj = nt(choose, proj_in[...])
     proj = jnp.concatenate([proj[0:48], proj[48:96]], axis=1).astype(BF16)
     for n in range(3):
         c_own[n] = proj[16 * n : 16 * n + 16]
     c_own[3] = conv_in[:, 0:128]
     c_own[4] = head_in[:, 0:128]
-    c_own[5] = tail_in[...]
+    c_own[5] = (
+        nn(conv_in[:, 128:144], tail_perm[0:16, :]) + nn(head_in[:, 128:192], tail_perm[16:80, :])
+    ).astype(BF16)
     patch = nn(patch_in[...], patch_perm[...])
     patch = jnp.concatenate([patch, jnp.zeros((8, 640), F32)], axis=0).astype(BF16)
     for u in range(5):
@@ -364,7 +367,7 @@
         return jnp.concatenate([values, jnp.zeros((8, lanes), F32)], axis=0)
 
     attn = tall(attn_in[...], 512)
-    back = tall(back_in[...], 256)
+    back = tall(nn(back_in[...], back_perm[...]), 256)
     vit = tall(vit_in[:, pl.ds(pl.multiple_of(128 * s, 128), 128)], 128)
     tiles = [attn[:, 128 * u : 128 * u + 128] for u in range(4)] + [back[:, 0:128], back[:, 128:256]]
     for u in range(3):
@@ -387,14 +390,13 @@
 
 
 def step_kernel(
-    fetch, hidden, shards, mods, noisy, sigma_ref, proj_bias, class_in, gain_in, shift_in,
-    back_bias, down_bias, position_in, text, conv_b_in, norm_g_in, norm_s_in, head_b_in,
-    perm, perm_t, inter, columns_w, rows_w, ph0, ph1, lane_rows, patch_perm, wide_w,
+    fetch, hidden, shards, mods, noisy, sigma_ref, flat, gain_in, shift_in, position_in, text,
+    perm, perm_t, inter, columns_w, rows_w, ph0, ph1, lane_rows, patch_perm, wide_w, back_perm, tail_perm,
     grad_out, score_out,
     hid, mod, c_own, p_own, a_own, b_own, c_buf, p_buf, a_buf, b_buf, vecs, fill,
     proj_full, ext, halo_out, halo_in, nrm, dnrm, acc, stat_out, stat_in,
     cols_buf, pix, head_t, head_p, edge_out, edge_in, kd_out, kd_in, dirs, u_out, u_in,
-    row_out, row_in, text_in, emb_out, emb_in, vd_out, vd_in, rim_out, rim_in, gsplit, mine, landed,
+    ao_out, ao_in, row_out, row_in, text_in, emb_out, emb_in, vd_out, vd_in, rim_out, rim_in, gsplit, mine, landed,
     terms, arrived, collected,
     x_send, x_recv, hid_sem, *sems,
 ):
@@ -438,6 +440,9 @@
         for copy in copies:
             copy.wait_recv()
 
+    def flat_row(first, count):
+        return jnp.concatenate([flat[k : k + 1, :] for k in range(first, first + count)], axis=1)
+
     targets = all_targets() if fetch else [target for _, target in pair_targets(f, s)]
     greet(targets)
 
@@ -460,7 +465,7 @@
     if fetch:
         weights = Weights(c_own, p_own, a_own, b_own, c_buf, p_buf, a_buf, b_buf, sems[:11])
         pack_tiles(
-            weights.g, s, *shards, patch_perm, wide_w, fill, c_own, p_own, a_own, b_own
+            weights.g, s, *shards, patch_perm, wide_w, back_perm, tail_perm, fill, c_own, p_own, a_own, b_own
         )
     else:
         weights = None
@@ -472,7 +477,6 @@
     if fetch:
         weights.c_start()
         weights.start()
-        weights.p_start()
     words_copy = remote(
         text, text_in.at[half], x_send.at[12, 0], x_recv.at[12, 0], {"fsdp": f + 1 - 2 * half}
     )
@@ -486,23 +490,22 @@
                 if step is not None:
                     weights.pump(kind, step)
 
-    fill[0:1, :] = class_in[...]
+    fill[0:1, :] = flat_row(14, 10)
     fill[1:5, :] = gain_in[...]
     fill[5:9, :] = shift_in[...]
-    fill[9:10, :] = back_bias[...]
-    fill[10:11, :] = down_bias[...]
+    fill[9:10, :] = flat_row(24, 10)
+    fill[10:11, :] = flat_row(34, 10)
     fill[11:16, :] = jnp.zeros((5, WIDTH), F32)
     fill[16:48, :] = position_in[...].astype(F32)
     for k in range(2):
         parts = jnp.concatenate(thirds(fill[:, 640 * k : 640 * k + 640]), axis=0)
         parts = nn(parts, wide_w[...])
         vecs[:, 768 * k : 768 * k + 768] = parts[0:48] + (parts[48:96] + parts[96:144])
-    pump(None, 0)
-    modulate(8, 12)
-    pump(0)
-    modulate(12, 16)
+    modulate(8, 16)
     if weights is not None:
         weights.c_share()
+        pump(0, 0)
+        weights.p_start()
         pump(1)
         weights.c_core()
         pump(2, 1)
@@ -526,7 +529,8 @@
             at = 96 * k + 16 * n
             proj_full[at : at + 16, :] = c_buf[n, k]
             proj_full[at + 48 : at + 64, :] = turned[16 * k : 16 * k + 16]
-    velocity = nn(mod[...], proj_full[...])[:, :64] + proj_bias[...]
+    velocity = nn(mod[...], proj_full[...])[:, :64] + flat[13:14, 0:64]
+    pump(3)
     clean = noisy[...].astype(F32) - sigma * velocity
     lat_tok = (clean / LAT_SCALE + LAT_SHIFT).astype(BF16)
     tok_t = nt(perm_t[...], lat_tok)
@@ -559,7 +563,7 @@
         return jnp.transpose(jnp.concatenate([rows, jnp.zeros((120, width), F32)], axis=0))
 
     chan = jnp.concatenate(
-        [conv_b_in[...], norm_g_in[...], norm_s_in[...], jnp.zeros((5, 512), F32)], axis=0
+        [flat_row(0, 4), flat_row(4, 4), flat_row(8, 4), jnp.zeros((5, 512), F32)], axis=0
     )
     chan_cols = columns_of(chan)
     conv_bias, gain, gshift = chan_cols[:, 0:1], chan_cols[:, 1:2], chan_cols[:, 2:3]
@@ -572,12 +576,11 @@
         lax.dot_general(ph0[...], head0, (((0,), (1,)), ((), ())), preferred_element_type=F32)
         + lax.dot_general(ph1[...], tail, (((0,), (1,)), ((), ())), preferred_element_type=F32)
     ).astype(BF16)
-    head_bias = jnp.broadcast_to(head_b_in[...], (8, 256))
-    bias_row = nn(head_bias[:, 0:128], ph0[...].astype(F32), HIGH) + nn(
-        head_bias[:, 128:256], ph1[...].astype(F32), HIGH
+    bias_row = nn(jnp.broadcast_to(flat[12:13, :], (8, 128)), ph0[...].astype(F32), HIGH) + nn(
+        jnp.broadcast_to(flat[44:45, :], (8, 128)), ph1[...].astype(F32), HIGH
     )
     head_col = columns_of(bias_row)[:, 0:1]
-    pump(3, 2)
+    pump(4, 2)
     if weights is not None:
         weights.p_ready()
     landed_all(copies)
@@ -607,7 +610,7 @@
             for part in (thirds(acc[0]), thirds(acc[1]))
         ]
         k = kind - 1
-        stat_out[k] = jnp.where(iota((8, 512), 0) == 0, first, second)
+        stat_out[k] = jnp.concatenate([first[0:1], second[0:1]], axis=0)
         copies = to_all(kind, stat_out.at[k], stat_in.at[k])
         stat_in[k, s] = stat_out[k]
         if step is not None:
@@ -616,11 +619,12 @@
         total = stat_in[k, 0]
         for index in range(1, NS):
             total = total + stat_in[k, index]
+        total = jnp.concatenate([total, jnp.zeros((6, 512), F32)], axis=0)
         sums = nn(jnp.concatenate(thirds(total), axis=0), same)
         columns = columns_of(sums[0:8] + (sums[8:16] + sums[16:24]))
         return columns[:, 0:1] * (1.0 / CELLS), columns[:, 1:2] * (1.0 / CELLS)
 
-    average, square = group_totals(1, (4, 3))
+    average, square = group_totals(1, (5, 3))
     inverse = 1.0 / jnp.sqrt(square - average * average + 1e-06)
     if weights is not None:
         weights.p_share(4, 5, 6, 7)
@@ -640,8 +644,10 @@
                 ]
         return carry
 
-    lax.fori_loop(0, 8, head_chunk, 0)
-    pump(5, 4)
+    lax.fori_loop(0, 4, head_chunk, 0)
+    pump(6, 4)
+    lax.fori_loop(4, 8, head_chunk, 0)
+    pump(7, 5)
     narrow = nt(columns_w[...], pix[...]).astype(BF16)
     raw = jnp.zeros((80, 512), F32)
     for m in range(3):
@@ -649,37 +655,14 @@
     edge_out[0, 0] = raw[:, 256:384]
     edge_out[0, 1] = raw[:, 384:512]
     copies = to_sides(2 + 1, edge_out.at[0], edge_in.at[0])
-    pump(6, 5)
+    pump(8, 6)
     if weights is not None:
         weights.p_core()
-    corr0 = jnp.where(low, 1.0, lane_rows[0:1, :])
-    corr1 = jnp.where(high, 1.0, lane_rows[1:2, :])
-    img_scale, img_shift = lane_rows[2:3, :], lane_rows[3:4, :]
-    if weights is not None:
-        weights.p_done()
-    landed_all(copies)
-    top = (raw[:, 0:128] * corr0 + edge_in[0, 0] * low_f) * img_scale + img_shift
-    bottom = (raw[:, 128:256] * corr1 + edge_in[0, 1] * high_f) * img_scale + img_shift
-    patches = jnp.concatenate(
-        [
-            jnp.concatenate([part[16 * u : 16 * u + 16] for u in range(5)], axis=1)
-            for part in (top, bottom)
-        ],
-        axis=0,
-    ).astype(BF16)
-    pump(7)
-    embedded = vecs[16:48, :]
-    for u in range(5):
-        embedded = embedded + nt(patches[:, 128 * u : 128 * u + 128], patch_unit(u))
+        weights.landed(0)
     lane = iota((1, WIDE), 1)
-    inner = lax.rem(lane, 48)
-    mask = (inner < 40).astype(F32)
+    mask = (lax.rem(lane, 48) < 40).astype(F32)
     gains = [vecs[1 + i : 2 + i, :] for i in range(4)]
     shifts = [vecs[5 + i : 6 + i, :] for i in range(4)]
-    pump(8, 6)
-    if weights is not None:
-        weights.landed(0)
-
     class_hat, _ = norm_stats(vecs[0:1, :], mask, 1e-05)
     class_pre = class_hat * gains[0] + shifts[0]
     class_hat, _ = norm_stats(class_pre, mask, 1e-05)
@@ -700,23 +683,40 @@
     for i in range(1, 4):
         key_dir = key_dir + nt(query_b[:, 128 * i : 128 * i + 128], attn[i])
     kd_out[...] = key_dir[0:2]
-    copies = to_all(4, kd_out, kd_in)
+    kd_copies = to_all(4, kd_out, kd_in)
     kd_in[s] = key_dir[0:2]
+    corr0 = jnp.where(low, 1.0, lane_rows[0:1, :])
+    corr1 = jnp.where(high, 1.0, lane_rows[1:2, :])
+    img_scale, img_shift = lane_rows[2:3, :], lane_rows[3:4, :]
+    if weights is not None:
+        weights.p_done()
+    landed_all(copies)
+    top = (raw[:, 0:128] * corr0 + edge_in[0, 0] * low_f) * img_scale + img_shift
+    bottom = (raw[:, 128:256] * corr1 + edge_in[0, 1] * high_f) * img_scale + img_shift
+    patches = jnp.concatenate(
+        [
+            jnp.concatenate([part[16 * u : 16 * u + 16] for u in range(5)], axis=1)
+            for part in (top, bottom)
+        ],
+        axis=0,
+    ).astype(BF16)
+    embedded = vecs[16:48, :]
+    for u in range(5):
+        embedded = embedded + nt(patches[:, 128 * u : 128 * u + 128], patch_unit(u))
     hat0, inv0 = norm_stats(embedded, mask, 1e-05)
     hat1, inv1 = norm_stats(hat0 * gains[0] + shifts[0], mask, 1e-05)
     unit = hat1 * gains[1] + shifts[1]
     unit_b = unit.astype(BF16)
     unit = unit_b.astype(F32)
     pump(None, 7)
-    landed_all(copies)
+    landed_all(kd_copies)
     for index in range(NS):
         dirs[2 * index : 2 * index + 2, :] = kd_in[index]
     token_exp = jnp.exp(nt(dirs[0:16, :], unit, HIGH) / ROOT)
     gathered = nn(token_exp, unit, HIGH)
-    sums = jnp.broadcast_to(jnp.sum(token_exp, axis=1, keepdims=True), (16, WIDE))
+    gathered = jnp.where(lane == 40, jnp.sum(token_exp, axis=1, keepdims=True), gathered)
     for index in range(NS):
-        u_out[index, 0:2] = gathered[2 * index : 2 * index + 2]
-        u_out[index, 2:4] = sums[2 * index : 2 * index + 2]
+        u_out[index] = gathered[2 * index : 2 * index + 2]
     copies = to_all(5, u_out, u_in, swap=True)
     u_in[s] = u_out[s]
     pump(None, 8)
@@ -724,7 +724,7 @@
     total = u_in[0]
     for index in range(1, NS):
         total = total + u_in[index]
-    denominator = class_exp[0:2] + total[2:4, 0:1]
+    denominator = class_exp[0:2] + total[:, 40:41]
     mixed = halves(jnp.concatenate([total[0:2], jnp.zeros((6, WIDE), F32)], axis=0))
     first = nn(mixed[0], attn[1]) + nn(mixed[1], attn[1])
     second = nn(mixed[0], attn[3]) + nn(mixed[1], attn[3])
@@ -767,8 +767,23 @@
             sums.append(total)
         return sums
 
-    sums = pair_sum(6, 0, attn_part)
-    block_mid = class_pre + jnp.concatenate([sums[0][0:1], sums[1][0:1]], axis=0) + vecs[9:10, :]
+    ao_out[...] = attn_part[0:1]
+    copies = [
+        remote(ao_out, ao_in.at[half, s], x_send.at[6, index], x_recv.at[6, index], target)
+        for index, target in pair_targets(f, s)
+    ]
+    for copy in copies:
+        copy.start()
+    live.extend(copies)
+    ao_in[half, s] = attn_part[0:1]
+    landed_all(copies)
+    sums = []
+    for h in range(2):
+        total = ao_in[h, 0]
+        for index in range(1, NS):
+            total = total + ao_in[h, index]
+        sums.append(total)
+    block_mid = class_pre + jnp.concatenate(sums, axis=0) + vecs[9:10, :]
     hat2, inv2 = norm_stats(block_mid, mask, 1e-05)
     mlp_input = hat2 * gains[2] + shifts[2]
     mlp_input = wide8(jnp.where(lane == 40, 1.0, mlp_input))
@@ -833,10 +848,9 @@
     value1 = nt(jnp.where(val_at[1:2, 384:512], d_heads3.astype(F32), 0.0).astype(BF16), attn[3])
     expect0 = jnp.sum(d_heads1[0:1].astype(F32) * heads1, axis=-1, keepdims=True)
     expect1 = jnp.sum(d_heads3[0:1].astype(F32) * heads3, axis=-1, keepdims=True)
-    vd_out[0:1, :] = value0[0:1]
-    vd_out[1:2, :] = value1[0:1]
-    vd_out[2:3, :] = jnp.where(lane < 128, denominator[0:1], denominator[1:2])
-    vd_out[3:4, :] = jnp.where(lane < 128, expect0, expect1)
+    values = jnp.concatenate([value0[0:1], value1[0:1]], axis=0)
+    expects = jnp.concatenate([expect0, expect1], axis=0)
+    vd_out[...] = jnp.where(lane == 40, denominator, jnp.where(lane == 41, expects, values))
     copies = to_all(9, vd_out, vd_in)
     vd_in[s] = vd_out[...]
     token_logits = nt(unit, dirs[0:16, :], HIGH) / ROOT
@@ -845,11 +859,11 @@
     denominators = jnp.zeros((1, 16), F32)
     expects = jnp.zeros((1, 16), F32)
     for index in range(NS):
-        dirs[16 + 2 * index : 18 + 2 * index, :] = vd_in[index, 0:2]
+        dirs[16 + 2 * index : 18 + 2 * index, :] = vd_in[index]
         for h in range(2):
             here = head_at == 2 * index + h
-            denominators = jnp.where(here, vd_in[index, 2:3, 128 * h : 128 * h + 1], denominators)
-            expects = jnp.where(here, vd_in[index, 3:4, 128 * h : 128 * h + 1], expects)
+            denominators = jnp.where(here, vd_in[index, h : h + 1, 40:41], denominators)
+            expects = jnp.where(here, vd_in[index, h : h + 1, 41:42], expects)
     token_weight = jnp.exp(token_logits) / denominators
     token_dots = nt(unit, dirs[16:32, :], HIGH)
     logit_grads = token_weight * (token_dots - expects)
@@ -1043,6 +1057,11 @@
         for a in range(14):
             for b in range(14):
                 order[c, a, b, 128 * (b // 3) + 42 * (b % 3) + 14 * c + a] = 1
+    back = np.zeros((160, 256))
+    back[np.arange(80), 32 + np.arange(80)] = 1
+    back[80 + np.arange(80), 128 + 16 + np.arange(80)] = 1
+    tail = np.zeros((80, 128))
+    tail[np.arange(80), np.arange(80)] = 1
     wide = np.zeros((16, 40, 16, 48))
     for k in range(16):
         wide[k, np.arange(40), k, np.arange(40)] = 1
@@ -1050,19 +1069,14 @@
         one(perm), one(perm.T), one(inter.reshape(256, 768)),
         one(columns.reshape(384, 1024)), one(rows.reshape(1536, 512)),
         one(ph[0]), one(ph[1]), jnp.asarray(lanes.astype(np.float32)),
-        one(order.reshape(588, 640)), one(wide.reshape(640, 768)),
+        one(order.reshape(588, 640)), one(wide.reshape(640, 768)), one(back), one(tail),
     )
 
 
 def raw_shards(proj, conv, head, patch, attn_in, attn_out, mlp_in, mlp_bias, mlp_out, vit):
     conv_t = conv.reshape(144, 16).T
-    tail = jnp.pad(jnp.concatenate([conv_t[:, 128:], head[:, 128:]], axis=1), ((0, 0), (0, 48)))
-    back = attn_out.T
-    back = jnp.concatenate(
-        [jnp.pad(back[:, :80], ((0, 0), (32, 16))), jnp.pad(back[:, 80:], ((0, 0), (16, 32)))], axis=1
-    )
     return (
-        proj, conv_t, tail, head, patch.T, attn_in, back, mlp_in.T, mlp_bias[None], mlp_out, vit
+        proj.T, conv_t, head, patch.T, attn_in, attn_out.T, mlp_in.T, mlp_bias[None], mlp_out, vit
     )
 
 
@@ -1076,14 +1090,15 @@
         vm((48, WIDE), F32), vm((48, WIDTH), F32),
         vm((3072, 128), BF16), vm((48, 2304), BF16), vm((2, 48, 128), BF16), vm((2, 48, 128), BF16),
         vm((512, LANES), F32), vm((512, LANES), F32), vm((2, 512, 128), F32),
-        vm((2, 8, 512), F32), vm((2, NS, 8, 512), F32),
+        vm((2, 2, 512), F32), vm((2, NS, 2, 512), F32),
         vm((256, LANES), BF16), vm((512, 1024), BF16), vm((256, 512), BF16), vm((512, 256), BF16),
         vm((2, 2, 80, 128), F32), vm((2, 2, 80, 128), F32),
         vm((2, WIDE), F32), vm((NS, 2, WIDE), F32), vm((32, WIDE), F32),
-        vm((NS, 4, WIDE), F32), vm((NS, 4, WIDE), F32),
+        vm((NS, 2, WIDE), F32), vm((NS, 2, WIDE), F32),
+        vm((1, WIDE), F32), vm((2, NS, 1, WIDE), F32),
         vm((3, 2, WIDE), F32), vm((3, 2, NS, 2, WIDE), F32), vm((2, 1, 1024), F32),
         vm((4, WIDE), F32), vm((NS, 4, WIDE), F32),
-        vm((4, WIDE), F32), vm((NS, 4, WIDE), F32),
+        vm((2, WIDE), F32), vm((NS, 2, WIDE), F32),
         vm((2, 16, 128), F32), vm((2, 16, 128), F32),
         vm((16, 16, 768), F32), vm((16, 16, 768), BF16), vm((16, 16, 768), BF16),
         vm((NF, 4, 128), F32), vm((NF, 4, 128), F32), vm((16, 4, 128), F32),
@@ -1122,13 +1137,16 @@
     modulation, noisy, proj_bias, conv_bias, norm_gain, norm_shift, head_bias,
     position, class_token, vit_gain, vit_shift, attn_out_bias, mlp_out_bias, text_embed,
 ):
-    padded = jnp.concatenate(
-        [head_bias[:128], jnp.zeros((16,), F32), head_bias[128:], jnp.zeros((48,), F32)]
+    flat = jnp.concatenate(
+        [
+            conv_bias, norm_gain, norm_shift, head_bias[:128], proj_bias, jnp.zeros((64,), F32),
+            class_token, attn_out_bias, mlp_out_bias, jnp.zeros((16,), F32), head_bias[128:],
+            jnp.zeros((432,), F32),
+        ]
     )
     return (
-        modulation[0], noisy.reshape(512, 64), proj_bias[None], class_token[None], vit_gain, vit_shift,
-        attn_out_bias[None], mlp_out_bias[None], position, text_embed, conv_bias[None],
-        norm_gain[None], norm_shift[None], padded[None],
+        modulation[0], noisy.reshape(512, 64), flat.reshape(48, 128), vit_gain, vit_shift, position,
+        text_embed,
     )
 
 

time: 187 us -> 173 us (0.925)
  Pallas kernels: 171 us -> 164 us
  local copies, waits for them, and re-layouts: 11.7 us -> 6.96 us
  other arithmetic: 1.98 us -> 0 us
    pallas_call x1, Pallas kernels: 171 us -> 164 us  [run_step(): pl.pallas_call(kernel, out_shape=[jax.ShapeDtypeStruct(grad_shape, F32),...]
    broadcast_in_dim x4 -> x2, local copies, waits for them, and re-layouts: 3.87 us -> 0.01 us  [the longest x1 0.01 us: prepare(): jnp.zeros((64,), F32)]
    concatenate x3 -> x0, other arithmetic: 1.98 us -> none  [the longest x1 0.68 us: raw_shards(): jnp.concatenate([conv_t[:, 128:], head[:, 128:]], axis=1)]
where the time goes in v4:
time: 173 us; the launch traced here: 172 us
  Pallas kernels  164 us (95%)
  local copies, waits for them, and re-layouts  6.96 us (4%)
    pallas_call x1, Pallas kernels, run_step(): pl.pallas_call(kernel, out_shape=[jax.ShapeDtypeStruct(grad_shape, F32),...  164 us

profile of v4, /device:TPU:1, one launch (start us, length us, event | category | flops | bytes accessed | tf_op | source)
XLA Modules:
  0.0 172.4 jit_solution(6570913551314628047)
XLA Ops:
  1.3 0.7 slice.10
  2.0 0.7 slice.9
  2.7 1.4 copy.44
  4.1 1.5 concatenate.3
  5.6 164.1 %step.1 = (f32[96,64]{1,0:T(8,128)}, f32[8,128]{1,0:T(8,128)}) custom-call(bf16[512,3072]{1,0:T(8,128)(2,1)} %bitcast.13, bf16[64,96]{1,0:T(8,128)(2,1)} %bitcast.21, bf16[16,144]{1,0:T(8,128)(2,1)} %bitcast.19, bf16[16,192]{1,0:T(8,128)(2,1)} %refs_2_.1, bf16[40,588]{1,0:T(8,128)(2,1)} %bitcast.17, bf16[40,480]{1,0:T(8,128)(2,1)} %refs_4_.1, ...), custom_call_target="tpu_custom_call" | custom-call | tf_op jit(solution)/shard_map/step/pallas_call | solution.py:1118
  169.7 1.2 slice.11
  170.9 1.5 copy.43
  (3 shorter events, 0.0 us)

commit v5 on v4

--- a/solution.py
+++ b/solution.py
@@ -41,6 +41,10 @@
     )
 
 
+def sigmoid(values):
+    return 0.5 + 0.5 * jnp.tanh(0.5 * values)
+
+
 def halves(values):
     high = values.astype(BF16)
     return high, (values - high.astype(F32)).astype(BF16)
@@ -293,7 +297,7 @@
     )
 
 
-def reduce_gradient(mine, landed, terms, arrived, collected, sems):
+def reduce_gradient(mine, landed, terms, arrived, collected, sems, meanwhile):
     a_send, a_recv, b_send, b_recv, c_send, c_recv = sems
     f, g, s = lax.axis_index("fsdp"), lax.axis_index("grp"), lax.axis_index("slab")
     w = g * NS + s
@@ -304,6 +308,7 @@
         copy.start()
         copies.append(copy)
     landed[w] = mine[w]
+    meanwhile()
     for copy in copies:
         copy.wait()
     total = landed[0].astype(F32)
@@ -471,8 +476,6 @@
         weights = None
         for ref, given in zip((c_buf, p_buf, a_buf, b_buf), shards):
             ref[...] = given[...]
-    hid_copy.wait()
-    modulate(0, 8)
     greeted(targets)
     if fetch:
         weights.c_start()
@@ -501,7 +504,8 @@
         parts = jnp.concatenate(thirds(fill[:, 640 * k : 640 * k + 640]), axis=0)
         parts = nn(parts, wide_w[...])
         vecs[:, 768 * k : 768 * k + 768] = parts[0:48] + (parts[48:96] + parts[96:144])
-    modulate(8, 16)
+    hid_copy.wait()
+    modulate(0, 16)
     if weights is not None:
         weights.c_share()
         pump(0, 0)
@@ -529,7 +533,7 @@
             at = 96 * k + 16 * n
             proj_full[at : at + 16, :] = c_buf[n, k]
             proj_full[at + 48 : at + 64, :] = turned[16 * k : 16 * k + 16]
-    velocity = nn(mod[...], proj_full[...])[:, :64] + flat[13:14, 0:64]
+    velocity = nn(mod[...], proj_full[...])[:, :64] + flat[13:14, 64:128]
     pump(3)
     clean = noisy[...].astype(F32) - sigma * velocity
     lat_tok = (clean / LAT_SCALE + LAT_SHIFT).astype(BF16)
@@ -577,7 +581,7 @@
         + lax.dot_general(ph1[...], tail, (((0,), (1,)), ((), ())), preferred_element_type=F32)
     ).astype(BF16)
     bias_row = nn(jnp.broadcast_to(flat[12:13, :], (8, 128)), ph0[...].astype(F32), HIGH) + nn(
-        jnp.broadcast_to(flat[44:45, :], (8, 128)), ph1[...].astype(F32), HIGH
+        jnp.broadcast_to(flat[13:14, 0:64], (8, 64)), ph1[16:80, :].astype(F32), HIGH
     )
     head_col = columns_of(bias_row)[:, 0:1]
     pump(4, 2)
@@ -634,7 +638,7 @@
         normed = (nrm[:, pl.ds(at, 256)] - average) * inverse
         nrm[:, pl.ds(at, 256)] = normed
         gained = normed * gain + gshift
-        active = (gained * (1.0 / (1.0 + jnp.exp(-gained)))).astype(BF16)
+        active = (gained * sigmoid(gained)).astype(BF16)
         cells = (nn(head_t[...], active) + head_col).astype(BF16)
         for rr in range(2):
             rows = pl.ds(pl.multiple_of(i * 64 + 32 * rr, 32), 32)
@@ -907,7 +911,7 @@
         grads = nn(head_p[...], cols_buf[:, pl.ds(at, 256)])
         normed = nrm[:, pl.ds(at, 256)]
         gained = normed * gain + gshift
-        gate = 1.0 / (1.0 + jnp.exp(-gained))
+        gate = sigmoid(gained)
         grads = grads * (gate * (1.0 + gained * (1.0 - gate))) * gain
         dnrm[:, pl.ds(at, 256)] = grads
         acc[0] += grads[:, 0:128] + grads[:, 128:256]
@@ -978,15 +982,19 @@
         part = nn(d_vel, mod[:, 768 * quarter : 768 * quarter + 768])
         for w in range(2 * NS):
             gsplit[w, 4 * quarter : 4 * quarter + 4] = part[4 * w : 4 * w + 4]
-    for copy in live:
-        copy.wait_send()
+    def sent_all():
+        for copy in live:
+            copy.wait_send()
+        if weights is not None:
+            weights.finish()
+
     if weights is not None:
-        weights.finish()
         mine[...] = gsplit[...].astype(BF16)
-        reduce_gradient(mine, landed, terms, arrived, collected, sems[11:])
+        reduce_gradient(mine, landed, terms, arrived, collected, sems[11:], sent_all)
         whole = jnp.concatenate([collected[w] for w in range(2 * NS)], axis=0)
         grad_out[...] = jnp.transpose(whole)[0:96, :]
     else:
+        sent_all()
         grad_out[...] = gsplit[...]
 
 
@@ -1139,9 +1147,8 @@
 ):
     flat = jnp.concatenate(
         [
-            conv_bias, norm_gain, norm_shift, head_bias[:128], proj_bias, jnp.zeros((64,), F32),
-            class_token, attn_out_bias, mlp_out_bias, jnp.zeros((16,), F32), head_bias[128:],
-            jnp.zeros((432,), F32),
+            conv_bias, norm_gain, norm_shift, head_bias, proj_bias,
+            class_token, attn_out_bias, mlp_out_bias, jnp.zeros((512,), F32),
         ]
     )
     return (

time: 173 us -> 172 us (level)
  no operation moved by 1% of the time
where the time goes in v5:
time: 172 us
  Pallas kernels  165 us (96%)
  local copies, waits for them, and re-layouts  5.61 us (3%)
    pallas_call x1, Pallas kernels, run_step(): pl.pallas_call(kernel, out_shape=[jax.ShapeDtypeStruct(grad_shape, F32),...  165 us

profile of v5, /device:TPU:1, one launch (start us, length us, event | category | flops | bytes accessed | tf_op | source)
XLA Modules:
  0.0 171.6 jit_solution(18155130671143872158)
XLA Ops:
  1.3 1.4 copy.44
  2.8 1.5 concatenate.3
  4.2 164.7 %step.1 = (f32[96,64]{1,0:T(8,128)}, f32[8,128]{1,0:T(8,128)}) custom-call(bf16[512,3072]{1,0:T(8,128)(2,1)} %bitcast.13, bf16[64,96]{1,0:T(8,128)(2,1)} %bitcast.21, bf16[16,144]{1,0:T(8,128)(2,1)} %bitcast.19, bf16[16,192]{1,0:T(8,128)(2,1)} %refs_2_.1, bf16[40,588]{1,0:T(8,128)(2,1)} %bitcast.17, bf16[40,480]{1,0:T(8,128)(2,1)} %refs_4_.1, ...), custom_call_target="tpu_custom_call" | custom-call | tf_op jit(solution)/shard_map/step/pallas_call | solution.py:1126
  168.9 1.2 slice.3
  170.1 1.5 copy.43
  (1 shorter events, 0.0 us)
